TPU v7x, 1024 devices: a whole 8x8x8 slice. The times are simulated.
1024 devices in a mesh: blk: 128 (over x_hi, z, y), tower: 8 (over x_lo, core).
Axes of the slice: x: 8 (x_hi: 2, x_lo: 4; x = x_hi * 4 + x_lo), y: 8, z: 8, core: 2. Of those that a mesh axis runs over, the one named last changes fastest.
Arguments:
- image_embed: bfloat16 [16384, 1152], P('blk'), may hold values from -0.19921875 to 0.19921875
- text_embed: bfloat16 [16384, 1152], P(('blk', 'tower')), may hold values from -0.19921875 to 0.19921875
- image_feat: bfloat16 [16384, 6144], P('blk', 'tower'), may hold values from -0.75 to 0.75
- head: bfloat16 [1152, 6144], P(None, 'tower'), may hold values from -0.078125 to 0.078125
- sample_id: int32 [16384], P('blk'), may hold values from 0 to 4095
- domain: int32 [16384], P('blk'), may hold values from 0 to 7
- domain_bias: float32 [8], replicated, may hold values from -6 to -1
Outputs:
- image_grad: bfloat16 [16384, 6144], P('blk', 'tower')
- text_grad: float32 [16384, 1152], P(('blk', 'tower'))
- head_grad: float32 [1152, 6144], P('blk', 'tower')
All inputs are finite; a program needn't handle non-finite values.
Results may differ from a plain program's by a relative error of at most 0.007.
Values may be sent and summed in bfloat16 or wider, within the bound.
No kernel may reach another device: no remote copies, remote signals or barrier semaphores. Data moves between devices by JAX's collectives and lax.ppermute only.
A program may use at most 32 MiB of HBM per device.

v0:
```python
import jax
import jax.numpy as jnp
from jax import lax
from jax.sharding import PartitionSpec as P

STEPS = 4


epsilon = 1e-06
similarity_scaling_factor = 10.0


def shifted(block, axis, distance):
    devices = range(lax.axis_size(axis))
    route = [((i - distance) % len(devices), i) for i in devices]
    return lax.ppermute(block, axis, route)


def to_unit(values):
    floats = values.astype(jnp.float32)
    norms = jnp.sqrt(jnp.sum(floats * floats, -1, keepdims=True) + epsilon)
    return (floats / norms, norms)


def unit_back(unit_vals, norms, cotangent):
    return (cotangent - unit_vals * jnp.sum(unit_vals * cotangent, -1, keepdims=True)) / norms


def local(image_embed, text_embed, image_feat, head, sample_id, domain, domain_bias):
    text_count = text_embed.shape[0]
    tower_pos = lax.axis_index("tower")
    own_start = tower_pos * text_count
    own_ids = lax.dynamic_slice_in_dim(sample_id, own_start, text_count, 0)
    own_domain = lax.dynamic_slice_in_dim(domain, own_start, text_count, 0)
    image_unit, image_norm = to_unit(image_embed)
    text_unit, text_norm = to_unit(text_embed)
    image_round = image_unit.astype(jnp.bfloat16)
    table = jnp.arange(domain_bias.shape[0], dtype=jnp.int32)
    current = (text_unit.astype(jnp.bfloat16), own_ids, own_domain)
    picture_unit_vector = jnp.zeros(image_embed.shape, jnp.float32)
    carried = None
    for offset in range(STEPS):
        if offset > 0:
            current = shifted((current[0], current[1], current[2]), "blk", 1)
        caption_sample_range, text_ids, text_domain = current
        caption_score_offset = jnp.sum(
            jnp.where(text_domain[:, None] == table[None, :], domain_bias[None, :], 0.0), -1
        )
        similarity_scores = (
            similarity_scaling_factor
            * lax.dot_general(
                image_round,
                caption_sample_range,
                (((1,), (1,)), ((), ())),
                preferred_element_type=jnp.float32,
            )
            + caption_score_offset[None, :]
        )
        signs = jnp.where(sample_id[:, None] == text_ids[None, :], 1.0, -1.0).astype(jnp.float32)
        objective_derivative = (-signs * jax.nn.sigmoid(-signs * similarity_scores)).astype(
            jnp.bfloat16
        )
        picture_unit_vector = picture_unit_vector + similarity_scaling_factor * jnp.dot(
            objective_derivative, caption_sample_range, preferred_element_type=jnp.float32
        )
        caption_fraction = similarity_scaling_factor * lax.dot_general(
            objective_derivative,
            image_round,
            (((0,), (0,)), ((), ())),
            preferred_element_type=jnp.float32,
        )
        if offset == 0:
            carried = caption_fraction
        else:
            carried = shifted(carried, "blk", 1) + caption_fraction
    text_dir = shifted(carried.astype(jnp.bfloat16), "blk", -(STEPS - 1)).astype(carried.dtype)
    text_grad = unit_back(text_unit, text_norm, text_dir)
    summed_share = lax.psum_scatter(picture_unit_vector, "tower", scatter_dimension=0, tiled=True)
    share_count = summed_share.shape[0]
    share_start = tower_pos * share_count
    unit_share = lax.dynamic_slice_in_dim(image_unit, share_start, share_count, 0)
    norm_share = lax.dynamic_slice_in_dim(image_norm, share_start, share_count, 0)
    grad_share = unit_back(unit_share, norm_share, summed_share).astype(jnp.bfloat16)
    embed_grad = lax.all_gather(grad_share, "tower", axis=0, tiled=True)
    image_grad = jnp.dot(embed_grad, head, preferred_element_type=jnp.float32).astype(jnp.bfloat16)
    head_grad = lax.psum_scatter(
        lax.dot_general(
            embed_grad, image_feat, (((0,), (0,)), ((), ())), preferred_element_type=jnp.float32
        ),
        "blk",
        scatter_dimension=0,
        tiled=True,
    )
    return (image_grad, text_grad, head_grad)


def solution(mesh):
    in_specs = (
        P("blk", None),
        P(("blk", "tower"), None),
        P("blk", "tower"),
        P(None, "tower"),
        P("blk"),
        P("blk"),
        P(),
    )
    out_specs = (P("blk", "tower"), P(("blk", "tower"), None), P("blk", "tower"))
    return jax.shard_map(local, mesh=mesh, in_specs=in_specs, out_specs=out_specs, check_vma=False)
```

profile of v0, /device:TPU:14, one launch (start us, length us, event | category | flops | bytes accessed | tf_op | source)
XLA Modules:
  0.0 1801.6 jit_solution(4621060768849707653)
XLA Ops:
  8.1 3.6 collective-permute-start.2
  13.4 3.6 collective-permute-start.1
  17.8 3.6 collective-permute-start
  21.4 1.1 fusion.34
  23.6 9.6 collective-permute-done.2
  33.2 1.9 collective-permute-start.5
  35.1 4.4 collective-permute-done
  39.5 1.9 collective-permute-start.3
  41.4 5.3 collective-permute-done.5
  46.7 1.9 collective-permute-start.8
  48.7 4.4 collective-permute-done.3
  53.1 1.9 collective-permute-start.6
  55.0 5.3 collective-permute-done.8
  62.2 1.9 collective-permute-start.4
  65.3 10.9 collective-permute-done.4
  76.2 1.9 collective-permute-start.7
  78.7 11.5 collective-permute-done.7
  91.7 26.7 %reduce-scatter.2.cloned.1.call-done = f32[16,1152]{1,0:T(8,128)} async-done(((f32[128,1152]{1,0:T(8,128)}), f32[16,1152]{1,0:T(8,128)}) %reduce-scatter.2.cloned.1.call-update) | async-done | bytes 73744 | tf_op jit(solution)/shard_map/reduce_scatter | solution.py:78
  120.4 15.0 all_gather.3
  135.4 2.5 fusion.41
  138.0 3.4 collective-permute-start.9
  141.4 13.1 collective-permute-done.9
  154.6 1.9 collective-permute-start.10
  156.7 13.1 collective-permute-done.10
  169.8 1.9 collective-permute-start.11
  171.9 12.6 collective-permute-done.11
  184.5 1.9 collective-permute-start.12
  186.5 1.3 dynamic-slice.4
  188.4 3.9 collective-permute-done.12
  193.2 1.1 convolution_convert_fusion
  194.3 1599.0 %all-reduce.3.cloned.1.call-done = f32[1152,768]{1,0:T(8,128)} async-done(((f32[1152,768]{1,0:T(8,128)}), f32[1152,768]{1,0:T(8,128)}) %all-reduce.3.cloned.1.call-update) | async-done | bytes 3538960
  1793.3 1.5 constant_dynamic-slice_fusion
  (41 shorter events, 13.1 us)
Async XLA Ops:
  7.2 186.0 %copy-start = (bf16[1152,768]{1,0:T(8,128)(2,1)S(1)}, bf16[1152,768]{1,0:T(8,128)(2,1)}, u32[]{:S(2)}) copy-start(bf16[1152,768]{1,0:T(8,128)(2,1)} %param.10) | copy-start | bytes 5308420
  7.2 71.0 %copy-start.3 = (s32[128]{0:T(128)S(1)}, s32[128]{0:T(128)}, u32[]{:S(2)}) copy-start(s32[128]{0:T(128)} %param.11) | copy-start | bytes 1540
  7.2 111.2 %reduce-scatter.2.cloned.1.call-start = ((), (), s32[]{:S(2)}) async-start(), calls=%async_computation.1 | async-start | bytes 663552 | tf_op jit(solution)/shard_map/reduce_scatter | solution.py:78
  8.1 25.1 %collective-permute-start.2 = (s32[16]{0:T(128)S(1)}, s32[16]{0:T(128)S(1)}, u32[]{:S(2)}, u32[]{:S(2)}) collective-permute-start(s32[16]{0:T(128)S(1)} %dynamic_slice.11), channel_id=1, source_target_pairs={{1016,0},{0,8},{8,16},{16,24},{24,32},{32,40},{40,48},{48,56},{56,... | collective-permute-start | bytes 200 | tf_op jit(solution)/shard_map/ppermute | solution.py:16
  13.4 48.8 %collective-permute-start.1 = (bf16[16,1152]{1,0:T(8,128)(2,1)S(1)}, bf16[16,1152]{1,0:T(8,128)(2,1)S(1)}, u32[]{:S(2)}, u32[]{:S(2)}) collective-permute-start(bf16[16,1152]{1,0:T(8,128)(2,1)S(1)} %fusion.38), channel_id=1, source_target_pairs={{1016,0},{0,8},{8,16},{16,24},{24,32},{32,40},{40,48},{48,56},{56,... | collective-permute-start | bytes 110600 | tf_op jit(solution)/shard_map/ppermute | solution.py:16
  17.8 21.7 %collective-permute-start = (s32[16]{0:T(128)S(1)}, s32[16]{0:T(128)S(1)}, u32[]{:S(2)}, u32[]{:S(2)}) collective-permute-start(s32[16]{0:T(128)S(1)} %dynamic_slice.10), channel_id=1, source_target_pairs={{1016,0},{0,8},{8,16},{16,24},{24,32},{32,40},{40,48},{48,56},{56,... | collective-permute-start | bytes 200 | tf_op jit(solution)/shard_map/ppermute | solution.py:16
  33.2 13.5 collective-permute-start.5
  39.5 13.5 collective-permute-start.3
  46.7 13.5 collective-permute-start.8
  53.1 25.6 %collective-permute-start.6 = (s32[16]{0:T(128)S(1)}, s32[16]{0:T(128)S(1)}, u32[]{:S(2)}, u32[]{:S(2)}) collective-permute-start(s32[16]{0:T(128)S(1)} %collective-permute-done.3), channel_id=1, source_target_pairs={{1016,0},{0,8},{8,16},{16,24},{24,32},{32,40},{40,48},{48,56},{56,... | collective-permute-start | bytes 200 | tf_op jit(solution)/shard_map/ppermute | solution.py:16
  61.0 74.3 %copy-start.2 = (bf16[128,768]{1,0:T(8,128)(2,1)S(1)}, bf16[128,768]{1,0:T(8,128)(2,1)}, u32[]{:S(2)}) copy-start(bf16[128,768]{1,0:T(8,128)(2,1)} %param.9) | copy-start | bytes 589828
  62.2 14.0 collective-permute-start.4
  76.2 14.0 collective-permute-start.7
  91.5 1701.7 %all-reduce.3.cloned.1.call-start = ((), (), s32[]{:S(2)}) async-start(), calls=%async_computation.2 | async-start | bytes 7077888
  137.8 54.4 %copy-start.1 = (bf16[16,1152]{1,0:T(8,128)(2,1)S(1)}, bf16[16,1152]{1,0:T(8,128)(2,1)}, u32[]{:S(2)}) copy-start(bf16[16,1152]{1,0:T(8,128)(2,1)} %param.8) | copy-start | bytes 110596
  138.0 16.5 collective-permute-start.9
  154.6 15.2 collective-permute-start.10
  169.8 14.7 collective-permute-start.11
  184.5 7.7 collective-permute-start.12
Sparse Core Ops, SparseCore 0:
  91.6 26.7 reduce-scatter.1
  138.0 1655.2 all-reduce.2
where the time goes:
time: 1800 us
  waiting for transfers between devices  1720 us (96%)
  starting transfers between devices  31.5 us (2%)
    unnamed x3, waiting for transfers between devices  1600 us
    ppermute x13, waiting for transfers between devices, shifted(): return lax.ppermute(block, axis, route)  94.1 us
  transfers between devices with their start and end apart: 15, of which 13 were waited for; matrix products, arithmetic and copies ran while one was open for 1% of the time, Pallas kernels for 0%

commit v1 on v0

v1 whole, which is shorter than its diff:
```python
import functools

import jax
import jax.numpy as jnp
from jax import lax
from jax.experimental import pallas as pl
from jax.experimental.pallas import tpu as pltpu
from jax.sharding import Mesh, PartitionSpec as P

EPSILON = 1e-06
SCALE = 10.0
TAIL = 128
SPLIT = (("xh", 2), ("z", 8), ("y", 8), ("xl", 4), ("core", 2))
BLK = ("xh", "z", "y")
TOWER = ("xl", "core")
ALL = BLK + TOWER

bf16, f32, i32 = jnp.bfloat16, jnp.float32, jnp.int32
NT = (((1,), (1,)), ((), ()))
TN = (((0,), (0,)), ((), ()))
PARAMS = pltpu.CompilerParams(vmem_limit_bytes=32 * 1024 * 1024)


def shifted(block, axis, distance):
    size = lax.axis_size(axis)
    return lax.ppermute(block, axis, [((i - distance) % size, i) for i in range(size)])


def norms_of(floats):
    return jnp.sqrt(jnp.sum(floats * floats, -1, keepdims=True) + EPSILON)


def vmem(count):
    return [pl.BlockSpec(memory_space=pltpu.VMEM)] * count


def iota(shape, dim):
    return lax.broadcasted_iota(i32, shape, dim)


def prepare(pos_ref, bias_ref, text_ref, ids_ref, domain_ref, out_ref):
    rows, width = text_ref.shape
    floats = text_ref[...].astype(f32)
    out_ref[:, :width] = (floats / norms_of(floats)).astype(bf16)
    wide = (rows, ids_ref.shape[1])
    mine = iota(wide, 1) == iota(wide, 0) + pos_ref[0] * rows
    own_id = jnp.sum(jnp.where(mine, ids_ref[...].astype(f32), 0.0), -1, keepdims=True)
    own_domain = jnp.sum(jnp.where(mine, domain_ref[...].astype(f32), 0.0), -1, keepdims=True)
    bias = jnp.zeros((rows, 1), f32)
    for k in range(bias_ref.shape[0]):
        bias = bias + jnp.where(own_domain == float(k), bias_ref[k], 0.0)
    whole = own_id.astype(i32)
    high = (whole >> 6).astype(f32)
    low = (whole & 63).astype(f32)
    first = bias.astype(bf16).astype(f32)
    second = (bias - first).astype(bf16).astype(f32)
    third = bias - first - second
    lane = iota((rows, TAIL), 1)
    tail = jnp.zeros((rows, TAIL), f32)
    for k, part in enumerate((high, low, first, second, third)):
        tail = jnp.where(lane == k, part, tail)
    out_ref[:, width:] = tail.astype(bf16)


def slopes(rows, image_round, ids):
    width = image_round.shape[1]
    images = image_round.shape[0]
    tail = rows[:, width:]
    which = iota((TAIL, images), 0)
    take_id = jnp.where(which == 0, 64.0, jnp.where(which == 1, 1.0, 0.0)).astype(bf16)
    take_bias = jnp.where((which >= 2) & (which < 5), 1.0, 0.0).astype(bf16)
    logits = SCALE * lax.dot_general(rows[:, :width], image_round, NT, preferred_element_type=f32)
    logits = logits + jnp.dot(tail, take_bias, preferred_element_type=f32)
    text_ids = jnp.dot(tail, take_id, preferred_element_type=f32)
    signs = jnp.where(text_ids == ids.astype(f32), 1.0, -1.0)
    return (-signs * jax.nn.sigmoid(-signs * logits)).astype(bf16)


def text_side(own_ref, image_ref, ids_ref, near_ref, far_ref):
    slope = slopes(own_ref[...], image_ref[...], ids_ref[...])
    share = SCALE * jnp.dot(slope, image_ref[...], preferred_element_type=f32)
    half = near_ref.shape[0]
    near_ref[...] = share[:half]
    far_ref[...] = share[half:].astype(far_ref.dtype)


def image_side(a_ref, b_ref, embed_ref, ids_ref, out_ref, turned_ref):
    floats = embed_ref[...].astype(f32)
    norms = norms_of(floats)
    units = floats / norms
    rounded = units.astype(bf16)
    width = floats.shape[1]
    total = jnp.zeros(floats.shape, f32)
    for ref in (a_ref, b_ref):
        rows = ref[...]
        slope = slopes(rows, rounded, ids_ref[...])
        total = total + lax.dot_general(slope, rows[:, :width], TN, preferred_element_type=f32)
    total = SCALE * total
    grad = (total - units * jnp.sum(units * total, -1, keepdims=True)) / norms
    out_ref[...] = grad.astype(bf16)
    turned = grad.T.astype(bf16)
    planes, pieces, run = turned_ref.shape[0], turned_ref.shape[1], turned_ref.shape[2]
    for p in range(pieces):
        for z in range(planes):
            start = (p * planes + z) * run
            turned_ref[z, p] = turned[start : start + run]


def head_side(turned_ref, feat_ref, out_ref):
    blocks = turned_ref.shape[0]
    part = jnp.zeros((turned_ref.shape[1], feat_ref.shape[2]), f32)
    for k in range(blocks):
        part = part + jnp.dot(turned_ref[k], feat_ref[k], preferred_element_type=f32)
    targets, groups = out_ref.shape[0], part.shape[1] // 128
    run = part.shape[0] // targets
    for c in range(targets):
        for g in range(groups):
            out_ref[c, g * run : (g + 1) * run] = part[
                c * run : (c + 1) * run, g * 128 : (g + 1) * 128
            ].astype(bf16)


def head_sum(parts_ref, out_ref):
    total = jnp.sum(parts_ref[...].astype(f32), 0)
    run, groups = out_ref.shape[0], out_ref.shape[1] // 128
    for g in range(groups):
        out_ref[:, g * 128 : (g + 1) * 128] = total[g * run : (g + 1) * run]


def text_back(share_ref, last_ref, text_ref, out_ref):
    floats = text_ref[...].astype(f32)
    norms = norms_of(floats)
    units = floats / norms
    total = share_ref[...] + last_ref[...].astype(f32)
    out_ref[...] = (total - units * jnp.sum(units * total, -1, keepdims=True)) / norms


def call(kernel, shapes, *args, smem=0):
    specs = [pl.BlockSpec(memory_space=pltpu.SMEM)] * smem + vmem(len(args) - smem)
    outs = [jax.ShapeDtypeStruct(s, d) for s, d in shapes]
    single = len(outs) == 1
    return pl.pallas_call(
        kernel,
        out_shape=outs[0] if single else outs,
        in_specs=specs,
        out_specs=vmem(1)[0] if single else vmem(len(outs)),
        compiler_params=PARAMS,
        name=kernel.__name__,
    )(*args)


def local(image_embed, text_embed, image_feat, head, sample_id, domain, domain_bias):
    images, width = image_embed.shape
    texts = text_embed.shape[0]
    features = image_feat.shape[1]
    position = lax.axis_index(TOWER).astype(i32).reshape(1)
    ids = sample_id.reshape(1, images)
    planes = lax.axis_size("z")
    across = lax.axis_size("xh") * lax.axis_size("y")
    own_width = width // planes

    feats = lax.all_gather(image_feat, "z", axis=0, tiled=False)

    payload = call(
        prepare, [((texts, width + TAIL), bf16)],
        position, domain_bias, text_embed, ids, domain.reshape(1, images), smem=2,
    )
    floats = image_embed.astype(f32)
    image_round = (floats / norms_of(floats)).astype(bf16)

    two = jnp.concatenate([payload, shifted(payload, BLK, 1)], 0)
    own = jnp.concatenate([two, shifted(two, BLK, 2)], 0)

    turns = [shifted(own, "xl", d) for d in range(1, lax.axis_size("xl"))]
    near, far = call(
        text_side, [((2 * texts, width), f32), ((2 * texts, width), bf16)],
        own, image_round, ids,
    )
    here = jnp.concatenate([own] + turns, 0)
    there = shifted(here, "core", 1)

    back = shifted(far, BLK, -2).astype(f32)
    stay = near[:texts] + back[:texts]
    pass_on = (near[texts:] + back[texts:]).astype(bf16)
    last = shifted(pass_on, BLK, -1)
    text_grad = call(text_back, [((texts, width), f32)], stay, last, text_embed)

    pieces = lax.axis_size("xh")
    run = width // (planes * pieces)
    embed_grad, turned = call(
        image_side,
        [((images, width), bf16), ((planes, pieces, run, images), bf16)],
        here, there, image_embed, ids,
    )
    plane = lax.all_to_all(turned.reshape(planes, own_width, images), "z", 0, 0, tiled=True)
    image_grad = jnp.dot(embed_grad, head, preferred_element_type=f32).astype(bf16)
    rows = own_width // across
    parts = call(
        head_side, [((across, rows * features // 128, 128), bf16)], plane, feats
    )
    parts = lax.all_to_all(parts, ("xh", "y"), 0, 0, tiled=True)
    head_grad = call(head_sum, [((rows, features), f32)], parts)
    return (image_grad, text_grad, head_grad)


def solution(mesh):
    split = Mesh(mesh.devices.reshape([n for _, n in SPLIT]), [name for name, _ in SPLIT])
    in_specs = (
        P(BLK, None),
        P(ALL, None),
        P(BLK, TOWER),
        P(None, TOWER),
        P(BLK),
        P(BLK),
        P(),
    )
    out_specs = (P(BLK, TOWER), P(ALL, None), P(BLK, TOWER))
    return jax.shard_map(local, mesh=split, in_specs=in_specs, out_specs=out_specs, check_vma=False)
```

time: 1800 us -> 126 us (0.07)
  the two profiles are of different devices: /device:TPU:14 before, /device:TPU:2 now
where the time goes in v1:
time: 126 us; the launch traced here: 125 us
  waiting for transfers between devices  60.9 us (48%)
  starting transfers between devices  38.4 us (30%)
  between operations  14.2 us (11%)
  Pallas kernels  6.03 us (5%)
  local copies, waits for them, and re-layouts  4.39 us (3%)
    ppermute x8, waiting for transfers between devices, shifted(): lax.ppermute(block, axis, [((i - distance) % size, i) for i in range(size)])  55.6 us
    ppermute x8, starting transfers between devices, shifted(): lax.ppermute(block, axis, [((i - distance) % size, i) for i in range(size)])  31.4 us
    pallas_call x6, Pallas kernels, call(): pl.pallas_call(kernel, out_shape=outs[0] if single else outs, in_specs=sp...  6.03 us
    all_to_all x1, waiting for transfers between devices, local(): lax.all_to_all(turned.reshape(planes, own_width, images), 'z', 0, 0, tile...  5.29 us
    unnamed x23, local copies, waits for them, and re-layouts  4.38 us
    all_to_all x1, starting transfers between devices, local(): parts = lax.all_to_all(parts, ('xh', 'y'), 0, 0, tiled=True)  3.53 us
    all_to_all x1, starting transfers between devices, local(): lax.all_to_all(turned.reshape(planes, own_width, images), 'z', 0, 0, tile...  3.42 us
  transfers between devices with their start and end apart: 11, of which 9 were waited for; matrix products, arithmetic and copies ran while one was open for 1% of the time, Pallas kernels for 3%

profile of v1, /device:TPU:2, one launch (start us, length us, event | category | flops | bytes accessed | tf_op | source)
XLA Modules:
  0.0 125.4 jit_solution(16168026443692004120)
XLA Ops:
  7.3 0.9 copy-done.3
  8.2 0.7 copy-done.5
  8.9 0.7 copy-done.7
  9.5 0.7 copy-done.8
  10.2 0.6 prepare.1
  10.8 3.6 %collective-permute-start = (bf16[16,1280]{1,0:T(8,128)(2,1)S(1)}, bf16[16,1280]{1,0:T(8,128)(2,1)S(1)}, u32[]{:S(2)}, u32[]{:S(2)}) collective-permute-start(bf16[16,1280]{1,0:T(8,128)(2,1)S(1)} %prepare.1), channel_id=1, source_target_pairs={{1016,0},{0,8},{8,16},{16,24},{24,32},{32,40},{40,48},{48,56},{56,... | collective-permute-start | bytes 122888 | tf_op jit(solution)/shard_map/ppermute | solution.py:26
  14.5 23.8 %collective-permute-done = bf16[16,1280]{1,0:T(8,128)(2,1)S(1)} collective-permute-done((bf16[16,1280]{1,0:T(8,128)(2,1)S(1)}, bf16[16,1280]{1,0:T(8,128)(2,1)S(1)}, u32[]{:S(2)}, u32[]{:S(2)}) %collective-permute-start) | collective-permute-done | bytes 40992 | tf_op jit(solution)/shard_map/ppermute | solution.py:26
  38.3 1.9 %collective-permute-start.1 = (bf16[32,1280]{1,0:T(8,128)(2,1)S(1)}, bf16[32,1280]{1,0:T(8,128)(2,1)S(1)}, u32[]{:S(2)}, u32[]{:S(2)}) collective-permute-start(bf16[32,1280]{1,0:T(8,128)(2,1)S(1)} %pad_maximum_fusion.1), channel_id=1, source_target_pairs={{1008,0},{1016,8},{0,16},{8,24},{16,32},{24,40},{32,48},{40,56},{4... | collective-permute-start | bytes 245768 | tf_op jit(solution)/shard_map/ppermute | solution.py:26
  40.2 14.4 %collective-permute-done.1 = bf16[32,1280]{1,0:T(8,128)(2,1)S(1)} collective-permute-done((bf16[32,1280]{1,0:T(8,128)(2,1)S(1)}, bf16[32,1280]{1,0:T(8,128)(2,1)S(1)}, u32[]{:S(2)}, u32[]{:S(2)}) %collective-permute-start.1) | collective-permute-done | bytes 81952 | tf_op jit(solution)/shard_map/ppermute | solution.py:26
  54.6 2.1 %collective-permute-start.2 = (bf16[64,1280]{1,0:T(8,128)(2,1)S(1)}, bf16[64,1280]{1,0:T(8,128)(2,1)S(1)}, u32[]{:S(2)}, u32[]{:S(2)}) collective-permute-start(bf16[64,1280]{1,0:T(8,128)(2,1)S(1)} %pad_maximum_fusion.own_ref), channel_id=1, source_target_pairs={{6,0},{0,2},{2,4},{4,6},{7,1},{1,3},{3,5},{5,7},{14,8},{8,10},{10,... | collective-permute-start | bytes 491528 | tf_op jit(solution)/shard_map/ppermute | solution.py:26
  56.7 5.7 %collective-permute-start.3 = (bf16[64,1280]{1,0:T(8,128)(2,1)S(1)}, bf16[64,1280]{1,0:T(8,128)(2,1)S(1)}, u32[]{:S(2)}, u32[]{:S(2)}) collective-permute-start(bf16[64,1280]{1,0:T(8,128)(2,1)S(1)} %pad_maximum_fusion.own_ref), channel_id=1, source_target_pairs={{4,0},{6,2},{0,4},{2,6},{5,1},{7,3},{1,5},{3,7},{12,8},{14,10},{8,... | collective-permute-start | bytes 491528 | tf_op jit(solution)/shard_map/ppermute | solution.py:26
  62.4 1.9 %collective-permute-start.4 = (bf16[64,1280]{1,0:T(8,128)(2,1)S(1)}, bf16[64,1280]{1,0:T(8,128)(2,1)S(1)}, u32[]{:S(2)}, u32[]{:S(2)}) collective-permute-start(bf16[64,1280]{1,0:T(8,128)(2,1)S(1)} %pad_maximum_fusion.own_ref), channel_id=1, source_target_pairs={{2,0},{4,2},{6,4},{0,6},{3,1},{5,3},{7,5},{1,7},{10,8},{12,10},{14... | collective-permute-start | bytes 491528 | tf_op jit(solution)/shard_map/ppermute | solution.py:26
  64.3 1.6 %collective-permute-done.2 = bf16[64,1280]{1,0:T(8,128)(2,1)S(1)} collective-permute-done((bf16[64,1280]{1,0:T(8,128)(2,1)S(1)}, bf16[64,1280]{1,0:T(8,128)(2,1)S(1)}, u32[]{:S(2)}, u32[]{:S(2)}) %collective-permute-start.2) | collective-permute-done | bytes 163872 | tf_op jit(solution)/shard_map/ppermute | solution.py:26
  65.9 4.1 %collective-permute-done.3 = bf16[64,1280]{1,0:T(8,128)(2,1)S(1)} collective-permute-done((bf16[64,1280]{1,0:T(8,128)(2,1)S(1)}, bf16[64,1280]{1,0:T(8,128)(2,1)S(1)}, u32[]{:S(2)}, u32[]{:S(2)}) %collective-permute-start.3) | collective-permute-done | bytes 163872 | tf_op jit(solution)/shard_map/ppermute | solution.py:26
  70.0 2.8 %collective-permute-done.4 = bf16[64,1280]{1,0:T(8,128)(2,1)S(1)} collective-permute-done((bf16[64,1280]{1,0:T(8,128)(2,1)S(1)}, bf16[64,1280]{1,0:T(8,128)(2,1)S(1)}, u32[]{:S(2)}, u32[]{:S(2)}) %collective-permute-start.4) | collective-permute-done | bytes 163872 | tf_op jit(solution)/shard_map/ppermute | solution.py:26
  72.8 1.9 %collective-permute-start.5 = (bf16[256,1280]{1,0:T(8,128)(2,1)S(1)}, bf16[256,1280]{1,0:T(8,128)(2,1)S(1)}, u32[]{:S(2)}, u32[]{:S(2)}) collective-permute-start(bf16[256,1280]{1,0:T(8,128)(2,1)S(1)} %constant_dynamic-update-slice_fusion.a_ref), channel_id=1, source_target_pairs={{1,0},{0,1},{3,2},{2,3},{5,4},{4,5},{7,6},{6,7},{9,8},{8,9},{11,10... | collective-permute-start | bytes 1966088 | tf_op jit(solution)/shard_map/ppermute | solution.py:26
  74.8 0.1 fusion
  74.9 1.9 %collective-permute-done.5.b_ref = bf16[256,1280]{1,0:T(8,128)(2,1)S(1)} collective-permute-done((bf16[256,1280]{1,0:T(8,128)(2,1)S(1)}, bf16[256,1280]{1,0:T(8,128)(2,1)S(1)}, u32[]{:S(2)}, u32[]{:S(2)}) %collective-permute-start.5) | collective-permute-done | bytes 655392 | tf_op jit(solution)/shard_map/ppermute | solution.py:26
  76.8 2.0 %image_side.1 = (bf16[128,1152]{1,0:T(8,128)(2,1)S(1)}, bf16[8,2,72,128]{3,2,1,0:T(8,128)(2,1)}) custom-call(bf16[256,1280]{1,0:T(8,128)(2,1)S(1)} %constant_dynamic-update-slice_fusion.a_ref, bf16[256,1280]{1,0:T(8,128)(2,1)S(1)} %collective-permute-done.5.b_ref, bf16[128,1152]{1,0:T(8,128)(2,1)S(1)} %copy-done.1, s32[1,128]{1,0:T(1,128)S(1)} %bitcast.9), custom_call_target="tpu_custom_call" | custom-call | tf_op jit(solution)/shard_map/image_side/pallas_call | solution.py:142
  78.8 3.4 %all-to-all-start = ((bf16[8,144,128]{2,1,0:T(8,128)(2,1)}), bf16[8,144,128]{2,1,0:T(8,128)(2,1)S(1)}, u32[]{:S(2)}, u32[]{:S(2)}) async-start(bf16[8,144,128]{2,1,0:T(8,128)(2,1)} %bitcast.3), calls=%async_computation | async-start | bytes 589824 | tf_op jit(solution)/shard_map/all_to_all | solution.py:195
  82.4 0.5 text_side.1
  82.9 1.9 %collective-permute-start.6 = (bf16[32,1152]{1,0:T(8,128)(2,1)S(1)}, bf16[32,1152]{1,0:T(8,128)(2,1)S(1)}, u32[]{:S(2)}, u32[]{:S(2)}) collective-permute-start(bf16[32,1152]{1,0:T(8,128)(2,1)S(1)} %get-tuple-element.9), channel_id=1, source_target_pairs={{16,0},{24,8},{32,16},{40,24},{48,32},{56,40},{64,48},{72,56},{80,... | collective-permute-start | bytes 221192 | tf_op jit(solution)/shard_map/ppermute | solution.py:26
  84.8 5.2 %collective-permute-done.6 = bf16[32,1152]{1,0:T(8,128)(2,1)S(1)} collective-permute-done((bf16[32,1152]{1,0:T(8,128)(2,1)S(1)}, bf16[32,1152]{1,0:T(8,128)(2,1)S(1)}, u32[]{:S(2)}, u32[]{:S(2)}) %collective-permute-start.6) | collective-permute-done | bytes 73760 | tf_op jit(solution)/shard_map/ppermute | solution.py:26
  90.0 5.3 %all-to-all-done.turned_ref = bf16[8,144,128]{2,1,0:T(8,128)(2,1)S(1)} async-done(((bf16[8,144,128]{2,1,0:T(8,128)(2,1)}), bf16[8,144,128]{2,1,0:T(8,128)(2,1)S(1)}, u32[]{:S(2)}, u32[]{:S(2)}) %all-to-all-start) | async-done | bytes 294944 | tf_op jit(solution)/shard_map/all_to_all | solution.py:195
  95.3 1.4 %copy-done.2 = bf16[1024,768]{1,0:T(8,128)(2,1)S(1)} copy-done((bf16[1024,768]{1,0:T(8,128)(2,1)S(1)}, bf16[1024,768]{1,0:T(8,128)(2,1)}, u32[]{:S(2)}) %copy-start.2) | copy-done | bytes 1572888
  96.7 1.4 %head_side.1 = bf16[16,54,128]{2,1,0:T(8,128)(2,1)} custom-call(bf16[8,144,128]{2,1,0:T(8,128)(2,1)S(1)} %all-to-all-done.turned_ref, bf16[8,128,768]{2,1,0:T(8,128)(2,1)S(1)} %bitcast.7), custom_call_target="tpu_custom_call" | custom-call | tf_op jit(solution)/shard_map/head_side/pallas_call | solution.py:142
  98.2 3.5 %all-to-all-start.1 = ((bf16[16,54,128]{2,1,0:T(8,128)(2,1)}), bf16[16,54,128]{2,1,0:T(8,128)(2,1)S(1)}, u32[]{:S(2)}, u32[]{:S(2)}) async-start(bf16[16,54,128]{2,1,0:T(8,128)(2,1)} %head_side.1), calls=%async_computation.1 | async-start | bytes 458752 | tf_op jit(solution)/shard_map/all_to_all | solution.py:201
  101.7 12.4 %collective-permute-start.7 = (bf16[16,1152]{1,0:T(8,128)(2,1)S(1)}, bf16[16,1152]{1,0:T(8,128)(2,1)S(1)}, u32[]{:S(2)}, u32[]{:S(2)}) collective-permute-start(bf16[16,1152]{1,0:T(8,128)(2,1)S(1)} %get-tuple-element.11), channel_id=1, source_target_pairs={{8,0},{16,8},{24,16},{32,24},{40,32},{48,40},{56,48},{64,56},{72,6... | collective-permute-start | bytes 110600 | tf_op jit(solution)/shard_map/ppermute | solution.py:26
  114.1 1.8 %collective-permute-done.7.last_ref = bf16[16,1152]{1,0:T(8,128)(2,1)S(1)} collective-permute-done((bf16[16,1152]{1,0:T(8,128)(2,1)S(1)}, bf16[16,1152]{1,0:T(8,128)(2,1)S(1)}, u32[]{:S(2)}, u32[]{:S(2)}) %collective-permute-start.7) | collective-permute-done | bytes 36896 | tf_op jit(solution)/shard_map/ppermute | solution.py:26
  116.0 0.8 text_back.1
  116.8 1.1 convolution_convert_fusion
  117.9 0.7 head_sum.1
  (29 shorter events, 0.3 us)
Async XLA Ops:
  7.2 109.6 %copy-start = (bf16[1152,768]{1,0:T(8,128)(2,1)S(1)}, bf16[1152,768]{1,0:T(8,128)(2,1)}, u32[]{:S(2)}) copy-start(bf16[1152,768]{1,0:T(8,128)(2,1)} %param.10) | copy-start | bytes 5308420
  7.2 69.6 %copy-start.6 = (s32[128]{0:T(128)S(1)}, s32[128]{0:T(128)}, u32[]{:S(2)}) copy-start(s32[128]{0:T(128)} %param.11) | copy-start | bytes 1540
  7.2 67.6 %copy-start.1 = (bf16[128,1152]{1,0:T(8,128)(2,1)S(1)}, bf16[128,1152]{1,0:T(8,128)(2,1)}, u32[]{:S(2)}) copy-start(bf16[128,1152]{1,0:T(8,128)(2,1)} %embed_ref.1) | copy-start | bytes 884740
  7.2 88.1 %all-gather.3.cloned.1.call-start = ((), (), s32[]{:S(2)}) async-start(), calls=%async_computation.2 | async-start | bytes 1769472 | tf_op jit(solution)/shard_map/all_gather | solution.py:162
  7.3 0.9 copy-start.3
  8.2 0.7 copy-start.5
  8.9 0.7 copy-start.7
  9.5 0.7 copy-start.8
  10.8 27.4 %collective-permute-start = (bf16[16,1280]{1,0:T(8,128)(2,1)S(1)}, bf16[16,1280]{1,0:T(8,128)(2,1)S(1)}, u32[]{:S(2)}, u32[]{:S(2)}) collective-permute-start(bf16[16,1280]{1,0:T(8,128)(2,1)S(1)} %prepare.1), channel_id=1, source_target_pairs={{1016,0},{0,8},{8,16},{16,24},{24,32},{32,40},{40,48},{48,56},{56,... | collective-permute-start | bytes 122888 | tf_op jit(solution)/shard_map/ppermute | solution.py:26
  38.3 16.3 %collective-permute-start.1 = (bf16[32,1280]{1,0:T(8,128)(2,1)S(1)}, bf16[32,1280]{1,0:T(8,128)(2,1)S(1)}, u32[]{:S(2)}, u32[]{:S(2)}) collective-permute-start(bf16[32,1280]{1,0:T(8,128)(2,1)S(1)} %pad_maximum_fusion.1), channel_id=1, source_target_pairs={{1008,0},{1016,8},{0,16},{8,24},{16,32},{24,40},{32,48},{40,56},{4... | collective-permute-start | bytes 245768 | tf_op jit(solution)/shard_map/ppermute | solution.py:26
  54.6 11.3 %collective-permute-start.2 = (bf16[64,1280]{1,0:T(8,128)(2,1)S(1)}, bf16[64,1280]{1,0:T(8,128)(2,1)S(1)}, u32[]{:S(2)}, u32[]{:S(2)}) collective-permute-start(bf16[64,1280]{1,0:T(8,128)(2,1)S(1)} %pad_maximum_fusion.own_ref), channel_id=1, source_target_pairs={{6,0},{0,2},{2,4},{4,6},{7,1},{1,3},{3,5},{5,7},{14,8},{8,10},{10,... | collective-permute-start | bytes 491528 | tf_op jit(solution)/shard_map/ppermute | solution.py:26
  56.7 13.3 %collective-permute-start.3 = (bf16[64,1280]{1,0:T(8,128)(2,1)S(1)}, bf16[64,1280]{1,0:T(8,128)(2,1)S(1)}, u32[]{:S(2)}, u32[]{:S(2)}) collective-permute-start(bf16[64,1280]{1,0:T(8,128)(2,1)S(1)} %pad_maximum_fusion.own_ref), channel_id=1, source_target_pairs={{4,0},{6,2},{0,4},{2,6},{5,1},{7,3},{1,5},{3,7},{12,8},{14,10},{8,... | collective-permute-start | bytes 491528 | tf_op jit(solution)/shard_map/ppermute | solution.py:26
  62.4 10.5 %collective-permute-start.4 = (bf16[64,1280]{1,0:T(8,128)(2,1)S(1)}, bf16[64,1280]{1,0:T(8,128)(2,1)S(1)}, u32[]{:S(2)}, u32[]{:S(2)}) collective-permute-start(bf16[64,1280]{1,0:T(8,128)(2,1)S(1)} %pad_maximum_fusion.own_ref), channel_id=1, source_target_pairs={{2,0},{4,2},{6,4},{0,6},{3,1},{5,3},{7,5},{1,7},{10,8},{12,10},{14... | collective-permute-start | bytes 491528 | tf_op jit(solution)/shard_map/ppermute | solution.py:26
  72.8 4.0 %collective-permute-start.5 = (bf16[256,1280]{1,0:T(8,128)(2,1)S(1)}, bf16[256,1280]{1,0:T(8,128)(2,1)S(1)}, u32[]{:S(2)}, u32[]{:S(2)}) collective-permute-start(bf16[256,1280]{1,0:T(8,128)(2,1)S(1)} %constant_dynamic-update-slice_fusion.a_ref), channel_id=1, source_target_pairs={{1,0},{0,1},{3,2},{2,3},{5,4},{4,5},{7,6},{6,7},{9,8},{8,9},{11,10... | collective-permute-start | bytes 1966088 | tf_op jit(solution)/shard_map/ppermute | solution.py:26
  78.8 16.5 %all-to-all-start = ((bf16[8,144,128]{2,1,0:T(8,128)(2,1)}), bf16[8,144,128]{2,1,0:T(8,128)(2,1)S(1)}, u32[]{:S(2)}, u32[]{:S(2)}) async-start(bf16[8,144,128]{2,1,0:T(8,128)(2,1)} %bitcast.3), calls=%async_computation | async-start | bytes 589824 | tf_op jit(solution)/shard_map/all_to_all | solution.py:195
  82.4 33.6 %copy-start.4 = (bf16[16,1152]{1,0:T(8,128)(2,1)S(1)}, bf16[16,1152]{1,0:T(8,128)(2,1)}, u32[]{:S(2)}) copy-start(bf16[16,1152]{1,0:T(8,128)(2,1)} %text_ref.3) | copy-start | bytes 110596
  82.9 7.1 %collective-permute-start.6 = (bf16[32,1152]{1,0:T(8,128)(2,1)S(1)}, bf16[32,1152]{1,0:T(8,128)(2,1)S(1)}, u32[]{:S(2)}, u32[]{:S(2)}) collective-permute-start(bf16[32,1152]{1,0:T(8,128)(2,1)S(1)} %get-tuple-element.9), channel_id=1, source_target_pairs={{16,0},{24,8},{32,16},{40,24},{48,32},{56,40},{64,48},{72,56},{80,... | collective-permute-start | bytes 221192 | tf_op jit(solution)/shard_map/ppermute | solution.py:26
  95.3 1.4 %copy-start.2 = (bf16[1024,768]{1,0:T(8,128)(2,1)S(1)}, bf16[1024,768]{1,0:T(8,128)(2,1)}, u32[]{:S(2)}) copy-start(bf16[1024,768]{1,0:T(8,128)(2,1)} %all-gather.3.cloned.1.call-done) | copy-start | bytes 4718596
  98.2 19.8 %all-to-all-start.1 = ((bf16[16,54,128]{2,1,0:T(8,128)(2,1)}), bf16[16,54,128]{2,1,0:T(8,128)(2,1)S(1)}, u32[]{:S(2)}, u32[]{:S(2)}) async-start(bf16[16,54,128]{2,1,0:T(8,128)(2,1)} %head_side.1), calls=%async_computation.1 | async-start | bytes 458752 | tf_op jit(solution)/shard_map/all_to_all | solution.py:201
  101.7 14.2 %collective-permute-start.7 = (bf16[16,1152]{1,0:T(8,128)(2,1)S(1)}, bf16[16,1152]{1,0:T(8,128)(2,1)S(1)}, u32[]{:S(2)}, u32[]{:S(2)}) collective-permute-start(bf16[16,1152]{1,0:T(8,128)(2,1)S(1)} %get-tuple-element.11), channel_id=1, source_target_pairs={{8,0},{16,8},{24,16},{32,24},{40,32},{48,40},{56,48},{64,56},{72,6... | collective-permute-start | bytes 110600 | tf_op jit(solution)/shard_map/ppermute | solution.py:26
Sparse Core Ops, SparseCore 0:
  14.6 57.7 all-gather.2

commit v2 on v1

--- a/solution.py
+++ b/solution.py
@@ -76,15 +76,15 @@
     return (-signs * jax.nn.sigmoid(-signs * logits)).astype(bf16)
 
 
-def text_side(own_ref, image_ref, ids_ref, near_ref, far_ref):
+def text_side(own_ref, image_ref, ids_ref, kept_ref, away_ref):
     slope = slopes(own_ref[...], image_ref[...], ids_ref[...])
     share = SCALE * jnp.dot(slope, image_ref[...], preferred_element_type=f32)
-    half = near_ref.shape[0]
-    near_ref[...] = share[:half]
-    far_ref[...] = share[half:].astype(far_ref.dtype)
-
-
-def image_side(a_ref, b_ref, embed_ref, ids_ref, out_ref, turned_ref):
+    count = kept_ref.shape[0]
+    kept_ref[...] = share[:count]
+    away_ref[...] = share[count:].astype(away_ref.dtype)
+
+
+def image_side(a_ref, b_ref, embed_ref, ids_ref, _away, out_ref, turned_ref):
     floats = embed_ref[...].astype(f32)
     norms = norms_of(floats)
     units = floats / norms
@@ -127,16 +127,19 @@
         out_ref[:, g * 128 : (g + 1) * 128] = total[g * run : (g + 1) * run]
 
 
-def text_back(share_ref, last_ref, text_ref, out_ref):
+def text_back(share_ref, one_ref, two_ref, three_ref, text_ref, out_ref):
     floats = text_ref[...].astype(f32)
     norms = norms_of(floats)
     units = floats / norms
-    total = share_ref[...] + last_ref[...].astype(f32)
+    total = share_ref[...]
+    for ref in (one_ref, two_ref, three_ref):
+        total = total + ref[...].astype(f32)
     out_ref[...] = (total - units * jnp.sum(units * total, -1, keepdims=True)) / norms
 
 
-def call(kernel, shapes, *args, smem=0):
-    specs = [pl.BlockSpec(memory_space=pltpu.SMEM)] * smem + vmem(len(args) - smem)
+def call(kernel, shapes, *args, smem=0, after=0):
+    specs = [pl.BlockSpec(memory_space=pltpu.SMEM)] * smem + vmem(len(args) - smem - after)
+    specs += [pl.BlockSpec(memory_space=pl.ANY)] * after
     outs = [jax.ShapeDtypeStruct(s, d) for s, d in shapes]
     single = len(outs) == 1
     return pl.pallas_call(
@@ -159,46 +162,45 @@
     across = lax.axis_size("xh") * lax.axis_size("y")
     own_width = width // planes
 
-    feats = lax.all_gather(image_feat, "z", axis=0, tiled=False)
-
     payload = call(
         prepare, [((texts, width + TAIL), bf16)],
         position, domain_bias, text_embed, ids, domain.reshape(1, images), smem=2,
     )
+    payload, feat = lax.optimization_barrier((payload, image_feat))
+    feats = jnp.broadcast_to(feat[None], (planes, images, features))
+    feats = lax.all_to_all(feats, "z", 0, 0, tiled=True)
     floats = image_embed.astype(f32)
     image_round = (floats / norms_of(floats)).astype(bf16)
 
-    two = jnp.concatenate([payload, shifted(payload, BLK, 1)], 0)
-    own = jnp.concatenate([two, shifted(two, BLK, 2)], 0)
+    own = jnp.concatenate([payload] + [shifted(payload, BLK, d) for d in (1, 2, 3)], 0)
 
     turns = [shifted(own, "xl", d) for d in range(1, lax.axis_size("xl"))]
-    near, far = call(
-        text_side, [((2 * texts, width), f32), ((2 * texts, width), bf16)],
+    kept, away = call(
+        text_side, [((texts, width), f32), ((3 * texts, width), bf16)],
         own, image_round, ids,
     )
     here = jnp.concatenate([own] + turns, 0)
     there = shifted(here, "core", 1)
-
-    back = shifted(far, BLK, -2).astype(f32)
-    stay = near[:texts] + back[:texts]
-    pass_on = (near[texts:] + back[texts:]).astype(bf16)
-    last = shifted(pass_on, BLK, -1)
-    text_grad = call(text_back, [((texts, width), f32)], stay, last, text_embed)
 
     pieces = lax.axis_size("xh")
     run = width // (planes * pieces)
     embed_grad, turned = call(
         image_side,
         [((images, width), bf16), ((planes, pieces, run, images), bf16)],
-        here, there, image_embed, ids,
-    )
+        here, there, image_embed, ids, away, after=1,
+    )
+    turned, feats = lax.optimization_barrier((turned, feats))
     plane = lax.all_to_all(turned.reshape(planes, own_width, images), "z", 0, 0, tiled=True)
-    image_grad = jnp.dot(embed_grad, head, preferred_element_type=f32).astype(bf16)
+
+    backs = [shifted(away[(d - 1) * texts : d * texts], BLK, -d) for d in (1, 2, 3)]
+
     rows = own_width // across
     parts = call(
         head_side, [((across, rows * features // 128, 128), bf16)], plane, feats
     )
     parts = lax.all_to_all(parts, ("xh", "y"), 0, 0, tiled=True)
+    text_grad = call(text_back, [((texts, width), f32)], kept, *backs, text_embed)
+    image_grad = jnp.dot(embed_grad, head, preferred_element_type=f32).astype(bf16)
     head_grad = call(head_sum, [((rows, features), f32)], parts)
     return (image_grad, text_grad, head_grad)
 

time: 126 us -> 125 us (level)
  the two profiles are of different devices: /device:TPU:2 before, /device:TPU:16 now
where the time goes in v2:
time: 125 us; the launch traced here: 124 us
  starting transfers between devices  68.4 us (55%)
  waiting for transfers between devices  21.2 us (17%)
  blocking collectives  16.6 us (13%)
  local copies, waits for them, and re-layouts  8.83 us (7%)
  Pallas kernels  4.61 us (4%)
  matrix products  2.07 us (2%)
    ppermute x10, starting transfers between devices, shifted(): lax.ppermute(block, axis, [((i - distance) % size, i) for i in range(size)])  42.5 us
    ppermute x10, waiting for transfers between devices, shifted(): lax.ppermute(block, axis, [((i - distance) % size, i) for i in range(size)])  21.2 us
    all_to_all x1, starting transfers between devices, local(): feats = lax.all_to_all(feats, 'z', 0, 0, tiled=True)  16.7 us
    all_to_all x1, blocking collectives, local(): lax.all_to_all(turned.reshape(planes, own_width, images), 'z', 0, 0, tile...  16.6 us
    all_to_all x1, starting transfers between devices, local(): parts = lax.all_to_all(parts, ('xh', 'y'), 0, 0, tiled=True)  9.17 us
    unnamed x31, local copies, waits for them, and re-layouts  6.57 us
    pallas_call x6, Pallas kernels, call(): pl.pallas_call(kernel, out_shape=outs[0] if single else outs, in_specs=sp...  4.61 us
  transfers between devices with their start and end apart: 12, of which 6 were waited for; matrix products, arithmetic and copies ran while one was open for 3% of the time, Pallas kernels for 2%

profile of v2, /device:TPU:16, one launch (start us, length us, event | category | flops | bytes accessed | tf_op | source)
XLA Modules:
  0.0 123.8 jit_solution(6867642957277064299)
XLA Ops:
  0.7 0.9 copy-done.5
  1.6 0.7 copy-done.9
  2.9 0.7 copy-done.12
  4.2 2.2 %broadcast_in_dim.2 = bf16[8,128,768]{2,1,0:T(8,128)(2,1)} broadcast(bf16[128,768]{1,0:T(8,128)(2,1)} %param.9), dimensions={1,2} | broadcast | bytes 1769472 | tf_op jit(solution)/shard_map/broadcast_in_dim | solution.py:170
  6.4 16.7 %all-to-all-start = ((bf16[8,128,768]{2,1,0:T(8,128)(2,1)}), bf16[8,128,768]{2,1,0:T(8,128)(2,1)S(1)}, u32[]{:S(2)}, u32[]{:S(2)}) async-start(bf16[8,128,768]{2,1,0:T(8,128)(2,1)} %broadcast_in_dim.2), calls=%async_computation | async-start | bytes 3145728 | tf_op jit(solution)/shard_map/all_to_all | solution.py:171
  23.1 7.2 %collective-permute-start.2 = (bf16[16,1280]{1,0:T(8,128)(2,1)S(1)}, bf16[16,1280]{1,0:T(8,128)(2,1)S(1)}, u32[]{:S(2)}, u32[]{:S(2)}) collective-permute-start(bf16[16,1280]{1,0:T(8,128)(2,1)S(1)} %prepare.1), channel_id=1, source_target_pairs={{1000,0},{1008,8},{1016,16},{0,24},{8,32},{16,40},{24,48},{32,56},... | collective-permute-start | bytes 122888 | tf_op jit(solution)/shard_map/ppermute | solution.py:26
  30.3 2.9 %collective-permute-start.1 = (bf16[16,1280]{1,0:T(8,128)(2,1)S(1)}, bf16[16,1280]{1,0:T(8,128)(2,1)S(1)}, u32[]{:S(2)}, u32[]{:S(2)}) collective-permute-start(bf16[16,1280]{1,0:T(8,128)(2,1)S(1)} %prepare.1), channel_id=1, source_target_pairs={{1008,0},{1016,8},{0,16},{8,24},{16,32},{24,40},{32,48},{40,56},{4... | collective-permute-start | bytes 122888 | tf_op jit(solution)/shard_map/ppermute | solution.py:26
  33.2 2.7 %collective-permute-start = (bf16[16,1280]{1,0:T(8,128)(2,1)S(1)}, bf16[16,1280]{1,0:T(8,128)(2,1)S(1)}, u32[]{:S(2)}, u32[]{:S(2)}) collective-permute-start(bf16[16,1280]{1,0:T(8,128)(2,1)S(1)} %prepare.1), channel_id=1, source_target_pairs={{1016,0},{0,8},{8,16},{16,24},{24,32},{32,40},{40,48},{48,56},{56,... | collective-permute-start | bytes 122888 | tf_op jit(solution)/shard_map/ppermute | solution.py:26
  36.0 3.2 %collective-permute-done = bf16[16,1280]{1,0:T(8,128)(2,1)S(1)} collective-permute-done((bf16[16,1280]{1,0:T(8,128)(2,1)S(1)}, bf16[16,1280]{1,0:T(8,128)(2,1)S(1)}, u32[]{:S(2)}, u32[]{:S(2)}) %collective-permute-start) | collective-permute-done | bytes 40992 | tf_op jit(solution)/shard_map/ppermute | solution.py:26
  39.1 6.4 %collective-permute-done.1 = bf16[16,1280]{1,0:T(8,128)(2,1)S(1)} collective-permute-done((bf16[16,1280]{1,0:T(8,128)(2,1)S(1)}, bf16[16,1280]{1,0:T(8,128)(2,1)S(1)}, u32[]{:S(2)}, u32[]{:S(2)}) %collective-permute-start.1) | collective-permute-done | bytes 40992 | tf_op jit(solution)/shard_map/ppermute | solution.py:26
  45.6 3.9 %collective-permute-start.3 = (bf16[64,1280]{1,0:T(8,128)(2,1)S(1)}, bf16[64,1280]{1,0:T(8,128)(2,1)S(1)}, u32[]{:S(2)}, u32[]{:S(2)}) collective-permute-start(bf16[64,1280]{1,0:T(8,128)(2,1)S(1)} %get-tuple-element.22.own_ref), channel_id=1, source_target_pairs={{6,0},{0,2},{2,4},{4,6},{7,1},{1,3},{3,5},{5,7},{14,8},{8,10},{10,... | collective-permute-start | bytes 491528 | tf_op jit(solution)/shard_map/ppermute | solution.py:26
  49.6 1.1 fusion
  50.7 3.7 %collective-permute-start.5 = (bf16[64,1280]{1,0:T(8,128)(2,1)S(1)}, bf16[64,1280]{1,0:T(8,128)(2,1)S(1)}, u32[]{:S(2)}, u32[]{:S(2)}) collective-permute-start(bf16[64,1280]{1,0:T(8,128)(2,1)S(1)} %get-tuple-element.22.own_ref), channel_id=1, source_target_pairs={{2,0},{4,2},{6,4},{0,6},{3,1},{5,3},{7,5},{1,7},{10,8},{12,10},{14... | collective-permute-start | bytes 491528 | tf_op jit(solution)/shard_map/ppermute | solution.py:26
  54.4 3.5 %collective-permute-start.4 = (bf16[64,1280]{1,0:T(8,128)(2,1)S(1)}, bf16[64,1280]{1,0:T(8,128)(2,1)S(1)}, u32[]{:S(2)}, u32[]{:S(2)}) collective-permute-start(bf16[64,1280]{1,0:T(8,128)(2,1)S(1)} %get-tuple-element.22.own_ref), channel_id=1, source_target_pairs={{4,0},{6,2},{0,4},{2,6},{5,1},{7,3},{1,5},{3,7},{12,8},{14,10},{8,... | collective-permute-start | bytes 491528 | tf_op jit(solution)/shard_map/ppermute | solution.py:26
  57.9 7.4 %collective-permute-done.4 = bf16[64,1280]{1,0:T(8,128)(2,1)S(1)} collective-permute-done((bf16[64,1280]{1,0:T(8,128)(2,1)S(1)}, bf16[64,1280]{1,0:T(8,128)(2,1)S(1)}, u32[]{:S(2)}, u32[]{:S(2)}) %collective-permute-start.4) | collective-permute-done | bytes 163872 | tf_op jit(solution)/shard_map/ppermute | solution.py:26
  65.3 1.9 %collective-permute-start.6 = (bf16[256,1280]{1,0:T(8,128)(2,1)S(1)}, bf16[256,1280]{1,0:T(8,128)(2,1)S(1)}, u32[]{:S(2)}, u32[]{:S(2)}) collective-permute-start(bf16[256,1280]{1,0:T(8,128)(2,1)S(1)} %constant_dynamic-update-slice_fusion.4.a_ref), channel_id=1, source_target_pairs={{1,0},{0,1},{3,2},{2,3},{5,4},{4,5},{7,6},{6,7},{9,8},{8,9},{11,10... | collective-permute-start | bytes 1966088 | tf_op jit(solution)/shard_map/ppermute | solution.py:26
  68.5 0.8 collective-permute-done.6.b_ref
  69.3 1.3 %image_side.1 = (bf16[128,1152]{1,0:T(8,128)(2,1)S(1)}, bf16[8,2,72,128]{3,2,1,0:T(8,128)(2,1)S(1)}) custom-call(bf16[256,1280]{1,0:T(8,128)(2,1)S(1)} %constant_dynamic-update-slice_fusion.4.a_ref, bf16[256,1280]{1,0:T(8,128)(2,1)S(1)} %collective-permute-done.6.b_ref, bf16[128,1152]{1,0:T(8,128)(2,1)S(1)} %copy-done.1, s32[1,128]{1,0:T(1,128)S(1)} %bitcast.9, ...), custom_call_target="tpu_custom_call" | custom-call | tf_op jit(solution)/shard_map/image_side/pallas_call | solution.py:145
  70.6 0.7 copy-done.3
  71.3 0.7 copy-done.4
  72.0 16.6 %all_to_all.15.turned_ref = bf16[8,144,128]{2,1,0:T(8,128)(2,1)S(1)} all-to-all(bf16[8,144,128]{2,1,0:T(8,128)(2,1)} %bitcast.6), channel_id=1, replica_groups=mesh['xh'=2,'z'=8,'y'=8,'xl'=4,'core'=2] {'z'}, dimensions={0} | all-to-all | bytes 589824 | tf_op jit(solution)/shard_map/all_to_all | solution.py:193
  88.7 0.7 head_side.1
  89.4 0.7 copy-done.2
  90.1 9.2 %all-to-all-start.2 = ((bf16[16,54,128]{2,1,0:T(8,128)(2,1)}), bf16[16,54,128]{2,1,0:T(8,128)(2,1)S(1)}, u32[]{:S(2)}, u32[]{:S(2)}) async-start(bf16[16,54,128]{2,1,0:T(8,128)(2,1)} %copy-done.2), calls=%async_computation.2 | async-start | bytes 458752 | tf_op jit(solution)/shard_map/all_to_all | solution.py:201
  99.2 10.0 %collective-permute-start.9 = (bf16[16,1152]{1,0:T(8,128)(2,1)S(1)}, bf16[16,1152]{1,0:T(8,128)(2,1)S(1)}, u32[]{:S(2)}, u32[]{:S(2)}) collective-permute-start(bf16[16,1152]{1,0:T(8,128)(2,1)S(1)} %get-tuple-element.19), channel_id=1, source_target_pairs={{24,0},{32,8},{40,16},{48,24},{56,32},{64,40},{72,48},{80,56},{88,... | collective-permute-start | bytes 110600 | tf_op jit(solution)/shard_map/ppermute | solution.py:26
  109.2 4.3 %collective-permute-start.8 = (bf16[16,1152]{1,0:T(8,128)(2,1)S(1)}, bf16[16,1152]{1,0:T(8,128)(2,1)S(1)}, u32[]{:S(2)}, u32[]{:S(2)}) collective-permute-start(bf16[16,1152]{1,0:T(8,128)(2,1)S(1)} %get-tuple-element.20), channel_id=1, source_target_pairs={{16,0},{24,8},{32,16},{40,24},{48,32},{56,40},{64,48},{72,56},{80,... | collective-permute-start | bytes 110600 | tf_op jit(solution)/shard_map/ppermute | solution.py:26
  113.5 2.5 %collective-permute-start.7 = (bf16[16,1152]{1,0:T(8,128)(2,1)S(1)}, bf16[16,1152]{1,0:T(8,128)(2,1)S(1)}, u32[]{:S(2)}, u32[]{:S(2)}) collective-permute-start(bf16[16,1152]{1,0:T(8,128)(2,1)S(1)} %get-tuple-element.21), channel_id=1, source_target_pairs={{8,0},{16,8},{24,16},{32,24},{40,32},{48,40},{56,48},{64,56},{72,6... | collective-permute-start | bytes 110600 | tf_op jit(solution)/shard_map/ppermute | solution.py:26
  116.1 3.3 %collective-permute-done.7.one_ref = bf16[16,1152]{1,0:T(8,128)(2,1)S(1)} collective-permute-done((bf16[16,1152]{1,0:T(8,128)(2,1)S(1)}, bf16[16,1152]{1,0:T(8,128)(2,1)S(1)}, u32[]{:S(2)}, u32[]{:S(2)}) %collective-permute-start.7) | collective-permute-done | bytes 36896 | tf_op jit(solution)/shard_map/ppermute | solution.py:26
  119.4 0.9 copy-done.8
  120.3 0.8 text_back.1
  121.1 2.1 %convolution_convert_fusion = bf16[128,768]{1,0:T(8,128)(2,1)} fusion(bf16[128,1152]{1,0:T(8,128)(2,1)} %copy-done.3, bf16[1152,768]{1,0:T(8,128)(2,1)S(1)} %copy-done), kind=kOutput, calls=%fused_computation | convolution fusion | flops 226590720 | bytes 2260992 | tf_op jit(solution)/shard_map/dot_general | solution.py:203
  123.2 0.7 head_sum.1
  (38 shorter events, 2.7 us)
Async XLA Ops:
  0.6 120.5 %copy-start = (bf16[1152,768]{1,0:T(8,128)(2,1)S(1)}, bf16[1152,768]{1,0:T(8,128)(2,1)}, u32[]{:S(2)}) copy-start(bf16[1152,768]{1,0:T(8,128)(2,1)} %param.10) | copy-start | bytes 5308420
  0.7 0.9 copy-start.5
  1.6 0.7 copy-start.9
  2.2 0.7 copy-start.11
  2.9 0.7 copy-start.12
  6.4 65.6 %all-to-all-start = ((bf16[8,128,768]{2,1,0:T(8,128)(2,1)}), bf16[8,128,768]{2,1,0:T(8,128)(2,1)S(1)}, u32[]{:S(2)}, u32[]{:S(2)}) async-start(bf16[8,128,768]{2,1,0:T(8,128)(2,1)} %broadcast_in_dim.2), calls=%async_computation | async-start | bytes 3145728 | tf_op jit(solution)/shard_map/all_to_all | solution.py:171
  23.1 44.2 %copy-start.1 = (bf16[128,1152]{1,0:T(8,128)(2,1)S(1)}, bf16[128,1152]{1,0:T(8,128)(2,1)}, u32[]{:S(2)}) copy-start(bf16[128,1152]{1,0:T(8,128)(2,1)} %embed_ref.1) | copy-start | bytes 884740
  23.1 44.3 %copy-start.10 = (s32[128]{0:T(128)S(1)}, s32[128]{0:T(128)}, u32[]{:S(2)}) copy-start(s32[128]{0:T(128)} %param.11) | copy-start | bytes 1540
  23.1 22.5 %collective-permute-start.2 = (bf16[16,1280]{1,0:T(8,128)(2,1)S(1)}, bf16[16,1280]{1,0:T(8,128)(2,1)S(1)}, u32[]{:S(2)}, u32[]{:S(2)}) collective-permute-start(bf16[16,1280]{1,0:T(8,128)(2,1)S(1)} %prepare.1), channel_id=1, source_target_pairs={{1000,0},{1008,8},{1016,16},{0,24},{8,32},{16,40},{24,48},{32,56},... | collective-permute-start | bytes 122888 | tf_op jit(solution)/shard_map/ppermute | solution.py:26
  30.3 15.3 %collective-permute-start.1 = (bf16[16,1280]{1,0:T(8,128)(2,1)S(1)}, bf16[16,1280]{1,0:T(8,128)(2,1)S(1)}, u32[]{:S(2)}, u32[]{:S(2)}) collective-permute-start(bf16[16,1280]{1,0:T(8,128)(2,1)S(1)} %prepare.1), channel_id=1, source_target_pairs={{1008,0},{1016,8},{0,16},{8,24},{16,32},{24,40},{32,48},{40,56},{4... | collective-permute-start | bytes 122888 | tf_op jit(solution)/shard_map/ppermute | solution.py:26
  33.2 5.9 %collective-permute-start = (bf16[16,1280]{1,0:T(8,128)(2,1)S(1)}, bf16[16,1280]{1,0:T(8,128)(2,1)S(1)}, u32[]{:S(2)}, u32[]{:S(2)}) collective-permute-start(bf16[16,1280]{1,0:T(8,128)(2,1)S(1)} %prepare.1), channel_id=1, source_target_pairs={{1016,0},{0,8},{8,16},{16,24},{24,32},{32,40},{40,48},{48,56},{56,... | collective-permute-start | bytes 122888 | tf_op jit(solution)/shard_map/ppermute | solution.py:26
  45.6 12.2 %collective-permute-start.3 = (bf16[64,1280]{1,0:T(8,128)(2,1)S(1)}, bf16[64,1280]{1,0:T(8,128)(2,1)S(1)}, u32[]{:S(2)}, u32[]{:S(2)}) collective-permute-start(bf16[64,1280]{1,0:T(8,128)(2,1)S(1)} %get-tuple-element.22.own_ref), channel_id=1, source_target_pairs={{6,0},{0,2},{2,4},{4,6},{7,1},{1,3},{3,5},{5,7},{14,8},{8,10},{10,... | collective-permute-start | bytes 491528 | tf_op jit(solution)/shard_map/ppermute | solution.py:26
  50.7 14.6 %collective-permute-start.5 = (bf16[64,1280]{1,0:T(8,128)(2,1)S(1)}, bf16[64,1280]{1,0:T(8,128)(2,1)S(1)}, u32[]{:S(2)}, u32[]{:S(2)}) collective-permute-start(bf16[64,1280]{1,0:T(8,128)(2,1)S(1)} %get-tuple-element.22.own_ref), channel_id=1, source_target_pairs={{2,0},{4,2},{6,4},{0,6},{3,1},{5,3},{7,5},{1,7},{10,8},{12,10},{14... | collective-permute-start | bytes 491528 | tf_op jit(solution)/shard_map/ppermute | solution.py:26
  54.4 10.9 %collective-permute-start.4 = (bf16[64,1280]{1,0:T(8,128)(2,1)S(1)}, bf16[64,1280]{1,0:T(8,128)(2,1)S(1)}, u32[]{:S(2)}, u32[]{:S(2)}) collective-permute-start(bf16[64,1280]{1,0:T(8,128)(2,1)S(1)} %get-tuple-element.22.own_ref), channel_id=1, source_target_pairs={{4,0},{6,2},{0,4},{2,6},{5,1},{7,3},{1,5},{3,7},{12,8},{14,10},{8,... | collective-permute-start | bytes 491528 | tf_op jit(solution)/shard_map/ppermute | solution.py:26
  65.3 4.0 %collective-permute-start.6 = (bf16[256,1280]{1,0:T(8,128)(2,1)S(1)}, bf16[256,1280]{1,0:T(8,128)(2,1)S(1)}, u32[]{:S(2)}, u32[]{:S(2)}) collective-permute-start(bf16[256,1280]{1,0:T(8,128)(2,1)S(1)} %constant_dynamic-update-slice_fusion.4.a_ref), channel_id=1, source_target_pairs={{1,0},{0,1},{3,2},{2,3},{5,4},{4,5},{7,6},{6,7},{9,8},{8,9},{11,10... | collective-permute-start | bytes 1966088 | tf_op jit(solution)/shard_map/ppermute | solution.py:26
  67.9 0.6 copy-start.7
  70.6 0.7 copy-start.3
  71.3 0.7 copy-start.4
  72.0 47.3 %copy-start.6 = (bf16[16,1152]{1,0:T(8,128)(2,1)S(1)}, bf16[16,1152]{1,0:T(8,128)(2,1)}, u32[]{:S(2)}) copy-start(bf16[16,1152]{1,0:T(8,128)(2,1)} %text_ref.3) | copy-start | bytes 110596
  89.4 0.7 copy-start.2
  90.1 33.1 %all-to-all-start.2 = ((bf16[16,54,128]{2,1,0:T(8,128)(2,1)}), bf16[16,54,128]{2,1,0:T(8,128)(2,1)S(1)}, u32[]{:S(2)}, u32[]{:S(2)}) async-start(bf16[16,54,128]{2,1,0:T(8,128)(2,1)} %copy-done.2), calls=%async_computation.2 | async-start | bytes 458752 | tf_op jit(solution)/shard_map/all_to_all | solution.py:201
  99.2 16.7 %collective-permute-start.9 = (bf16[16,1152]{1,0:T(8,128)(2,1)S(1)}, bf16[16,1152]{1,0:T(8,128)(2,1)S(1)}, u32[]{:S(2)}, u32[]{:S(2)}) collective-permute-start(bf16[16,1152]{1,0:T(8,128)(2,1)S(1)} %get-tuple-element.19), channel_id=1, source_target_pairs={{24,0},{32,8},{40,16},{48,24},{56,32},{64,40},{72,48},{80,56},{88,... | collective-permute-start | bytes 110600 | tf_op jit(solution)/shard_map/ppermute | solution.py:26
  109.2 6.9 %collective-permute-start.8 = (bf16[16,1152]{1,0:T(8,128)(2,1)S(1)}, bf16[16,1152]{1,0:T(8,128)(2,1)S(1)}, u32[]{:S(2)}, u32[]{:S(2)}) collective-permute-start(bf16[16,1152]{1,0:T(8,128)(2,1)S(1)} %get-tuple-element.20), channel_id=1, source_target_pairs={{16,0},{24,8},{32,16},{40,24},{48,32},{56,40},{64,48},{72,56},{80,... | collective-permute-start | bytes 110600 | tf_op jit(solution)/shard_map/ppermute | solution.py:26
  113.5 5.9 %collective-permute-start.7 = (bf16[16,1152]{1,0:T(8,128)(2,1)S(1)}, bf16[16,1152]{1,0:T(8,128)(2,1)S(1)}, u32[]{:S(2)}, u32[]{:S(2)}) collective-permute-start(bf16[16,1152]{1,0:T(8,128)(2,1)S(1)} %get-tuple-element.21), channel_id=1, source_target_pairs={{8,0},{16,8},{24,16},{32,24},{40,32},{48,40},{56,48},{64,56},{72,6... | collective-permute-start | bytes 110600 | tf_op jit(solution)/shard_map/ppermute | solution.py:26
  119.4 0.9 copy-start.8

commit v3 on v2

--- a/solution.py
+++ b/solution.py
@@ -18,7 +18,7 @@
 bf16, f32, i32 = jnp.bfloat16, jnp.float32, jnp.int32
 NT = (((1,), (1,)), ((), ()))
 TN = (((0,), (0,)), ((), ()))
-PARAMS = pltpu.CompilerParams(vmem_limit_bytes=32 * 1024 * 1024)
+ROOM = 32 * 1024 * 1024
 
 
 def shifted(block, axis, distance):
@@ -38,7 +38,13 @@
     return lax.broadcasted_iota(i32, shape, dim)
 
 
-def prepare(pos_ref, bias_ref, text_ref, ids_ref, domain_ref, out_ref):
+def prepare(pos_ref, text_hbm, ids_hbm, domain_hbm, bias_hbm, out_ref, text_ref, ids_ref, domain_ref, bias_ref, sems):
+    pairs = ((text_hbm, text_ref), (ids_hbm, ids_ref), (domain_hbm, domain_ref), (bias_hbm, bias_ref))
+    copies = [pltpu.make_async_copy(src, dst, sems.at[k]) for k, (src, dst) in enumerate(pairs)]
+    for copy in copies:
+        copy.start()
+    for copy in copies:
+        copy.wait()
     rows, width = text_ref.shape
     floats = text_ref[...].astype(f32)
     out_ref[:, :width] = (floats / norms_of(floats)).astype(bf16)
@@ -46,9 +52,9 @@
     mine = iota(wide, 1) == iota(wide, 0) + pos_ref[0] * rows
     own_id = jnp.sum(jnp.where(mine, ids_ref[...].astype(f32), 0.0), -1, keepdims=True)
     own_domain = jnp.sum(jnp.where(mine, domain_ref[...].astype(f32), 0.0), -1, keepdims=True)
-    bias = jnp.zeros((rows, 1), f32)
-    for k in range(bias_ref.shape[0]):
-        bias = bias + jnp.where(own_domain == float(k), bias_ref[k], 0.0)
+    table = (rows, bias_ref.shape[1])
+    chosen = own_domain.astype(i32) == iota(table, 1)
+    bias = jnp.sum(jnp.where(chosen, jnp.broadcast_to(bias_ref[...], table), 0.0), -1, keepdims=True)
     whole = own_id.astype(i32)
     high = (whole >> 6).astype(f32)
     low = (whole & 63).astype(f32)
@@ -60,6 +66,16 @@
     for k, part in enumerate((high, low, first, second, third)):
         tail = jnp.where(lane == k, part, tail)
     out_ref[:, width:] = tail.astype(bf16)
+
+
+def fan_out(embed_ref, feat_ref, _payload, round_ref, feats_hbm, sem):
+    copies = [pltpu.make_async_copy(feat_ref, feats_hbm.at[k], sem) for k in range(feats_hbm.shape[0])]
+    for copy in copies:
+        copy.start()
+    floats = embed_ref[...].astype(f32)
+    round_ref[...] = (floats / norms_of(floats)).astype(bf16)
+    for copy in copies:
+        copy.wait()
 
 
 def slopes(rows, image_round, ids):
@@ -76,15 +92,15 @@
     return (-signs * jax.nn.sigmoid(-signs * logits)).astype(bf16)
 
 
-def text_side(own_ref, image_ref, ids_ref, kept_ref, away_ref):
+def text_side(own_ref, image_ref, ids_ref, kept_ref, one_ref, two_ref, three_ref):
     slope = slopes(own_ref[...], image_ref[...], ids_ref[...])
     share = SCALE * jnp.dot(slope, image_ref[...], preferred_element_type=f32)
     count = kept_ref.shape[0]
-    kept_ref[...] = share[:count]
-    away_ref[...] = share[count:].astype(away_ref.dtype)
-
-
-def image_side(a_ref, b_ref, embed_ref, ids_ref, _away, out_ref, turned_ref):
+    for k, ref in enumerate((kept_ref, one_ref, two_ref, three_ref)):
+        ref[...] = share[k * count : (k + 1) * count].astype(ref.dtype)
+
+
+def image_side(a_ref, b_ref, embed_ref, ids_ref, out_ref, turned_ref):
     floats = embed_ref[...].astype(f32)
     norms = norms_of(floats)
     units = floats / norms
@@ -137,19 +153,28 @@
     out_ref[...] = (total - units * jnp.sum(units * total, -1, keepdims=True)) / norms
 
 
-def call(kernel, shapes, *args, smem=0, after=0):
-    specs = [pl.BlockSpec(memory_space=pltpu.SMEM)] * smem + vmem(len(args) - smem - after)
+def call(kernel, shapes, *args, smem=0, hbm=0, after=0, out_hbm=0, scratch=(), cost=None, room=None):
+    specs = [pl.BlockSpec(memory_space=pltpu.SMEM)] * smem
+    specs += [pl.BlockSpec(memory_space=pltpu.HBM)] * hbm
+    specs += vmem(len(args) - smem - hbm - after)
     specs += [pl.BlockSpec(memory_space=pl.ANY)] * after
     outs = [jax.ShapeDtypeStruct(s, d) for s, d in shapes]
+    out_specs = vmem(len(outs) - out_hbm) + [pl.BlockSpec(memory_space=pltpu.HBM)] * out_hbm
     single = len(outs) == 1
     return pl.pallas_call(
         kernel,
         out_shape=outs[0] if single else outs,
         in_specs=specs,
-        out_specs=vmem(1)[0] if single else vmem(len(outs)),
-        compiler_params=PARAMS,
+        out_specs=out_specs[0] if single else out_specs,
+        scratch_shapes=list(scratch),
+        compiler_params=pltpu.CompilerParams(vmem_limit_bytes=room),
+        cost_estimate=cost,
         name=kernel.__name__,
     )(*args)
+
+
+def lasting(us):
+    return pl.CostEstimate(flops=int(us * 1e9), bytes_accessed=0, transcendentals=0)
 
 
 def local(image_embed, text_embed, image_feat, head, sample_id, domain, domain_bias):
@@ -162,46 +187,49 @@
     across = lax.axis_size("xh") * lax.axis_size("y")
     own_width = width // planes
 
+    inputs = (text_embed, ids, domain.reshape(1, images), domain_bias.reshape(1, -1))
     payload = call(
-        prepare, [((texts, width + TAIL), bf16)],
-        position, domain_bias, text_embed, ids, domain.reshape(1, images), smem=2,
-    )
-    payload, feat = lax.optimization_barrier((payload, image_feat))
-    feats = jnp.broadcast_to(feat[None], (planes, images, features))
+        prepare, [((texts, width + TAIL), bf16)], position, *inputs, smem=1, hbm=4,
+        scratch=[pltpu.VMEM(v.shape, v.dtype) for v in inputs] + [pltpu.SemaphoreType.DMA((4,))],
+    )
+    image_round, feats = call(
+        fan_out, [((images, width), bf16), ((planes, images, features), bf16)],
+        image_embed, image_feat, payload, after=1, out_hbm=1,
+        scratch=[pltpu.SemaphoreType.DMA], cost=lasting(20),
+    )
     feats = lax.all_to_all(feats, "z", 0, 0, tiled=True)
-    floats = image_embed.astype(f32)
-    image_round = (floats / norms_of(floats)).astype(bf16)
 
     own = jnp.concatenate([payload] + [shifted(payload, BLK, d) for d in (1, 2, 3)], 0)
 
-    turns = [shifted(own, "xl", d) for d in range(1, lax.axis_size("xl"))]
-    kept, away = call(
-        text_side, [((texts, width), f32), ((3 * texts, width), bf16)],
+    here = lax.all_gather(own, "xl", axis=0, tiled=True)
+    there = shifted(here, "core", 1)
+    kept, *aways = call(
+        text_side, [((texts, width), f32)] + [((texts, width), bf16)] * 3,
         own, image_round, ids,
     )
-    here = jnp.concatenate([own] + turns, 0)
-    there = shifted(here, "core", 1)
 
     pieces = lax.axis_size("xh")
     run = width // (planes * pieces)
     embed_grad, turned = call(
         image_side,
         [((images, width), bf16), ((planes, pieces, run, images), bf16)],
-        here, there, image_embed, ids, away, after=1,
+        here, there, image_embed, ids,
     )
     turned, feats = lax.optimization_barrier((turned, feats))
     plane = lax.all_to_all(turned.reshape(planes, own_width, images), "z", 0, 0, tiled=True)
 
-    backs = [shifted(away[(d - 1) * texts : d * texts], BLK, -d) for d in (1, 2, 3)]
+    backs = [shifted(away, BLK, -d) for d, away in zip((1, 2, 3), aways)]
 
     rows = own_width // across
     parts = call(
-        head_side, [((across, rows * features // 128, 128), bf16)], plane, feats
+        head_side, [((across, rows * features // 128, 128), bf16)], plane, feats, room=ROOM
     )
     parts = lax.all_to_all(parts, ("xh", "y"), 0, 0, tiled=True)
-    text_grad = call(text_back, [((texts, width), f32)], kept, *backs, text_embed)
+    text_grad = call(
+        text_back, [((texts, width), f32)], kept, *backs, text_embed, cost=lasting(60), room=ROOM
+    )
     image_grad = jnp.dot(embed_grad, head, preferred_element_type=f32).astype(bf16)
-    head_grad = call(head_sum, [((rows, features), f32)], parts)
+    head_grad = call(head_sum, [((rows, features), f32)], parts, room=ROOM)
     return (image_grad, text_grad, head_grad)
 
 

time: 125 us -> 115 us (0.920)
  starting transfers between devices: 68.4 us -> 57.3 us
  Pallas kernels: 4.61 us -> 14.1 us
  local copies, waits for them, and re-layouts: 8.83 us -> 1.56 us
    all_gather x0 -> x1, blocking collectives: none -> 17.6 us  [local(): here = lax.all_gather(own, 'xl', axis=0, tiled=True)]
    all_to_all x1 -> x0, blocking collectives: 16.6 us -> none  [local(): lax.all_to_all(turned.reshape(planes, own_width, images), 'z', 0, 0, tile...]
    ppermute x10 -> x7, starting transfers between devices: 42.5 us -> 28.1 us  [shifted(): lax.ppermute(block, axis, [((i - distance) % size, i) for i in range(size)])]
    pallas_call x6 -> x7, Pallas kernels: 4.61 us -> 14.1 us  [call(): pl.pallas_call(kernel, out_shape=outs[0] if single else outs, in_specs=sp...]
    ppermute x10 -> x7, waiting for transfers between devices: 21.2 us -> 11.9 us  [shifted(): lax.ppermute(block, axis, [((i - distance) % size, i) for i in range(size)])]
    all_to_all x1, waiting for transfers between devices: 0.01 us -> 9.14 us  [local(): parts = lax.all_to_all(parts, ('xh', 'y'), 0, 0, tiled=True)]
    unnamed x31 -> x16, local copies, waits for them, and re-layouts: 6.57 us -> 1.56 us
    all_to_all x0 -> x1, starting transfers between devices: none -> 4.19 us  [local(): lax.all_to_all(turned.reshape(planes, own_width, images), 'z', 0, 0, tile...]
  transfers between devices with their start and end apart: 12 -> 10, of which waited for: 6 -> 4; matrix products, arithmetic and copies ran while one was open for 3% -> 2% of each run, Pallas kernels for 2% -> 8%
where the time goes in v3:
time: 115 us; the launch traced here: 114 us
  starting transfers between devices  57.3 us (50%)
  waiting for transfers between devices  21 us (18%)
  blocking collectives  17.6 us (15%)
  Pallas kernels  14.1 us (12%)
  local copies, waits for them, and re-layouts  1.56 us (1%)
    ppermute x7, starting transfers between devices, shifted(): lax.ppermute(block, axis, [((i - distance) % size, i) for i in range(size)])  28.1 us
    all_gather x1, blocking collectives, local(): here = lax.all_gather(own, 'xl', axis=0, tiled=True)  17.6 us
    all_to_all x1, starting transfers between devices, local(): feats = lax.all_to_all(feats, 'z', 0, 0, tiled=True)  16.7 us
    pallas_call x7, Pallas kernels, call(): pl.pallas_call(kernel, out_shape=outs[0] if single else outs, in_specs=sp...  14.1 us
    ppermute x7, waiting for transfers between devices, shifted(): lax.ppermute(block, axis, [((i - distance) % size, i) for i in range(size)])  11.9 us
    all_to_all x1, waiting for transfers between devices, local(): parts = lax.all_to_all(parts, ('xh', 'y'), 0, 0, tiled=True)  9.14 us
    all_to_all x1, starting transfers between devices, local(): parts = lax.all_to_all(parts, ('xh', 'y'), 0, 0, tiled=True)  8.31 us
    all_to_all x1, starting transfers between devices, local(): lax.all_to_all(turned.reshape(planes, own_width, images), 'z', 0, 0, tile...  4.19 us
  transfers between devices with their start and end apart: 10, of which 4 were waited for; matrix products, arithmetic and copies ran while one was open for 2% of the time, Pallas kernels for 8%

profile of v3, /device:TPU:16, one launch (start us, length us, event | category | flops | bytes accessed | tf_op | source)
XLA Modules:
  0.0 114.3 jit_solution(6728303753290936566)
XLA Ops:
  0.6 0.0 copy-start
  0.7 1.7 %prepare.1._payload = bf16[16,1280]{1,0:T(8,128)(2,1)} custom-call(s32[1]{0:T(128)} %bitcast.pos_ref, bf16[16,1152]{1,0:T(8,128)(2,1)} %text_ref.1, s32[1,128]{1,0:T(1,128)} %bitcast.8, s32[1,128]{1,0:T(1,128)} %bitcast.11, f32[1,8]{1,0:T(1,128)} %bitcast.12), custom_call_target="tpu_custom_call" | custom-call | tf_op jit(solution)/shard_map/prepare/pallas_call | solution.py:164
  2.4 2.9 %fan_out.1 = (bf16[128,1152]{1,0:T(8,128)(2,1)}, bf16[8,128,768]{2,1,0:T(8,128)(2,1)}) custom-call(bf16[128,1152]{1,0:T(8,128)(2,1)} %embed_ref.3, bf16[128,768]{1,0:T(8,128)(2,1)} %feat_ref.1, bf16[16,1280]{1,0:T(8,128)(2,1)} %prepare.1._payload), custom_call_target="tpu_custom_call" | custom-call | flops 20000000000 | tf_op jit(solution)/shard_map/fan_out/pallas_call | solution.py:164
  5.3 0.0 copy-start.7
  5.3 16.7 %all-to-all-start = ((bf16[8,128,768]{2,1,0:T(8,128)(2,1)}), bf16[8,128,768]{2,1,0:T(8,128)(2,1)S(1)}, u32[]{:S(2)}, u32[]{:S(2)}) async-start(bf16[8,128,768]{2,1,0:T(8,128)(2,1)} %get-tuple-element.20), calls=%async_computation | async-start | bytes 3145728 | tf_op jit(solution)/shard_map/all_to_all | solution.py:200
  22.0 7.1 %collective-permute-start.2 = (bf16[16,1280]{1,0:T(8,128)(2,1)S(1)}, bf16[16,1280]{1,0:T(8,128)(2,1)S(1)}, u32[]{:S(2)}, u32[]{:S(2)}) collective-permute-start(bf16[16,1280]{1,0:T(8,128)(2,1)S(1)} %copy-done.7), channel_id=1, source_target_pairs={{1000,0},{1008,8},{1016,16},{0,24},{8,32},{16,40},{24,48},{32,56},... | collective-permute-start | bytes 122888 | tf_op jit(solution)/shard_map/ppermute | solution.py:26
  29.1 2.9 %collective-permute-start.1 = (bf16[16,1280]{1,0:T(8,128)(2,1)S(1)}, bf16[16,1280]{1,0:T(8,128)(2,1)S(1)}, u32[]{:S(2)}, u32[]{:S(2)}) collective-permute-start(bf16[16,1280]{1,0:T(8,128)(2,1)S(1)} %copy-done.7), channel_id=1, source_target_pairs={{1008,0},{1016,8},{0,16},{8,24},{16,32},{24,40},{32,48},{40,56},{4... | collective-permute-start | bytes 122888 | tf_op jit(solution)/shard_map/ppermute | solution.py:26
  32.0 2.7 %collective-permute-start = (bf16[16,1280]{1,0:T(8,128)(2,1)S(1)}, bf16[16,1280]{1,0:T(8,128)(2,1)S(1)}, u32[]{:S(2)}, u32[]{:S(2)}) collective-permute-start(bf16[16,1280]{1,0:T(8,128)(2,1)S(1)} %copy-done.7), channel_id=1, source_target_pairs={{1016,0},{0,8},{8,16},{16,24},{24,32},{32,40},{40,48},{48,56},{56,... | collective-permute-start | bytes 122888 | tf_op jit(solution)/shard_map/ppermute | solution.py:26
  34.7 3.9 %collective-permute-done.2 = bf16[16,1280]{1,0:T(8,128)(2,1)S(1)} collective-permute-done((bf16[16,1280]{1,0:T(8,128)(2,1)S(1)}, bf16[16,1280]{1,0:T(8,128)(2,1)S(1)}, u32[]{:S(2)}, u32[]{:S(2)}) %collective-permute-start.2) | collective-permute-done | bytes 40992 | tf_op jit(solution)/shard_map/ppermute | solution.py:26
  38.6 5.8 %collective-permute-done.1 = bf16[16,1280]{1,0:T(8,128)(2,1)S(1)} collective-permute-done((bf16[16,1280]{1,0:T(8,128)(2,1)S(1)}, bf16[16,1280]{1,0:T(8,128)(2,1)S(1)}, u32[]{:S(2)}, u32[]{:S(2)}) %collective-permute-start.1) | collective-permute-done | bytes 40992 | tf_op jit(solution)/shard_map/ppermute | solution.py:26
  44.4 0.0 collective-permute-done
  44.4 0.8 pad_maximum_fusion.own_ref
  45.2 0.0 copy-start.5
  45.2 17.6 %all_gather.3.a_ref = bf16[256,1280]{1,0:T(8,128)(2,1)S(1)} all-gather(bf16[64,1280]{1,0:T(8,128)(2,1)S(1)} %pad_maximum_fusion.own_ref), channel_id=1, replica_groups=mesh['xh'=2,'z'=8,'y'=8,'xl'=4,'core'=2] {'xl'}, dimensions={0}, use_global_device_ids=true | all-gather | bytes 819200 | tf_op jit(solution)/shard_map/all_gather | solution.py:204
  62.7 0.8 copy-done.4
  63.6 1.9 %collective-permute-start.3 = (bf16[256,1280]{1,0:T(8,128)(2,1)S(1)}, bf16[256,1280]{1,0:T(8,128)(2,1)}, u32[]{:S(2)}, u32[]{:S(2)}) collective-permute-start(bf16[256,1280]{1,0:T(8,128)(2,1)S(1)} %all_gather.3.a_ref), channel_id=1, source_target_pairs={{1,0},{0,1},{3,2},{2,3},{5,4},{4,5},{7,6},{6,7},{9,8},{8,9},{11,10... | collective-permute-start | bytes 1966088 | tf_op jit(solution)/shard_map/ppermute | solution.py:26
  65.5 2.2 %collective-permute-done.3.b_ref = bf16[256,1280]{1,0:T(8,128)(2,1)} collective-permute-done((bf16[256,1280]{1,0:T(8,128)(2,1)S(1)}, bf16[256,1280]{1,0:T(8,128)(2,1)}, u32[]{:S(2)}, u32[]{:S(2)}) %collective-permute-start.3) | collective-permute-done | bytes 655392 | tf_op jit(solution)/shard_map/ppermute | solution.py:26
  67.7 3.4 %image_side.1 = (bf16[128,1152]{1,0:T(8,128)(2,1)}, bf16[8,2,72,128]{3,2,1,0:T(8,128)(2,1)}) custom-call(bf16[256,1280]{1,0:T(8,128)(2,1)} %copy-done.4, bf16[256,1280]{1,0:T(8,128)(2,1)} %collective-permute-done.3.b_ref, bf16[128,1152]{1,0:T(8,128)(2,1)} %embed_ref.3, s32[1,128]{1,0:T(1,128)} %bitcast.9), custom_call_target="tpu_custom_call" | custom-call | tf_op jit(solution)/shard_map/image_side/pallas_call | solution.py:164
  71.1 0.0 all-to-all-done.feat_ref
  71.1 4.2 %all-to-all-start.1 = ((bf16[8,144,128]{2,1,0:T(8,128)(2,1)}), bf16[8,144,128]{2,1,0:T(8,128)(2,1)}, u32[]{:S(2)}, u32[]{:S(2)}) async-start(bf16[8,144,128]{2,1,0:T(8,128)(2,1)} %bitcast.7), calls=%async_computation.1 | async-start | bytes 589824 | tf_op jit(solution)/shard_map/all_to_all | solution.py:219
  75.3 2.1 %text_side.1 = (f32[16,1152]{1,0:T(8,128)}, bf16[16,1152]{1,0:T(8,128)(2,1)}, bf16[16,1152]{1,0:T(8,128)(2,1)}, bf16[16,1152]{1,0:T(8,128)(2,1)}) custom-call(bf16[64,1280]{1,0:T(8,128)(2,1)} %copy-done.5, bf16[128,1152]{1,0:T(8,128)(2,1)} %get-tuple-element.14.image_ref, s32[1,128]{1,0:T(1,128)} %bitcast.10), custom_call_target="tpu_custom_call" | custom-call | tf_op jit(solution)/shard_map/text_side/pallas_call | solution.py:164
  77.4 4.5 %collective-permute-start.4 = (bf16[16,1152]{1,0:T(8,128)(2,1)}, bf16[16,1152]{1,0:T(8,128)(2,1)S(1)}, u32[]{:S(2)}, u32[]{:S(2)}) collective-permute-start(bf16[16,1152]{1,0:T(8,128)(2,1)} %get-tuple-element.16), channel_id=1, source_target_pairs={{8,0},{16,8},{24,16},{32,24},{40,32},{48,40},{56,48},{64,56},{72,6... | collective-permute-start | bytes 110600 | tf_op jit(solution)/shard_map/ppermute | solution.py:26
  81.9 5.1 %collective-permute-start.5 = (bf16[16,1152]{1,0:T(8,128)(2,1)}, bf16[16,1152]{1,0:T(8,128)(2,1)S(1)}, u32[]{:S(2)}, u32[]{:S(2)}) collective-permute-start(bf16[16,1152]{1,0:T(8,128)(2,1)} %get-tuple-element.17), channel_id=1, source_target_pairs={{16,0},{24,8},{32,16},{40,24},{48,32},{56,40},{64,48},{72,56},{80,... | collective-permute-start | bytes 110600 | tf_op jit(solution)/shard_map/ppermute | solution.py:26
  87.0 4.0 %collective-permute-start.6 = (bf16[16,1152]{1,0:T(8,128)(2,1)}, bf16[16,1152]{1,0:T(8,128)(2,1)}, u32[]{:S(2)}, u32[]{:S(2)}) collective-permute-start(bf16[16,1152]{1,0:T(8,128)(2,1)} %get-tuple-element.18), channel_id=1, source_target_pairs={{24,0},{32,8},{40,16},{48,24},{56,32},{64,40},{72,48},{80,56},{88,... | collective-permute-start | bytes 110600 | tf_op jit(solution)/shard_map/ppermute | solution.py:26
  91.0 0.0 all-to-all-done.1.turned_ref
  91.0 1.7 %head_side.1 = bf16[16,54,128]{2,1,0:T(8,128)(2,1)S(1)} custom-call(bf16[8,144,128]{2,1,0:T(8,128)(2,1)} %all-to-all-done.1.turned_ref, bf16[8,128,768]{2,1,0:T(8,128)(2,1)S(1)} %all-to-all-done.feat_ref), custom_call_target="tpu_custom_call" | custom-call | tf_op jit(solution)/shard_map/head_side/pallas_call | solution.py:164
  92.7 0.7 copy-done.1
  93.4 8.3 %all-to-all-start.2 = ((bf16[16,54,128]{2,1,0:T(8,128)(2,1)}), bf16[16,54,128]{2,1,0:T(8,128)(2,1)S(1)}, u32[]{:S(2)}, u32[]{:S(2)}) async-start(bf16[16,54,128]{2,1,0:T(8,128)(2,1)} %copy-done.1), calls=%async_computation.2 | async-start | bytes 458752 | tf_op jit(solution)/shard_map/all_to_all | solution.py:227
  101.7 1.6 %text_back.1 = f32[16,1152]{1,0:T(8,128)} custom-call(f32[16,1152]{1,0:T(8,128)S(1)} %copy-done.3, bf16[16,1152]{1,0:T(8,128)(2,1)S(1)} %collective-permute-done.4.one_ref, bf16[16,1152]{1,0:T(8,128)(2,1)S(1)} %collective-permute-done.5.two_ref, bf16[16,1152]{1,0:T(8,128)(2,1)} %collective-permute-done.6.three_ref, bf16[16,1152]{1,0:T(8,128)(2,1)S(1)} %copy-done.2), custom_call_target="tpu_custom_call" | custom-call | flops 60000002048 | tf_op jit(solution)/shard_map/text_back/pallas_call | solution.py:164
  103.4 1.1 convolution_convert_fusion
  104.5 9.1 %all-to-all-done.2.parts_ref = bf16[16,54,128]{2,1,0:T(8,128)(2,1)S(1)} async-done(((bf16[16,54,128]{2,1,0:T(8,128)(2,1)}), bf16[16,54,128]{2,1,0:T(8,128)(2,1)S(1)}, u32[]{:S(2)}, u32[]{:S(2)}) %all-to-all-start.2) | async-done | bytes 221216 | tf_op jit(solution)/shard_map/all_to_all | solution.py:227
  113.6 0.7 head_sum.1
  (14 shorter events, 0.0 us)
Async XLA Ops:
  0.6 102.8 %copy-start = (bf16[1152,768]{1,0:T(8,128)(2,1)S(1)}, bf16[1152,768]{1,0:T(8,128)(2,1)}, u32[]{:S(2)}) copy-start(bf16[1152,768]{1,0:T(8,128)(2,1)} %param.10) | copy-start | bytes 5308420
  5.3 16.7 %copy-start.7 = (bf16[16,1280]{1,0:T(8,128)(2,1)S(1)}, bf16[16,1280]{1,0:T(8,128)(2,1)}, u32[]{:S(2)}) copy-start(bf16[16,1280]{1,0:T(8,128)(2,1)} %prepare.1._payload) | copy-start | bytes 122884
  5.3 65.8 %all-to-all-start = ((bf16[8,128,768]{2,1,0:T(8,128)(2,1)}), bf16[8,128,768]{2,1,0:T(8,128)(2,1)S(1)}, u32[]{:S(2)}, u32[]{:S(2)}) async-start(bf16[8,128,768]{2,1,0:T(8,128)(2,1)} %get-tuple-element.20), calls=%async_computation | async-start | bytes 3145728 | tf_op jit(solution)/shard_map/all_to_all | solution.py:200
  22.0 16.6 %collective-permute-start.2 = (bf16[16,1280]{1,0:T(8,128)(2,1)S(1)}, bf16[16,1280]{1,0:T(8,128)(2,1)S(1)}, u32[]{:S(2)}, u32[]{:S(2)}) collective-permute-start(bf16[16,1280]{1,0:T(8,128)(2,1)S(1)} %copy-done.7), channel_id=1, source_target_pairs={{1000,0},{1008,8},{1016,16},{0,24},{8,32},{16,40},{24,48},{32,56},... | collective-permute-start | bytes 122888 | tf_op jit(solution)/shard_map/ppermute | solution.py:26
  29.1 15.3 %collective-permute-start.1 = (bf16[16,1280]{1,0:T(8,128)(2,1)S(1)}, bf16[16,1280]{1,0:T(8,128)(2,1)S(1)}, u32[]{:S(2)}, u32[]{:S(2)}) collective-permute-start(bf16[16,1280]{1,0:T(8,128)(2,1)S(1)} %copy-done.7), channel_id=1, source_target_pairs={{1008,0},{1016,8},{0,16},{8,24},{16,32},{24,40},{32,48},{40,56},{4... | collective-permute-start | bytes 122888 | tf_op jit(solution)/shard_map/ppermute | solution.py:26
  32.0 12.4 %collective-permute-start = (bf16[16,1280]{1,0:T(8,128)(2,1)S(1)}, bf16[16,1280]{1,0:T(8,128)(2,1)S(1)}, u32[]{:S(2)}, u32[]{:S(2)}) collective-permute-start(bf16[16,1280]{1,0:T(8,128)(2,1)S(1)} %copy-done.7), channel_id=1, source_target_pairs={{1016,0},{0,8},{8,16},{16,24},{24,32},{32,40},{40,48},{48,56},{56,... | collective-permute-start | bytes 122888 | tf_op jit(solution)/shard_map/ppermute | solution.py:26
  45.2 30.1 %copy-start.5 = (bf16[64,1280]{1,0:T(8,128)(2,1)}, bf16[64,1280]{1,0:T(8,128)(2,1)S(1)}, u32[]{:S(2)}) copy-start(bf16[64,1280]{1,0:T(8,128)(2,1)S(1)} %pad_maximum_fusion.own_ref) | copy-start | bytes 491524
  62.7 0.8 copy-start.4
  63.6 4.1 %collective-permute-start.3 = (bf16[256,1280]{1,0:T(8,128)(2,1)S(1)}, bf16[256,1280]{1,0:T(8,128)(2,1)}, u32[]{:S(2)}, u32[]{:S(2)}) collective-permute-start(bf16[256,1280]{1,0:T(8,128)(2,1)S(1)} %all_gather.3.a_ref), channel_id=1, source_target_pairs={{1,0},{0,1},{3,2},{2,3},{5,4},{4,5},{7,6},{6,7},{9,8},{8,9},{11,10... | collective-permute-start | bytes 1966088 | tf_op jit(solution)/shard_map/ppermute | solution.py:26
  71.1 30.6 %copy-start.2 = (bf16[16,1152]{1,0:T(8,128)(2,1)S(1)}, bf16[16,1152]{1,0:T(8,128)(2,1)}, u32[]{:S(2)}) copy-start(bf16[16,1152]{1,0:T(8,128)(2,1)} %text_ref.1) | copy-start | bytes 110596
  71.1 19.9 %all-to-all-start.1 = ((bf16[8,144,128]{2,1,0:T(8,128)(2,1)}), bf16[8,144,128]{2,1,0:T(8,128)(2,1)}, u32[]{:S(2)}, u32[]{:S(2)}) async-start(bf16[8,144,128]{2,1,0:T(8,128)(2,1)} %bitcast.7), calls=%async_computation.1 | async-start | bytes 589824 | tf_op jit(solution)/shard_map/all_to_all | solution.py:219
  77.4 24.3 %copy-start.3 = (f32[16,1152]{1,0:T(8,128)S(1)}, f32[16,1152]{1,0:T(8,128)}, u32[]{:S(2)}) copy-start(f32[16,1152]{1,0:T(8,128)} %get-tuple-element.15.share_ref) | copy-start | bytes 221188
  77.4 24.3 %collective-permute-start.4 = (bf16[16,1152]{1,0:T(8,128)(2,1)}, bf16[16,1152]{1,0:T(8,128)(2,1)S(1)}, u32[]{:S(2)}, u32[]{:S(2)}) collective-permute-start(bf16[16,1152]{1,0:T(8,128)(2,1)} %get-tuple-element.16), channel_id=1, source_target_pairs={{8,0},{16,8},{24,16},{32,24},{40,32},{48,40},{56,48},{64,56},{72,6... | collective-permute-start | bytes 110600 | tf_op jit(solution)/shard_map/ppermute | solution.py:26
  81.9 19.8 %collective-permute-start.5 = (bf16[16,1152]{1,0:T(8,128)(2,1)}, bf16[16,1152]{1,0:T(8,128)(2,1)S(1)}, u32[]{:S(2)}, u32[]{:S(2)}) collective-permute-start(bf16[16,1152]{1,0:T(8,128)(2,1)} %get-tuple-element.17), channel_id=1, source_target_pairs={{16,0},{24,8},{32,16},{40,24},{48,32},{56,40},{64,48},{72,56},{80,... | collective-permute-start | bytes 110600 | tf_op jit(solution)/shard_map/ppermute | solution.py:26
  87.0 14.7 %collective-permute-start.6 = (bf16[16,1152]{1,0:T(8,128)(2,1)}, bf16[16,1152]{1,0:T(8,128)(2,1)}, u32[]{:S(2)}, u32[]{:S(2)}) collective-permute-start(bf16[16,1152]{1,0:T(8,128)(2,1)} %get-tuple-element.18), channel_id=1, source_target_pairs={{24,0},{32,8},{40,16},{48,24},{56,32},{64,40},{72,48},{80,56},{88,... | collective-permute-start | bytes 110600 | tf_op jit(solution)/shard_map/ppermute | solution.py:26
  92.7 0.7 copy-start.1
  93.4 20.3 %all-to-all-start.2 = ((bf16[16,54,128]{2,1,0:T(8,128)(2,1)}), bf16[16,54,128]{2,1,0:T(8,128)(2,1)S(1)}, u32[]{:S(2)}, u32[]{:S(2)}) async-start(bf16[16,54,128]{2,1,0:T(8,128)(2,1)} %copy-done.1), calls=%async_computation.2 | async-start | bytes 458752 | tf_op jit(solution)/shard_map/all_to_all | solution.py:227
  101.7 1.7 %copy-start.6 = (bf16[128,1152]{1,0:T(8,128)(2,1)S(1)}, bf16[128,1152]{1,0:T(8,128)(2,1)}, u32[]{:S(2)}) copy-start(bf16[128,1152]{1,0:T(8,128)(2,1)} %get-tuple-element.13) | copy-start | bytes 884740

commit v4 on v3

--- a/solution.py
+++ b/solution.py
@@ -68,14 +68,18 @@
     out_ref[:, width:] = tail.astype(bf16)
 
 
-def fan_out(embed_ref, feat_ref, _payload, round_ref, feats_hbm, sem):
-    copies = [pltpu.make_async_copy(feat_ref, feats_hbm.at[k], sem) for k in range(feats_hbm.shape[0])]
+def fan_out(feat_hbm, _payload, feats_hbm, sem):
+    copies = [pltpu.make_async_copy(feat_hbm, feats_hbm.at[k], sem) for k in range(feats_hbm.shape[0])]
     for copy in copies:
         copy.start()
-    floats = embed_ref[...].astype(f32)
-    round_ref[...] = (floats / norms_of(floats)).astype(bf16)
     for copy in copies:
         copy.wait()
+
+
+def assemble(*refs):
+    out_ref, count = refs[-1], refs[0].shape[0]
+    for k, ref in enumerate(refs[:-1]):
+        out_ref[k * count : (k + 1) * count] = ref[...]
 
 
 def slopes(rows, image_round, ids):
@@ -92,12 +96,23 @@
     return (-signs * jax.nn.sigmoid(-signs * logits)).astype(bf16)
 
 
-def text_side(own_ref, image_ref, ids_ref, kept_ref, one_ref, two_ref, three_ref):
-    slope = slopes(own_ref[...], image_ref[...], ids_ref[...])
-    share = SCALE * jnp.dot(slope, image_ref[...], preferred_element_type=f32)
-    count = kept_ref.shape[0]
-    for k, ref in enumerate((kept_ref, one_ref, two_ref, three_ref)):
+def text_shares(places, own_ref, embed_ref, ids_ref, refs):
+    count = refs[0].shape[0]
+    floats = embed_ref[...].astype(f32)
+    rounded = (floats / norms_of(floats)).astype(bf16)
+    rows = jnp.concatenate([own_ref[p * count : (p + 1) * count] for p in places], 0)
+    slope = slopes(rows, rounded, ids_ref[...])
+    share = SCALE * jnp.dot(slope, rounded, preferred_element_type=f32)
+    for k, ref in enumerate(refs):
         ref[...] = share[k * count : (k + 1) * count].astype(ref.dtype)
+
+
+def text_first(own_ref, embed_ref, ids_ref, _turned, one_ref, two_ref):
+    text_shares((1, 2), own_ref, embed_ref, ids_ref, (one_ref, two_ref))
+
+
+def text_second(own_ref, embed_ref, ids_ref, _parts, kept_ref, three_ref):
+    text_shares((0, 3), own_ref, embed_ref, ids_ref, (kept_ref, three_ref))
 
 
 def image_side(a_ref, b_ref, embed_ref, ids_ref, out_ref, turned_ref):
@@ -122,7 +137,7 @@
             turned_ref[z, p] = turned[start : start + run]
 
 
-def head_side(turned_ref, feat_ref, out_ref):
+def head_side(turned_ref, feat_ref, _one, _two, out_ref):
     blocks = turned_ref.shape[0]
     part = jnp.zeros((turned_ref.shape[1], feat_ref.shape[2]), f32)
     for k in range(blocks):
@@ -192,41 +207,48 @@
         prepare, [((texts, width + TAIL), bf16)], position, *inputs, smem=1, hbm=4,
         scratch=[pltpu.VMEM(v.shape, v.dtype) for v in inputs] + [pltpu.SemaphoreType.DMA((4,))],
     )
-    image_round, feats = call(
-        fan_out, [((images, width), bf16), ((planes, images, features), bf16)],
-        image_embed, image_feat, payload, after=1, out_hbm=1,
-        scratch=[pltpu.SemaphoreType.DMA], cost=lasting(20),
+    feats = call(
+        fan_out, [((planes, images, features), bf16)], image_feat, payload,
+        hbm=1, after=1, out_hbm=1, scratch=[pltpu.SemaphoreType.DMA], cost=lasting(20),
     )
     feats = lax.all_to_all(feats, "z", 0, 0, tiled=True)
 
-    own = jnp.concatenate([payload] + [shifted(payload, BLK, d) for d in (1, 2, 3)], 0)
+    window = [payload] + [shifted(payload, BLK, d) for d in (1, 2, 3)]
+    own = call(
+        assemble, [((len(window) * texts, width + TAIL), bf16)], *window,
+        cost=lasting(400), room=ROOM,
+    )
 
     here = lax.all_gather(own, "xl", axis=0, tiled=True)
     there = shifted(here, "core", 1)
-    kept, *aways = call(
-        text_side, [((texts, width), f32)] + [((texts, width), bf16)] * 3,
-        own, image_round, ids,
-    )
 
     pieces = lax.axis_size("xh")
     run = width // (planes * pieces)
     embed_grad, turned = call(
         image_side,
         [((images, width), bf16), ((planes, pieces, run, images), bf16)],
-        here, there, image_embed, ids,
-    )
+        here, there, image_embed, ids, room=ROOM,
+    )
+    shares = call(
+        text_first, [((texts, width), bf16)] * 2, own, image_embed, ids, turned, after=1,
+    )
+    backs = [shifted(away, BLK, -d) for d, away in zip((1, 2), shares)]
     turned, feats = lax.optimization_barrier((turned, feats))
     plane = lax.all_to_all(turned.reshape(planes, own_width, images), "z", 0, 0, tiled=True)
 
-    backs = [shifted(away, BLK, -d) for d, away in zip((1, 2, 3), aways)]
-
     rows = own_width // across
     parts = call(
-        head_side, [((across, rows * features // 128, 128), bf16)], plane, feats, room=ROOM
-    )
+        head_side, [((across, rows * features // 128, 128), bf16)], plane, feats, *backs,
+        after=2, room=ROOM,
+    )
+    kept, away = call(
+        text_second, [((texts, width), f32), ((texts, width), bf16)],
+        own, image_embed, ids, parts, after=1,
+    )
+    backs.append(shifted(away, BLK, -3))
     parts = lax.all_to_all(parts, ("xh", "y"), 0, 0, tiled=True)
     text_grad = call(
-        text_back, [((texts, width), f32)], kept, *backs, text_embed, cost=lasting(60), room=ROOM
+        text_back, [((texts, width), f32)], kept, *backs, text_embed, cost=lasting(1), room=ROOM
     )
     image_grad = jnp.dot(embed_grad, head, preferred_element_type=f32).astype(bf16)
     head_grad = call(head_sum, [((rows, features), f32)], parts, room=ROOM)

time: 115 us -> 178 us (1.55)
  the two profiles are of different devices: /device:TPU:16 before, /device:TPU:2 now
where the time goes in v4:
time: 178 us; the launch traced here: 177 us
  starting transfers between devices  73.1 us (41%)
  Pallas kernels  61.2 us (34%)
  waiting for transfers between devices  23.8 us (13%)
  blocking collectives  16.7 us (9%)
    pallas_call x9, Pallas kernels, call(): pl.pallas_call(kernel, out_shape=outs[0] if single else outs, in_specs=sp...  61.2 us
    ppermute x7, starting transfers between devices, shifted(): lax.ppermute(block, axis, [((i - distance) % size, i) for i in range(size)])  49.3 us
    all_to_all x1, starting transfers between devices, local(): feats = lax.all_to_all(feats, 'z', 0, 0, tiled=True)  16.7 us
    all_gather x1, blocking collectives, local(): here = lax.all_gather(own, 'xl', axis=0, tiled=True)  16.7 us
    all_to_all x1, waiting for transfers between devices, local(): feats = lax.all_to_all(feats, 'z', 0, 0, tiled=True)  16.5 us
    ppermute x7, waiting for transfers between devices, shifted(): lax.ppermute(block, axis, [((i - distance) % size, i) for i in range(size)])  7.25 us
    all_to_all x1, starting transfers between devices, local(): parts = lax.all_to_all(parts, ('xh', 'y'), 0, 0, tiled=True)  3.66 us
  transfers between devices with their start and end apart: 10, of which 4 were waited for; matrix products, arithmetic and copies ran while one was open for 1% of the time, Pallas kernels for 32%

profile of v4, /device:TPU:2, one launch (start us, length us, event | category | flops | bytes accessed | tf_op | source)
XLA Modules:
  0.0 176.8 jit_solution(15971049930368178419)
XLA Ops:
  0.6 0.0 copy-start
  0.7 1.7 prepare.1.refs_0_._payload
  2.4 3.6 %collective-permute-start = (bf16[16,1280]{1,0:T(8,128)(2,1)}, bf16[16,1280]{1,0:T(8,128)(2,1)S(1)}, u32[]{:S(2)}, u32[]{:S(2)}) collective-permute-start(bf16[16,1280]{1,0:T(8,128)(2,1)} %prepare.1.refs_0_._payload), channel_id=1, source_target_pairs={{1016,0},{0,8},{8,16},{16,24},{24,32},{32,40},{40,48},{48,56},{56,... | collective-permute-start | bytes 122888 | tf_op jit(solution)/shard_map/ppermute | solution.py:26
  6.0 4.7 %collective-permute-start.1 = (bf16[16,1280]{1,0:T(8,128)(2,1)}, bf16[16,1280]{1,0:T(8,128)(2,1)S(1)}, u32[]{:S(2)}, u32[]{:S(2)}) collective-permute-start(bf16[16,1280]{1,0:T(8,128)(2,1)} %prepare.1.refs_0_._payload), channel_id=1, source_target_pairs={{1008,0},{1016,8},{0,16},{8,24},{16,32},{24,40},{32,48},{40,56},{4... | collective-permute-start | bytes 122888 | tf_op jit(solution)/shard_map/ppermute | solution.py:26
  10.7 5.3 %collective-permute-start.2 = (bf16[16,1280]{1,0:T(8,128)(2,1)}, bf16[16,1280]{1,0:T(8,128)(2,1)S(1)}, u32[]{:S(2)}, u32[]{:S(2)}) collective-permute-start(bf16[16,1280]{1,0:T(8,128)(2,1)} %prepare.1.refs_0_._payload), channel_id=1, source_target_pairs={{1000,0},{1008,8},{1016,16},{0,24},{8,32},{16,40},{24,48},{32,56},... | collective-permute-start | bytes 122888 | tf_op jit(solution)/shard_map/ppermute | solution.py:26
  16.0 48.8 %fan_out.1 = bf16[8,128,768]{2,1,0:T(8,128)(2,1)} custom-call(bf16[128,768]{1,0:T(8,128)(2,1)} %feat_hbm.1, bf16[16,1280]{1,0:T(8,128)(2,1)} %prepare.1.refs_0_._payload), custom_call_target="tpu_custom_call" | custom-call | flops 20000000000 | tf_op jit(solution)/shard_map/fan_out/pallas_call | solution.py:179
  64.8 0.0 copy-start.3
  64.8 16.7 %all-to-all-start = ((bf16[8,128,768]{2,1,0:T(8,128)(2,1)}), bf16[8,128,768]{2,1,0:T(8,128)(2,1)}, u32[]{:S(2)}, u32[]{:S(2)}) async-start(bf16[8,128,768]{2,1,0:T(8,128)(2,1)} %fan_out.1), calls=%async_computation | async-start | bytes 3145728 | tf_op jit(solution)/shard_map/all_to_all | solution.py:214
  81.5 0.0 collective-permute-done.1.refs_2_
  81.5 0.0 collective-permute-done.2.refs_3_
  81.5 0.0 copy-start.1
  81.5 0.0 copy-start.5
  81.5 0.0 copy-start.2
  81.6 16.7 %all_gather.3.a_ref = bf16[256,1280]{1,0:T(8,128)(2,1)S(1)} all-gather(bf16[64,1280]{1,0:T(8,128)(2,1)S(1)} %assemble.1.own_ref), channel_id=1, replica_groups=mesh['xh'=2,'z'=8,'y'=8,'xl'=4,'core'=2] {'xl'}, dimensions={0}, use_global_device_ids=true | all-gather | bytes 819200 | tf_op jit(solution)/shard_map/all_gather | solution.py:222
  98.2 1.9 %collective-permute-start.3 = (bf16[256,1280]{1,0:T(8,128)(2,1)S(1)}, bf16[256,1280]{1,0:T(8,128)(2,1)S(1)}, u32[]{:S(2)}, u32[]{:S(2)}) collective-permute-start(bf16[256,1280]{1,0:T(8,128)(2,1)S(1)} %all_gather.3.a_ref), channel_id=1, source_target_pairs={{1,0},{0,1},{3,2},{2,3},{5,4},{4,5},{7,6},{6,7},{9,8},{8,9},{11,10... | collective-permute-start | bytes 1966088 | tf_op jit(solution)/shard_map/ppermute | solution.py:26
  100.2 2.1 %collective-permute-done.3.b_ref = bf16[256,1280]{1,0:T(8,128)(2,1)S(1)} collective-permute-done((bf16[256,1280]{1,0:T(8,128)(2,1)S(1)}, bf16[256,1280]{1,0:T(8,128)(2,1)S(1)}, u32[]{:S(2)}, u32[]{:S(2)}) %collective-permute-start.3) | collective-permute-done | bytes 655392 | tf_op jit(solution)/shard_map/ppermute | solution.py:26
  102.2 2.0 %image_side.1 = (bf16[128,1152]{1,0:T(8,128)(2,1)S(1)}, bf16[8,2,72,128]{3,2,1,0:T(8,128)(2,1)}) custom-call(bf16[256,1280]{1,0:T(8,128)(2,1)S(1)} %all_gather.3.a_ref, bf16[256,1280]{1,0:T(8,128)(2,1)S(1)} %collective-permute-done.3.b_ref, bf16[128,1152]{1,0:T(8,128)(2,1)S(1)} %copy-done.1, s32[1,128]{1,0:T(1,128)S(1)} %bitcast.10), custom_call_target="tpu_custom_call" | custom-call | tf_op jit(solution)/shard_map/image_side/pallas_call | solution.py:179
  104.2 16.5 %all-to-all-done.feat_ref = bf16[8,128,768]{2,1,0:T(8,128)(2,1)} async-done(((bf16[8,128,768]{2,1,0:T(8,128)(2,1)}), bf16[8,128,768]{2,1,0:T(8,128)(2,1)}, u32[]{:S(2)}, u32[]{:S(2)}) %all-to-all-start) | async-done | bytes 1572896 | tf_op jit(solution)/shard_map/all_to_all | solution.py:214
  120.7 3.4 %all-to-all-start.1 = ((bf16[8,144,128]{2,1,0:T(8,128)(2,1)}), bf16[8,144,128]{2,1,0:T(8,128)(2,1)S(1)}, u32[]{:S(2)}, u32[]{:S(2)}) async-start(bf16[8,144,128]{2,1,0:T(8,128)(2,1)} %bitcast.4), calls=%async_computation.1 | async-start | bytes 589824 | tf_op jit(solution)/shard_map/all_to_all | solution.py:237
  124.2 2.2 %text_first.1 = (bf16[16,1152]{1,0:T(8,128)(2,1)}, bf16[16,1152]{1,0:T(8,128)(2,1)}) custom-call(bf16[64,1280]{1,0:T(8,128)(2,1)} %copy-done.2, bf16[128,1152]{1,0:T(8,128)(2,1)} %embed_ref.5, s32[1,128]{1,0:T(1,128)} %bitcast.8, bf16[8,2,72,128]{3,2,1,0:T(8,128)(2,1)} %get-tuple-element.13._turned), custom_call_target="tpu_custom_call" | custom-call | tf_op jit(solution)/shard_map/text_first/pallas_call | solution.py:179
  126.4 11.9 %collective-permute-start.4 = (bf16[16,1152]{1,0:T(8,128)(2,1)}, bf16[16,1152]{1,0:T(8,128)(2,1)S(1)}, u32[]{:S(2)}, u32[]{:S(2)}) collective-permute-start(bf16[16,1152]{1,0:T(8,128)(2,1)} %get-tuple-element.15), channel_id=1, source_target_pairs={{8,0},{16,8},{24,16},{32,24},{40,32},{48,40},{56,48},{64,56},{72,6... | collective-permute-start | bytes 110600 | tf_op jit(solution)/shard_map/ppermute | solution.py:26
  138.3 2.6 %collective-permute-start.5 = (bf16[16,1152]{1,0:T(8,128)(2,1)}, bf16[16,1152]{1,0:T(8,128)(2,1)S(1)}, u32[]{:S(2)}, u32[]{:S(2)}) collective-permute-start(bf16[16,1152]{1,0:T(8,128)(2,1)} %get-tuple-element.16), channel_id=1, source_target_pairs={{16,0},{24,8},{32,16},{40,24},{48,32},{56,40},{64,48},{72,56},{80,... | collective-permute-start | bytes 110600 | tf_op jit(solution)/shard_map/ppermute | solution.py:26
  140.9 0.0 collective-permute-done.4._one.one_ref
  140.9 4.3 %collective-permute-done.5._two.two_ref = bf16[16,1152]{1,0:T(8,128)(2,1)S(1)} collective-permute-done((bf16[16,1152]{1,0:T(8,128)(2,1)}, bf16[16,1152]{1,0:T(8,128)(2,1)S(1)}, u32[]{:S(2)}, u32[]{:S(2)}) %collective-permute-start.5) | collective-permute-done | bytes 36896 | tf_op jit(solution)/shard_map/ppermute | solution.py:26
  145.2 2.8 %head_side.1._parts = bf16[16,54,128]{2,1,0:T(8,128)(2,1)} custom-call(bf16[8,144,128]{2,1,0:T(8,128)(2,1)S(1)} %all-to-all-done.1.turned_ref, bf16[8,128,768]{2,1,0:T(8,128)(2,1)} %all-to-all-done.feat_ref, bf16[16,1152]{1,0:T(8,128)(2,1)S(1)} %collective-permute-done.4._one.one_ref, bf16[16,1152]{1,0:T(8,128)(2,1)S(1)} %collective-permute-done.5._two.two_ref), custom_call_target="tpu_custom_call" | custom-call | tf_op jit(solution)/shard_map/head_side/pallas_call | solution.py:179
  148.1 3.7 %all-to-all-start.2 = ((bf16[16,54,128]{2,1,0:T(8,128)(2,1)}), bf16[16,54,128]{2,1,0:T(8,128)(2,1)S(1)}, u32[]{:S(2)}, u32[]{:S(2)}) async-start(bf16[16,54,128]{2,1,0:T(8,128)(2,1)} %head_side.1._parts), calls=%async_computation.2 | async-start | bytes 458752 | tf_op jit(solution)/shard_map/all_to_all | solution.py:249
  151.7 2.2 %text_second.1 = (f32[16,1152]{1,0:T(8,128)}, bf16[16,1152]{1,0:T(8,128)(2,1)}) custom-call(bf16[64,1280]{1,0:T(8,128)(2,1)} %copy-done.2, bf16[128,1152]{1,0:T(8,128)(2,1)} %embed_ref.5, s32[1,128]{1,0:T(1,128)} %bitcast.9, bf16[16,54,128]{2,1,0:T(8,128)(2,1)} %head_side.1._parts), custom_call_target="tpu_custom_call" | custom-call | tf_op jit(solution)/shard_map/text_second/pallas_call | solution.py:179
  153.9 19.4 %collective-permute-start.6 = (bf16[16,1152]{1,0:T(8,128)(2,1)}, bf16[16,1152]{1,0:T(8,128)(2,1)S(1)}, u32[]{:S(2)}, u32[]{:S(2)}) collective-permute-start(bf16[16,1152]{1,0:T(8,128)(2,1)} %get-tuple-element.18), channel_id=1, source_target_pairs={{24,0},{32,8},{40,16},{48,24},{56,32},{64,40},{72,48},{80,56},{88,... | collective-permute-start | bytes 110600 | tf_op jit(solution)/shard_map/ppermute | solution.py:26
  173.4 1.1 convolution_convert_fusion
  174.5 0.8 collective-permute-done.6.three_ref
  175.3 0.8 text_back.1
  176.1 0.7 head_sum.1
  (13 shorter events, 0.0 us)
Async XLA Ops:
  0.6 172.7 %copy-start = (bf16[1152,768]{1,0:T(8,128)(2,1)S(1)}, bf16[1152,768]{1,0:T(8,128)(2,1)}, u32[]{:S(2)}) copy-start(bf16[1152,768]{1,0:T(8,128)(2,1)} %param.10) | copy-start | bytes 5308420
  2.4 79.1 %collective-permute-start = (bf16[16,1280]{1,0:T(8,128)(2,1)}, bf16[16,1280]{1,0:T(8,128)(2,1)S(1)}, u32[]{:S(2)}, u32[]{:S(2)}) collective-permute-start(bf16[16,1280]{1,0:T(8,128)(2,1)} %prepare.1.refs_0_._payload), channel_id=1, source_target_pairs={{1016,0},{0,8},{8,16},{16,24},{24,32},{32,40},{40,48},{48,56},{56,... | collective-permute-start | bytes 122888 | tf_op jit(solution)/shard_map/ppermute | solution.py:26
  6.0 75.5 %collective-permute-start.1 = (bf16[16,1280]{1,0:T(8,128)(2,1)}, bf16[16,1280]{1,0:T(8,128)(2,1)S(1)}, u32[]{:S(2)}, u32[]{:S(2)}) collective-permute-start(bf16[16,1280]{1,0:T(8,128)(2,1)} %prepare.1.refs_0_._payload), channel_id=1, source_target_pairs={{1008,0},{1016,8},{0,16},{8,24},{16,32},{24,40},{32,48},{40,56},{4... | collective-permute-start | bytes 122888 | tf_op jit(solution)/shard_map/ppermute | solution.py:26
  10.7 70.8 %collective-permute-start.2 = (bf16[16,1280]{1,0:T(8,128)(2,1)}, bf16[16,1280]{1,0:T(8,128)(2,1)S(1)}, u32[]{:S(2)}, u32[]{:S(2)}) collective-permute-start(bf16[16,1280]{1,0:T(8,128)(2,1)} %prepare.1.refs_0_._payload), channel_id=1, source_target_pairs={{1000,0},{1008,8},{1016,16},{0,24},{8,32},{16,40},{24,48},{32,56},... | collective-permute-start | bytes 122888 | tf_op jit(solution)/shard_map/ppermute | solution.py:26
  64.8 16.7 %copy-start.3 = (bf16[16,1280]{1,0:T(8,128)(2,1)S(1)}, bf16[16,1280]{1,0:T(8,128)(2,1)}, u32[]{:S(2)}) copy-start(bf16[16,1280]{1,0:T(8,128)(2,1)} %prepare.1.refs_0_._payload) | copy-start | bytes 122884
  64.8 56.0 %all-to-all-start = ((bf16[8,128,768]{2,1,0:T(8,128)(2,1)}), bf16[8,128,768]{2,1,0:T(8,128)(2,1)}, u32[]{:S(2)}, u32[]{:S(2)}) async-start(bf16[8,128,768]{2,1,0:T(8,128)(2,1)} %fan_out.1), calls=%async_computation | async-start | bytes 3145728 | tf_op jit(solution)/shard_map/all_to_all | solution.py:214
  81.5 20.7 %copy-start.1 = (bf16[128,1152]{1,0:T(8,128)(2,1)S(1)}, bf16[128,1152]{1,0:T(8,128)(2,1)}, u32[]{:S(2)}) copy-start(bf16[128,1152]{1,0:T(8,128)(2,1)} %embed_ref.5) | copy-start | bytes 884740
  81.5 20.7 %copy-start.5 = (s32[128]{0:T(128)S(1)}, s32[128]{0:T(128)}, u32[]{:S(2)}) copy-start(s32[128]{0:T(128)} %param.11) | copy-start | bytes 1540
  81.5 42.6 %copy-start.2 = (bf16[64,1280]{1,0:T(8,128)(2,1)}, bf16[64,1280]{1,0:T(8,128)(2,1)S(1)}, u32[]{:S(2)}) copy-start(bf16[64,1280]{1,0:T(8,128)(2,1)S(1)} %assemble.1.own_ref) | copy-start | bytes 491524
  98.2 4.0 %collective-permute-start.3 = (bf16[256,1280]{1,0:T(8,128)(2,1)S(1)}, bf16[256,1280]{1,0:T(8,128)(2,1)S(1)}, u32[]{:S(2)}, u32[]{:S(2)}) collective-permute-start(bf16[256,1280]{1,0:T(8,128)(2,1)S(1)} %all_gather.3.a_ref), channel_id=1, source_target_pairs={{1,0},{0,1},{3,2},{2,3},{5,4},{4,5},{7,6},{6,7},{9,8},{8,9},{11,10... | collective-permute-start | bytes 1966088 | tf_op jit(solution)/shard_map/ppermute | solution.py:26
  120.7 24.5 %all-to-all-start.1 = ((bf16[8,144,128]{2,1,0:T(8,128)(2,1)}), bf16[8,144,128]{2,1,0:T(8,128)(2,1)S(1)}, u32[]{:S(2)}, u32[]{:S(2)}) async-start(bf16[8,144,128]{2,1,0:T(8,128)(2,1)} %bitcast.4), calls=%async_computation.1 | async-start | bytes 589824 | tf_op jit(solution)/shard_map/all_to_all | solution.py:237
  126.4 14.5 %collective-permute-start.4 = (bf16[16,1152]{1,0:T(8,128)(2,1)}, bf16[16,1152]{1,0:T(8,128)(2,1)S(1)}, u32[]{:S(2)}, u32[]{:S(2)}) collective-permute-start(bf16[16,1152]{1,0:T(8,128)(2,1)} %get-tuple-element.15), channel_id=1, source_target_pairs={{8,0},{16,8},{24,16},{32,24},{40,32},{48,40},{56,48},{64,56},{72,6... | collective-permute-start | bytes 110600 | tf_op jit(solution)/shard_map/ppermute | solution.py:26
  138.3 7.0 %collective-permute-start.5 = (bf16[16,1152]{1,0:T(8,128)(2,1)}, bf16[16,1152]{1,0:T(8,128)(2,1)S(1)}, u32[]{:S(2)}, u32[]{:S(2)}) collective-permute-start(bf16[16,1152]{1,0:T(8,128)(2,1)} %get-tuple-element.16), channel_id=1, source_target_pairs={{16,0},{24,8},{32,16},{40,24},{48,32},{56,40},{64,48},{72,56},{80,... | collective-permute-start | bytes 110600 | tf_op jit(solution)/shard_map/ppermute | solution.py:26
  148.0 27.3 %copy-start.4 = (bf16[16,1152]{1,0:T(8,128)(2,1)S(1)}, bf16[16,1152]{1,0:T(8,128)(2,1)}, u32[]{:S(2)}) copy-start(bf16[16,1152]{1,0:T(8,128)(2,1)} %text_ref.1) | copy-start | bytes 110596
  148.1 28.1 %all-to-all-start.2 = ((bf16[16,54,128]{2,1,0:T(8,128)(2,1)}), bf16[16,54,128]{2,1,0:T(8,128)(2,1)S(1)}, u32[]{:S(2)}, u32[]{:S(2)}) async-start(bf16[16,54,128]{2,1,0:T(8,128)(2,1)} %head_side.1._parts), calls=%async_computation.2 | async-start | bytes 458752 | tf_op jit(solution)/shard_map/all_to_all | solution.py:249
  153.9 21.4 %copy-start.6 = (f32[16,1152]{1,0:T(8,128)S(1)}, f32[16,1152]{1,0:T(8,128)}, u32[]{:S(2)}) copy-start(f32[16,1152]{1,0:T(8,128)} %get-tuple-element.17.share_ref) | copy-start | bytes 221188
  153.9 21.4 %collective-permute-start.6 = (bf16[16,1152]{1,0:T(8,128)(2,1)}, bf16[16,1152]{1,0:T(8,128)(2,1)S(1)}, u32[]{:S(2)}, u32[]{:S(2)}) collective-permute-start(bf16[16,1152]{1,0:T(8,128)(2,1)} %get-tuple-element.18), channel_id=1, source_target_pairs={{24,0},{32,8},{40,16},{48,24},{56,32},{64,40},{72,48},{80,56},{88,... | collective-permute-start | bytes 110600 | tf_op jit(solution)/shard_map/ppermute | solution.py:26

commit v5 on v4

--- a/solution.py
+++ b/solution.py
@@ -68,8 +68,8 @@
     out_ref[:, width:] = tail.astype(bf16)
 
 
-def fan_out(feat_hbm, _payload, feats_hbm, sem):
-    copies = [pltpu.make_async_copy(feat_hbm, feats_hbm.at[k], sem) for k in range(feats_hbm.shape[0])]
+def fan_out(feat_ref, _payload, feats_hbm, sem):
+    copies = [pltpu.make_async_copy(feat_ref, feats_hbm.at[k], sem) for k in range(feats_hbm.shape[0])]
     for copy in copies:
         copy.start()
     for copy in copies:
@@ -96,23 +96,14 @@
     return (-signs * jax.nn.sigmoid(-signs * logits)).astype(bf16)
 
 
-def text_shares(places, own_ref, embed_ref, ids_ref, refs):
-    count = refs[0].shape[0]
+def text_side(own_ref, embed_ref, ids_ref, _turned, *refs):
     floats = embed_ref[...].astype(f32)
     rounded = (floats / norms_of(floats)).astype(bf16)
-    rows = jnp.concatenate([own_ref[p * count : (p + 1) * count] for p in places], 0)
-    slope = slopes(rows, rounded, ids_ref[...])
+    slope = slopes(own_ref[...], rounded, ids_ref[...])
     share = SCALE * jnp.dot(slope, rounded, preferred_element_type=f32)
+    count = refs[0].shape[0]
     for k, ref in enumerate(refs):
         ref[...] = share[k * count : (k + 1) * count].astype(ref.dtype)
-
-
-def text_first(own_ref, embed_ref, ids_ref, _turned, one_ref, two_ref):
-    text_shares((1, 2), own_ref, embed_ref, ids_ref, (one_ref, two_ref))
-
-
-def text_second(own_ref, embed_ref, ids_ref, _parts, kept_ref, three_ref):
-    text_shares((0, 3), own_ref, embed_ref, ids_ref, (kept_ref, three_ref))
 
 
 def image_side(a_ref, b_ref, embed_ref, ids_ref, out_ref, turned_ref):
@@ -137,7 +128,7 @@
             turned_ref[z, p] = turned[start : start + run]
 
 
-def head_side(turned_ref, feat_ref, _one, _two, out_ref):
+def head_side(turned_ref, feat_ref, out_ref):
     blocks = turned_ref.shape[0]
     part = jnp.zeros((turned_ref.shape[1], feat_ref.shape[2]), f32)
     for k in range(blocks):
@@ -158,7 +149,8 @@
         out_ref[:, g * 128 : (g + 1) * 128] = total[g * run : (g + 1) * run]
 
 
-def text_back(share_ref, one_ref, two_ref, three_ref, text_ref, out_ref):
+def finish(grad_ref, head_ref, share_ref, one_ref, two_ref, three_ref, text_ref, image_ref, out_ref):
+    image_ref[...] = jnp.dot(grad_ref[...], head_ref[...], preferred_element_type=f32).astype(bf16)
     floats = text_ref[...].astype(f32)
     norms = norms_of(floats)
     units = floats / norms
@@ -209,7 +201,7 @@
     )
     feats = call(
         fan_out, [((planes, images, features), bf16)], image_feat, payload,
-        hbm=1, after=1, out_hbm=1, scratch=[pltpu.SemaphoreType.DMA], cost=lasting(20),
+        after=1, out_hbm=1, scratch=[pltpu.SemaphoreType.DMA], cost=lasting(20),
     )
     feats = lax.all_to_all(feats, "z", 0, 0, tiled=True)
 
@@ -229,28 +221,24 @@
         [((images, width), bf16), ((planes, pieces, run, images), bf16)],
         here, there, image_embed, ids, room=ROOM,
     )
-    shares = call(
-        text_first, [((texts, width), bf16)] * 2, own, image_embed, ids, turned, after=1,
-    )
-    backs = [shifted(away, BLK, -d) for d, away in zip((1, 2), shares)]
     turned, feats = lax.optimization_barrier((turned, feats))
     plane = lax.all_to_all(turned.reshape(planes, own_width, images), "z", 0, 0, tiled=True)
 
+    kept, *aways = call(
+        text_side, [((texts, width), f32)] + [((texts, width), bf16)] * 3,
+        own, image_embed, ids, turned, after=1,
+    )
+    backs = [shifted(away, BLK, -d) for d, away in zip((1, 2, 3), aways)]
+
     rows = own_width // across
     parts = call(
-        head_side, [((across, rows * features // 128, 128), bf16)], plane, feats, *backs,
-        after=2, room=ROOM,
-    )
-    kept, away = call(
-        text_second, [((texts, width), f32), ((texts, width), bf16)],
-        own, image_embed, ids, parts, after=1,
-    )
-    backs.append(shifted(away, BLK, -3))
+        head_side, [((across, rows * features // 128, 128), bf16)], plane, feats, room=ROOM
+    )
     parts = lax.all_to_all(parts, ("xh", "y"), 0, 0, tiled=True)
-    text_grad = call(
-        text_back, [((texts, width), f32)], kept, *backs, text_embed, cost=lasting(1), room=ROOM
-    )
-    image_grad = jnp.dot(embed_grad, head, preferred_element_type=f32).astype(bf16)
+    image_grad, text_grad = call(
+        finish, [((images, features), bf16), ((texts, width), f32)],
+        embed_grad, head, kept, *backs, text_embed, cost=lasting(60), room=ROOM,
+    )
     head_grad = call(head_sum, [((rows, features), f32)], parts, room=ROOM)
     return (image_grad, text_grad, head_grad)
 

time: 178 us -> 123 us (0.69)
  the two profiles are of different devices: /device:TPU:2 before, /device:TPU:4 now
where the time goes in v5:
time: 123 us; the launch traced here: 122 us
  starting transfers between devices  60.7 us (49%)
  waiting for transfers between devices  32 us (26%)
  blocking collectives  15.9 us (13%)
  Pallas kernels  12.7 us (10%)
    ppermute x7, starting transfers between devices, shifted(): lax.ppermute(block, axis, [((i - distance) % size, i) for i in range(size)])  31.7 us
    all_to_all x1, waiting for transfers between devices, local(): feats = lax.all_to_all(feats, 'z', 0, 0, tiled=True)  17.3 us
    all_to_all x1, starting transfers between devices, local(): feats = lax.all_to_all(feats, 'z', 0, 0, tiled=True)  16.7 us
    all_gather x1, blocking collectives, local(): here = lax.all_gather(own, 'xl', axis=0, tiled=True)  15.9 us
    pallas_call x8, Pallas kernels, call(): pl.pallas_call(kernel, out_shape=outs[0] if single else outs, in_specs=sp...  12.7 us
    all_to_all x1, waiting for transfers between devices, local(): parts = lax.all_to_all(parts, ('xh', 'y'), 0, 0, tiled=True)  12.6 us
    all_to_all x1, starting transfers between devices, local(): parts = lax.all_to_all(parts, ('xh', 'y'), 0, 0, tiled=True)  8.92 us
    all_to_all x1, starting transfers between devices, local(): lax.all_to_all(turned.reshape(planes, own_width, images), 'z', 0, 0, tile...  3.42 us
  transfers between devices with their start and end apart: 10, of which 3 were waited for; matrix products, arithmetic and copies ran while one was open for 0% of the time, Pallas kernels for 9%

profile of v5, /device:TPU:4, one launch (start us, length us, event | category | flops | bytes accessed | tf_op | source)
XLA Modules:
  0.0 122.3 jit_solution(6581391728859206270)
XLA Ops:
  0.6 1.6 %prepare.1.refs_0_._payload = bf16[16,1280]{1,0:T(8,128)(2,1)} custom-call(s32[1]{0:T(128)} %bitcast.pos_ref, bf16[16,1152]{1,0:T(8,128)(2,1)} %text_ref.1, s32[1,128]{1,0:T(1,128)} %bitcast.5, s32[1,128]{1,0:T(1,128)} %bitcast.8, f32[1,8]{1,0:T(1,128)} %bitcast.9), custom_call_target="tpu_custom_call" | custom-call | tf_op jit(solution)/shard_map/prepare/pallas_call | solution.py:171
  2.2 5.9 %collective-permute-start.2 = (bf16[16,1280]{1,0:T(8,128)(2,1)}, bf16[16,1280]{1,0:T(8,128)(2,1)S(1)}, u32[]{:S(2)}, u32[]{:S(2)}) collective-permute-start(bf16[16,1280]{1,0:T(8,128)(2,1)} %prepare.1.refs_0_._payload), channel_id=1, source_target_pairs={{1000,0},{1008,8},{1016,16},{0,24},{8,32},{16,40},{24,48},{32,56},... | collective-permute-start | bytes 122888 | tf_op jit(solution)/shard_map/ppermute | solution.py:26
  8.1 5.0 %collective-permute-start.1 = (bf16[16,1280]{1,0:T(8,128)(2,1)}, bf16[16,1280]{1,0:T(8,128)(2,1)S(1)}, u32[]{:S(2)}, u32[]{:S(2)}) collective-permute-start(bf16[16,1280]{1,0:T(8,128)(2,1)} %prepare.1.refs_0_._payload), channel_id=1, source_target_pairs={{1008,0},{1016,8},{0,16},{8,24},{16,32},{24,40},{32,48},{40,56},{4... | collective-permute-start | bytes 122888 | tf_op jit(solution)/shard_map/ppermute | solution.py:26
  13.1 2.7 %collective-permute-start = (bf16[16,1280]{1,0:T(8,128)(2,1)}, bf16[16,1280]{1,0:T(8,128)(2,1)S(1)}, u32[]{:S(2)}, u32[]{:S(2)}) collective-permute-start(bf16[16,1280]{1,0:T(8,128)(2,1)} %prepare.1.refs_0_._payload), channel_id=1, source_target_pairs={{1016,0},{0,8},{8,16},{16,24},{24,32},{32,40},{40,48},{48,56},{56,... | collective-permute-start | bytes 122888 | tf_op jit(solution)/shard_map/ppermute | solution.py:26
  15.8 2.1 %fan_out.1 = bf16[8,128,768]{2,1,0:T(8,128)(2,1)} custom-call(bf16[128,768]{1,0:T(8,128)(2,1)} %feat_ref.1, bf16[16,1280]{1,0:T(8,128)(2,1)} %prepare.1.refs_0_._payload), custom_call_target="tpu_custom_call" | custom-call | flops 20000000000 | tf_op jit(solution)/shard_map/fan_out/pallas_call | solution.py:171
  17.9 0.0 copy-start.2
  17.9 16.7 %all-to-all-start = ((bf16[8,128,768]{2,1,0:T(8,128)(2,1)}), bf16[8,128,768]{2,1,0:T(8,128)(2,1)}, u32[]{:S(2)}, u32[]{:S(2)}) async-start(bf16[8,128,768]{2,1,0:T(8,128)(2,1)} %fan_out.1), calls=%async_computation | async-start | bytes 3145728 | tf_op jit(solution)/shard_map/all_to_all | solution.py:206
  34.6 0.0 collective-permute-done.2.refs_3_
  34.6 0.0 collective-permute-done.1.refs_2_
  34.7 0.0 copy-start
  34.7 0.0 copy-start.4
  34.7 0.0 copy-start.1
  34.7 15.9 %all_gather.3.a_ref = bf16[256,1280]{1,0:T(8,128)(2,1)S(1)} all-gather(bf16[64,1280]{1,0:T(8,128)(2,1)S(1)} %assemble.1.own_ref), channel_id=1, replica_groups=mesh['xh'=2,'z'=8,'y'=8,'xl'=4,'core'=2] {'xl'}, dimensions={0}, use_global_device_ids=true | all-gather | bytes 819200 | tf_op jit(solution)/shard_map/all_gather | solution.py:214
  50.6 1.9 %collective-permute-start.3 = (bf16[256,1280]{1,0:T(8,128)(2,1)S(1)}, bf16[256,1280]{1,0:T(8,128)(2,1)S(1)}, u32[]{:S(2)}, u32[]{:S(2)}) collective-permute-start(bf16[256,1280]{1,0:T(8,128)(2,1)S(1)} %all_gather.3.a_ref), channel_id=1, source_target_pairs={{1,0},{0,1},{3,2},{2,3},{5,4},{4,5},{7,6},{6,7},{9,8},{8,9},{11,10... | collective-permute-start | bytes 1966088 | tf_op jit(solution)/shard_map/ppermute | solution.py:26
  52.6 2.1 %collective-permute-done.3.b_ref = bf16[256,1280]{1,0:T(8,128)(2,1)S(1)} collective-permute-done((bf16[256,1280]{1,0:T(8,128)(2,1)S(1)}, bf16[256,1280]{1,0:T(8,128)(2,1)S(1)}, u32[]{:S(2)}, u32[]{:S(2)}) %collective-permute-start.3) | collective-permute-done | bytes 655392 | tf_op jit(solution)/shard_map/ppermute | solution.py:26
  54.6 2.0 %image_side.1 = (bf16[128,1152]{1,0:T(8,128)(2,1)S(1)}, bf16[8,2,72,128]{3,2,1,0:T(8,128)(2,1)}) custom-call(bf16[256,1280]{1,0:T(8,128)(2,1)S(1)} %all_gather.3.a_ref, bf16[256,1280]{1,0:T(8,128)(2,1)S(1)} %collective-permute-done.3.b_ref, bf16[128,1152]{1,0:T(8,128)(2,1)S(1)} %copy-done, s32[1,128]{1,0:T(1,128)S(1)} %bitcast.7), custom_call_target="tpu_custom_call" | custom-call | tf_op jit(solution)/shard_map/image_side/pallas_call | solution.py:171
  56.6 17.3 %all-to-all-done.feat_ref = bf16[8,128,768]{2,1,0:T(8,128)(2,1)} async-done(((bf16[8,128,768]{2,1,0:T(8,128)(2,1)}), bf16[8,128,768]{2,1,0:T(8,128)(2,1)}, u32[]{:S(2)}, u32[]{:S(2)}) %all-to-all-start) | async-done | bytes 1572896 | tf_op jit(solution)/shard_map/all_to_all | solution.py:206
  73.9 3.4 %all-to-all-start.1 = ((bf16[8,144,128]{2,1,0:T(8,128)(2,1)}), bf16[8,144,128]{2,1,0:T(8,128)(2,1)S(1)}, u32[]{:S(2)}, u32[]{:S(2)}) async-start(bf16[8,144,128]{2,1,0:T(8,128)(2,1)} %bitcast.4), calls=%async_computation.1 | async-start | bytes 589824 | tf_op jit(solution)/shard_map/all_to_all | solution.py:225
  77.4 0.0 copy-start.3
  77.4 0.0 copy-start.5
  77.4 2.4 %text_side.1 = (f32[16,1152]{1,0:T(8,128)}, bf16[16,1152]{1,0:T(8,128)(2,1)}, bf16[16,1152]{1,0:T(8,128)(2,1)}, bf16[16,1152]{1,0:T(8,128)(2,1)}) custom-call(bf16[64,1280]{1,0:T(8,128)(2,1)} %copy-done.1, bf16[128,1152]{1,0:T(8,128)(2,1)} %embed_ref.3, s32[1,128]{1,0:T(1,128)} %bitcast.6, bf16[8,2,72,128]{3,2,1,0:T(8,128)(2,1)} %get-tuple-element.15._turned), custom_call_target="tpu_custom_call" | custom-call | tf_op jit(solution)/shard_map/text_side/pallas_call | solution.py:171
  79.8 11.1 %collective-permute-start.4 = (bf16[16,1152]{1,0:T(8,128)(2,1)}, bf16[16,1152]{1,0:T(8,128)(2,1)S(1)}, u32[]{:S(2)}, u32[]{:S(2)}) collective-permute-start(bf16[16,1152]{1,0:T(8,128)(2,1)} %get-tuple-element.17), channel_id=1, source_target_pairs={{8,0},{16,8},{24,16},{32,24},{40,32},{48,40},{56,48},{64,56},{72,6... | collective-permute-start | bytes 110600 | tf_op jit(solution)/shard_map/ppermute | solution.py:26
  90.9 2.6 %collective-permute-start.5 = (bf16[16,1152]{1,0:T(8,128)(2,1)}, bf16[16,1152]{1,0:T(8,128)(2,1)S(1)}, u32[]{:S(2)}, u32[]{:S(2)}) collective-permute-start(bf16[16,1152]{1,0:T(8,128)(2,1)} %get-tuple-element.18), channel_id=1, source_target_pairs={{16,0},{24,8},{32,16},{40,24},{48,32},{56,40},{64,48},{72,56},{80,... | collective-permute-start | bytes 110600 | tf_op jit(solution)/shard_map/ppermute | solution.py:26
  93.5 2.5 %collective-permute-start.6 = (bf16[16,1152]{1,0:T(8,128)(2,1)}, bf16[16,1152]{1,0:T(8,128)(2,1)S(1)}, u32[]{:S(2)}, u32[]{:S(2)}) collective-permute-start(bf16[16,1152]{1,0:T(8,128)(2,1)} %get-tuple-element.19), channel_id=1, source_target_pairs={{24,0},{32,8},{40,16},{48,24},{56,32},{64,40},{72,48},{80,56},{88,... | collective-permute-start | bytes 110600 | tf_op jit(solution)/shard_map/ppermute | solution.py:26
  96.0 0.0 all-to-all-done.1.turned_ref
  96.0 2.8 %head_side.1 = bf16[16,54,128]{2,1,0:T(8,128)(2,1)} custom-call(bf16[8,144,128]{2,1,0:T(8,128)(2,1)S(1)} %all-to-all-done.1.turned_ref, bf16[8,128,768]{2,1,0:T(8,128)(2,1)} %all-to-all-done.feat_ref), custom_call_target="tpu_custom_call" | custom-call | tf_op jit(solution)/shard_map/head_side/pallas_call | solution.py:171
  98.8 8.9 %all-to-all-start.2 = ((bf16[16,54,128]{2,1,0:T(8,128)(2,1)}), bf16[16,54,128]{2,1,0:T(8,128)(2,1)S(1)}, u32[]{:S(2)}, u32[]{:S(2)}) async-start(bf16[16,54,128]{2,1,0:T(8,128)(2,1)} %head_side.1), calls=%async_computation.2 | async-start | bytes 458752 | tf_op jit(solution)/shard_map/all_to_all | solution.py:237
  107.8 0.0 collective-permute-done.4.one_ref
  107.8 0.0 collective-permute-done.5.two_ref
  107.8 1.1 finish.1
  109.0 12.6 %all-to-all-done.2.parts_ref = bf16[16,54,128]{2,1,0:T(8,128)(2,1)S(1)} async-done(((bf16[16,54,128]{2,1,0:T(8,128)(2,1)}), bf16[16,54,128]{2,1,0:T(8,128)(2,1)S(1)}, u32[]{:S(2)}, u32[]{:S(2)}) %all-to-all-start.2) | async-done | bytes 221216 | tf_op jit(solution)/shard_map/all_to_all | solution.py:237
  121.6 0.7 head_sum.1
  (11 shorter events, 0.0 us)
Async XLA Ops:
  2.2 32.4 %collective-permute-start.2 = (bf16[16,1280]{1,0:T(8,128)(2,1)}, bf16[16,1280]{1,0:T(8,128)(2,1)S(1)}, u32[]{:S(2)}, u32[]{:S(2)}) collective-permute-start(bf16[16,1280]{1,0:T(8,128)(2,1)} %prepare.1.refs_0_._payload), channel_id=1, source_target_pairs={{1000,0},{1008,8},{1016,16},{0,24},{8,32},{16,40},{24,48},{32,56},... | collective-permute-start | bytes 122888 | tf_op jit(solution)/shard_map/ppermute | solution.py:26
  8.1 26.6 %collective-permute-start.1 = (bf16[16,1280]{1,0:T(8,128)(2,1)}, bf16[16,1280]{1,0:T(8,128)(2,1)S(1)}, u32[]{:S(2)}, u32[]{:S(2)}) collective-permute-start(bf16[16,1280]{1,0:T(8,128)(2,1)} %prepare.1.refs_0_._payload), channel_id=1, source_target_pairs={{1008,0},{1016,8},{0,16},{8,24},{16,32},{24,40},{32,48},{40,56},{4... | collective-permute-start | bytes 122888 | tf_op jit(solution)/shard_map/ppermute | solution.py:26
  13.1 21.5 %collective-permute-start = (bf16[16,1280]{1,0:T(8,128)(2,1)}, bf16[16,1280]{1,0:T(8,128)(2,1)S(1)}, u32[]{:S(2)}, u32[]{:S(2)}) collective-permute-start(bf16[16,1280]{1,0:T(8,128)(2,1)} %prepare.1.refs_0_._payload), channel_id=1, source_target_pairs={{1016,0},{0,8},{8,16},{16,24},{24,32},{32,40},{40,48},{48,56},{56,... | collective-permute-start | bytes 122888 | tf_op jit(solution)/shard_map/ppermute | solution.py:26
  17.9 16.7 %copy-start.2 = (bf16[16,1280]{1,0:T(8,128)(2,1)S(1)}, bf16[16,1280]{1,0:T(8,128)(2,1)}, u32[]{:S(2)}) copy-start(bf16[16,1280]{1,0:T(8,128)(2,1)} %prepare.1.refs_0_._payload) | copy-start | bytes 122884
  17.9 56.0 %all-to-all-start = ((bf16[8,128,768]{2,1,0:T(8,128)(2,1)}), bf16[8,128,768]{2,1,0:T(8,128)(2,1)}, u32[]{:S(2)}, u32[]{:S(2)}) async-start(bf16[8,128,768]{2,1,0:T(8,128)(2,1)} %fan_out.1), calls=%async_computation | async-start | bytes 3145728 | tf_op jit(solution)/shard_map/all_to_all | solution.py:206
  34.7 19.9 %copy-start = (bf16[128,1152]{1,0:T(8,128)(2,1)S(1)}, bf16[128,1152]{1,0:T(8,128)(2,1)}, u32[]{:S(2)}) copy-start(bf16[128,1152]{1,0:T(8,128)(2,1)} %embed_ref.3) | copy-start | bytes 884740
  34.7 19.9 %copy-start.4 = (s32[128]{0:T(128)S(1)}, s32[128]{0:T(128)}, u32[]{:S(2)}) copy-start(s32[128]{0:T(128)} %param.11) | copy-start | bytes 1540
  34.7 42.6 %copy-start.1 = (bf16[64,1280]{1,0:T(8,128)(2,1)}, bf16[64,1280]{1,0:T(8,128)(2,1)S(1)}, u32[]{:S(2)}) copy-start(bf16[64,1280]{1,0:T(8,128)(2,1)S(1)} %assemble.1.own_ref) | copy-start | bytes 491524
  50.6 4.0 %collective-permute-start.3 = (bf16[256,1280]{1,0:T(8,128)(2,1)S(1)}, bf16[256,1280]{1,0:T(8,128)(2,1)S(1)}, u32[]{:S(2)}, u32[]{:S(2)}) collective-permute-start(bf16[256,1280]{1,0:T(8,128)(2,1)S(1)} %all_gather.3.a_ref), channel_id=1, source_target_pairs={{1,0},{0,1},{3,2},{2,3},{5,4},{4,5},{7,6},{6,7},{9,8},{8,9},{11,10... | collective-permute-start | bytes 1966088 | tf_op jit(solution)/shard_map/ppermute | solution.py:26
  73.9 22.1 %all-to-all-start.1 = ((bf16[8,144,128]{2,1,0:T(8,128)(2,1)}), bf16[8,144,128]{2,1,0:T(8,128)(2,1)S(1)}, u32[]{:S(2)}, u32[]{:S(2)}) async-start(bf16[8,144,128]{2,1,0:T(8,128)(2,1)} %bitcast.4), calls=%async_computation.1 | async-start | bytes 589824 | tf_op jit(solution)/shard_map/all_to_all | solution.py:225
  77.4 30.4 %copy-start.3 = (bf16[16,1152]{1,0:T(8,128)(2,1)S(1)}, bf16[16,1152]{1,0:T(8,128)(2,1)}, u32[]{:S(2)}) copy-start(bf16[16,1152]{1,0:T(8,128)(2,1)} %text_ref.1) | copy-start | bytes 110596
  77.4 30.4 %copy-start.5 = (bf16[1152,768]{1,0:T(8,128)(2,1)S(1)}, bf16[1152,768]{1,0:T(8,128)(2,1)}, u32[]{:S(2)}) copy-start(bf16[1152,768]{1,0:T(8,128)(2,1)} %head_ref.1) | copy-start | bytes 5308420
  79.8 28.1 %copy-start.6 = (f32[16,1152]{1,0:T(8,128)S(1)}, f32[16,1152]{1,0:T(8,128)}, u32[]{:S(2)}) copy-start(f32[16,1152]{1,0:T(8,128)} %get-tuple-element.16.share_ref) | copy-start | bytes 221188
  79.8 28.0 %collective-permute-start.4 = (bf16[16,1152]{1,0:T(8,128)(2,1)}, bf16[16,1152]{1,0:T(8,128)(2,1)S(1)}, u32[]{:S(2)}, u32[]{:S(2)}) collective-permute-start(bf16[16,1152]{1,0:T(8,128)(2,1)} %get-tuple-element.17), channel_id=1, source_target_pairs={{8,0},{16,8},{24,16},{32,24},{40,32},{48,40},{56,48},{64,56},{72,6... | collective-permute-start | bytes 110600 | tf_op jit(solution)/shard_map/ppermute | solution.py:26
  90.9 16.9 %collective-permute-start.5 = (bf16[16,1152]{1,0:T(8,128)(2,1)}, bf16[16,1152]{1,0:T(8,128)(2,1)S(1)}, u32[]{:S(2)}, u32[]{:S(2)}) collective-permute-start(bf16[16,1152]{1,0:T(8,128)(2,1)} %get-tuple-element.18), channel_id=1, source_target_pairs={{16,0},{24,8},{32,16},{40,24},{48,32},{56,40},{64,48},{72,56},{80,... | collective-permute-start | bytes 110600 | tf_op jit(solution)/shard_map/ppermute | solution.py:26
  93.5 14.3 %collective-permute-start.6 = (bf16[16,1152]{1,0:T(8,128)(2,1)}, bf16[16,1152]{1,0:T(8,128)(2,1)S(1)}, u32[]{:S(2)}, u32[]{:S(2)}) collective-permute-start(bf16[16,1152]{1,0:T(8,128)(2,1)} %get-tuple-element.19), channel_id=1, source_target_pairs={{24,0},{32,8},{40,16},{48,24},{56,32},{64,40},{72,48},{80,56},{88,... | collective-permute-start | bytes 110600 | tf_op jit(solution)/shard_map/ppermute | solution.py:26
  98.8 22.8 %all-to-all-start.2 = ((bf16[16,54,128]{2,1,0:T(8,128)(2,1)}), bf16[16,54,128]{2,1,0:T(8,128)(2,1)S(1)}, u32[]{:S(2)}, u32[]{:S(2)}) async-start(bf16[16,54,128]{2,1,0:T(8,128)(2,1)} %head_side.1), calls=%async_computation.2 | async-start | bytes 458752 | tf_op jit(solution)/shard_map/all_to_all | solution.py:237

commit v6 on v5

--- a/solution.py
+++ b/solution.py
@@ -96,17 +96,8 @@
     return (-signs * jax.nn.sigmoid(-signs * logits)).astype(bf16)
 
 
-def text_side(own_ref, embed_ref, ids_ref, _turned, *refs):
-    floats = embed_ref[...].astype(f32)
-    rounded = (floats / norms_of(floats)).astype(bf16)
-    slope = slopes(own_ref[...], rounded, ids_ref[...])
-    share = SCALE * jnp.dot(slope, rounded, preferred_element_type=f32)
-    count = refs[0].shape[0]
-    for k, ref in enumerate(refs):
-        ref[...] = share[k * count : (k + 1) * count].astype(ref.dtype)
-
-
-def image_side(a_ref, b_ref, embed_ref, ids_ref, out_ref, turned_ref):
+def image_side(pieces, plane_ref, a_ref, b_ref, own_ref, embed_ref, ids_ref, grad_ref, kept_ref, far_ref, *rest):
+    turned_refs, turned_f32 = rest[:-1], rest[-1]
     floats = embed_ref[...].astype(f32)
     norms = norms_of(floats)
     units = floats / norms
@@ -119,20 +110,38 @@
         total = total + lax.dot_general(slope, rows[:, :width], TN, preferred_element_type=f32)
     total = SCALE * total
     grad = (total - units * jnp.sum(units * total, -1, keepdims=True)) / norms
-    out_ref[...] = grad.astype(bf16)
-    turned = grad.T.astype(bf16)
-    planes, pieces, run = turned_ref.shape[0], turned_ref.shape[1], turned_ref.shape[2]
-    for p in range(pieces):
-        for z in range(planes):
-            start = (p * planes + z) * run
-            turned_ref[z, p] = turned[start : start + run]
-
-
-def head_side(turned_ref, feat_ref, out_ref):
-    blocks = turned_ref.shape[0]
-    part = jnp.zeros((turned_ref.shape[1], feat_ref.shape[2]), f32)
-    for k in range(blocks):
-        part = part + jnp.dot(turned_ref[k], feat_ref[k], preferred_element_type=f32)
+    grad_ref[...] = grad.astype(bf16)
+    turned_f32[...] = grad.T
+    planes = len(turned_refs)
+    run = width // (planes * pieces)
+    for ahead, ref in enumerate(turned_refs):
+        plane = lax.rem(plane_ref[0] + ahead, planes)
+        parts = [
+            turned_f32[pl.ds(pl.multiple_of((p * planes + plane) * run, 8), run)]
+            for p in range(pieces)
+        ]
+        ref[...] = jnp.concatenate(parts, 0).astype(bf16)
+    slope = slopes(own_ref[...], rounded, ids_ref[...])
+    share = SCALE * jnp.dot(slope, rounded, preferred_element_type=f32)
+    half = kept_ref.shape[0]
+    kept_ref[...] = share[:half]
+    far_ref[...] = share[half:].astype(bf16)
+
+
+def text_middle(kept_ref, back_ref, _parts, stay_ref, pass_ref):
+    count = stay_ref.shape[0]
+    total = kept_ref[...] + back_ref[...].astype(f32)
+    stay_ref[...] = total[:count]
+    pass_ref[...] = total[count:].astype(bf16)
+
+
+def head_side(plane_ref, feat_ref, *refs):
+    out_ref, planes = refs[-1], feat_ref.shape[0]
+    refs = refs[:planes]
+    part = jnp.zeros((refs[0].shape[0], feat_ref.shape[2]), f32)
+    for behind, ref in enumerate(refs):
+        plane = lax.rem(plane_ref[0] + (planes - behind), planes)
+        part = part + jnp.dot(ref[...], feat_ref[plane], preferred_element_type=f32)
     targets, groups = out_ref.shape[0], part.shape[1] // 128
     run = part.shape[0] // targets
     for c in range(targets):
@@ -149,14 +158,12 @@
         out_ref[:, g * 128 : (g + 1) * 128] = total[g * run : (g + 1) * run]
 
 
-def finish(grad_ref, head_ref, share_ref, one_ref, two_ref, three_ref, text_ref, image_ref, out_ref):
+def finish(grad_ref, head_ref, stay_ref, last_ref, text_ref, image_ref, out_ref):
     image_ref[...] = jnp.dot(grad_ref[...], head_ref[...], preferred_element_type=f32).astype(bf16)
     floats = text_ref[...].astype(f32)
     norms = norms_of(floats)
     units = floats / norms
-    total = share_ref[...]
-    for ref in (one_ref, two_ref, three_ref):
-        total = total + ref[...].astype(f32)
+    total = stay_ref[...] + last_ref[...].astype(f32)
     out_ref[...] = (total - units * jnp.sum(units * total, -1, keepdims=True)) / norms
 
 
@@ -176,7 +183,7 @@
         scratch_shapes=list(scratch),
         compiler_params=pltpu.CompilerParams(vmem_limit_bytes=room),
         cost_estimate=cost,
-        name=kernel.__name__,
+        name=getattr(kernel, "func", kernel).__name__,
     )(*args)
 
 
@@ -214,30 +221,32 @@
     here = lax.all_gather(own, "xl", axis=0, tiled=True)
     there = shifted(here, "core", 1)
 
-    pieces = lax.axis_size("xh")
-    run = width // (planes * pieces)
-    embed_grad, turned = call(
-        image_side,
-        [((images, width), bf16), ((planes, pieces, run, images), bf16)],
-        here, there, image_embed, ids, room=ROOM,
-    )
-    turned, feats = lax.optimization_barrier((turned, feats))
-    plane = lax.all_to_all(turned.reshape(planes, own_width, images), "z", 0, 0, tiled=True)
-
-    kept, *aways = call(
-        text_side, [((texts, width), f32)] + [((texts, width), bf16)] * 3,
-        own, image_embed, ids, turned, after=1,
-    )
-    backs = [shifted(away, BLK, -d) for d, away in zip((1, 2, 3), aways)]
+    plane = lax.axis_index("z").astype(i32).reshape(1)
+    embed_grad, kept, far, *turned = call(
+        functools.partial(image_side, lax.axis_size("xh")),
+        [((images, width), bf16), ((2 * texts, width), f32), ((2 * texts, width), bf16)]
+        + [((own_width, images), bf16)] * planes,
+        plane, here, there, own, image_embed, ids, smem=1, room=ROOM,
+        scratch=[pltpu.VMEM((width, images), f32)],
+    )
+    came = turned[:1] + [shifted(turned[d], "z", d) for d in range(1, planes)]
+
+    back = shifted(far, BLK, -2)
 
     rows = own_width // across
     parts = call(
-        head_side, [((across, rows * features // 128, 128), bf16)], plane, feats, room=ROOM
-    )
+        head_side, [((across, rows * features // 128, 128), bf16)],
+        plane, feats, *came, back, smem=1, after=1, room=ROOM,
+    )
+    stay, passed = call(
+        text_middle, [((texts, width), f32), ((texts, width), bf16)],
+        kept, back, parts, after=1, room=ROOM,
+    )
+    last = shifted(passed, BLK, -1)
     parts = lax.all_to_all(parts, ("xh", "y"), 0, 0, tiled=True)
     image_grad, text_grad = call(
         finish, [((images, features), bf16), ((texts, width), f32)],
-        embed_grad, head, kept, *backs, text_embed, cost=lasting(60), room=ROOM,
+        embed_grad, head, stay, last, text_embed, cost=lasting(1), room=ROOM,
     )
     head_grad = call(head_sum, [((rows, features), f32)], parts, room=ROOM)
     return (image_grad, text_grad, head_grad)

time: 123 us -> 122 us (level)
  the two profiles are of different devices: /device:TPU:4 before, /device:TPU:6 now
where the time goes in v6:
time: 122 us; the launch traced here: 121 us
  starting transfers between devices  84.6 us (69%)
  blocking collectives  17.2 us (14%)
  Pallas kernels  9.73 us (8%)
  waiting for transfers between devices  7.05 us (6%)
  local copies, waits for them, and re-layouts  1.5 us (1%)
    ppermute x13, starting transfers between devices, shifted(): lax.ppermute(block, axis, [((i - distance) % size, i) for i in range(size)])  63.1 us
    all_gather x1, blocking collectives, local(): here = lax.all_gather(own, 'xl', axis=0, tiled=True)  17.2 us
    all_to_all x1, starting transfers between devices, local(): feats = lax.all_to_all(feats, 'z', 0, 0, tiled=True)  16.7 us
    pallas_call x8, Pallas kernels, call(): pl.pallas_call(kernel, out_shape=outs[0] if single else outs, in_specs=sp...  9.73 us
    ppermute x13, waiting for transfers between devices, shifted(): lax.ppermute(block, axis, [((i - distance) % size, i) for i in range(size)])  7.04 us
    all_to_all x1, starting transfers between devices, local(): parts = lax.all_to_all(parts, ('xh', 'y'), 0, 0, tiled=True)  4.86 us
  transfers between devices with their start and end apart: 15, of which 3 were waited for; matrix products, arithmetic and copies ran while one was open for 0% of the time, Pallas kernels for 4%

profile of v6, /device:TPU:6, one launch (start us, length us, event | category | flops | bytes accessed | tf_op | source)
XLA Modules:
  0.0 121.0 jit_solution(6268156180571316340)
XLA Ops:
  0.6 1.6 %prepare.1.refs_0_._payload = bf16[16,1280]{1,0:T(8,128)(2,1)} custom-call(s32[1]{0:T(128)} %bitcast.1.pos_ref, bf16[16,1152]{1,0:T(8,128)(2,1)} %text_ref.1, s32[1,128]{1,0:T(1,128)} %bitcast.5, s32[1,128]{1,0:T(1,128)} %bitcast.7, f32[1,8]{1,0:T(1,128)} %bitcast.8), custom_call_target="tpu_custom_call" | custom-call | tf_op jit(solution)/shard_map/prepare/pallas_call | solution.py:178
  2.2 5.9 %collective-permute-start.2 = (bf16[16,1280]{1,0:T(8,128)(2,1)}, bf16[16,1280]{1,0:T(8,128)(2,1)S(1)}, u32[]{:S(2)}, u32[]{:S(2)}) collective-permute-start(bf16[16,1280]{1,0:T(8,128)(2,1)} %prepare.1.refs_0_._payload), channel_id=1, source_target_pairs={{1000,0},{1008,8},{1016,16},{0,24},{8,32},{16,40},{24,48},{32,56},... | collective-permute-start | bytes 122888 | tf_op jit(solution)/shard_map/ppermute | solution.py:26
  8.1 5.0 %collective-permute-start.1 = (bf16[16,1280]{1,0:T(8,128)(2,1)}, bf16[16,1280]{1,0:T(8,128)(2,1)S(1)}, u32[]{:S(2)}, u32[]{:S(2)}) collective-permute-start(bf16[16,1280]{1,0:T(8,128)(2,1)} %prepare.1.refs_0_._payload), channel_id=1, source_target_pairs={{1008,0},{1016,8},{0,16},{8,24},{16,32},{24,40},{32,48},{40,56},{4... | collective-permute-start | bytes 122888 | tf_op jit(solution)/shard_map/ppermute | solution.py:26
  13.1 2.7 %collective-permute-start = (bf16[16,1280]{1,0:T(8,128)(2,1)}, bf16[16,1280]{1,0:T(8,128)(2,1)S(1)}, u32[]{:S(2)}, u32[]{:S(2)}) collective-permute-start(bf16[16,1280]{1,0:T(8,128)(2,1)} %prepare.1.refs_0_._payload), channel_id=1, source_target_pairs={{1016,0},{0,8},{8,16},{16,24},{24,32},{32,40},{40,48},{48,56},{56,... | collective-permute-start | bytes 122888 | tf_op jit(solution)/shard_map/ppermute | solution.py:26
  15.8 2.1 %fan_out.1 = bf16[8,128,768]{2,1,0:T(8,128)(2,1)} custom-call(bf16[128,768]{1,0:T(8,128)(2,1)} %feat_ref.1, bf16[16,1280]{1,0:T(8,128)(2,1)} %prepare.1.refs_0_._payload), custom_call_target="tpu_custom_call" | custom-call | flops 20000000000 | tf_op jit(solution)/shard_map/fan_out/pallas_call | solution.py:178
  17.9 0.0 copy-start.1
  18.0 16.7 %all-to-all-start = ((bf16[8,128,768]{2,1,0:T(8,128)(2,1)}), bf16[8,128,768]{2,1,0:T(8,128)(2,1)}, u32[]{:S(2)}, u32[]{:S(2)}) async-start(bf16[8,128,768]{2,1,0:T(8,128)(2,1)} %fan_out.1), calls=%async_computation | async-start | bytes 3145728 | tf_op jit(solution)/shard_map/all_to_all | solution.py:213
  34.6 0.0 collective-permute-done.2.refs_3_
  34.7 0.0 collective-permute-done.1.refs_2_
  34.7 0.0 copy-start
  34.7 0.0 copy-start.3
  34.7 17.2 %all_gather.3.a_ref = bf16[256,1280]{1,0:T(8,128)(2,1)S(1)} all-gather(bf16[64,1280]{1,0:T(8,128)(2,1)S(1)} %assemble.1.own_ref), channel_id=1, replica_groups=mesh['xh'=2,'z'=8,'y'=8,'xl'=4,'core'=2] {'xl'}, dimensions={0}, use_global_device_ids=true | all-gather | bytes 819200 | tf_op jit(solution)/shard_map/all_gather | solution.py:221
  51.9 1.9 %collective-permute-start.3 = (bf16[256,1280]{1,0:T(8,128)(2,1)S(1)}, bf16[256,1280]{1,0:T(8,128)(2,1)S(1)}, u32[]{:S(2)}, u32[]{:S(2)}) collective-permute-start(bf16[256,1280]{1,0:T(8,128)(2,1)S(1)} %all_gather.3.a_ref), channel_id=1, source_target_pairs={{1,0},{0,1},{3,2},{2,3},{5,4},{4,5},{7,6},{6,7},{9,8},{8,9},{11,10... | collective-permute-start | bytes 1966088 | tf_op jit(solution)/shard_map/ppermute | solution.py:26
  53.9 2.1 %collective-permute-done.3.b_ref = bf16[256,1280]{1,0:T(8,128)(2,1)S(1)} collective-permute-done((bf16[256,1280]{1,0:T(8,128)(2,1)S(1)}, bf16[256,1280]{1,0:T(8,128)(2,1)S(1)}, u32[]{:S(2)}, u32[]{:S(2)}) %collective-permute-start.3) | collective-permute-done | bytes 655392 | tf_op jit(solution)/shard_map/ppermute | solution.py:26
  55.9 1.4 %image_side.1 = (bf16[128,1152]{1,0:T(8,128)(2,1)S(1)}, f32[32,1152]{1,0:T(8,128)S(1)}, bf16[32,1152]{1,0:T(8,128)(2,1)S(1)}, bf16[144,128]{1,0:T(8,128)(2,1)S(1...) custom-call(s32[1]{0:T(128)} %bitcast.plane_ref, ...), custom_call_target="tpu_custom_call" | custom-call | tf_op jit(solution)/shard_map/image_side/pallas_call | solution.py:178
  57.3 0.0 copy-start.2
  57.3 3.2 %collective-permute-start.5 = (bf16[144,128]{1,0:T(8,128)(2,1)S(1)}, bf16[144,128]{1,0:T(8,128)(2,1)S(1)}, u32[]{:S(2)}, u32[]{:S(2)}) collective-permute-start(bf16[144,128]{1,0:T(8,128)(2,1)S(1)} %get-tuple-element.22), channel_id=1, source_target_pairs={{448,0},{0,64},{64,128},{128,192},{192,256},{256,320},{320,384},{3... | collective-permute-start | bytes 110600 | tf_op jit(solution)/shard_map/ppermute | solution.py:26
  60.5 4.4 %collective-permute-start.6 = (bf16[144,128]{1,0:T(8,128)(2,1)S(1)}, bf16[144,128]{1,0:T(8,128)(2,1)S(1)}, u32[]{:S(2)}, u32[]{:S(2)}) collective-permute-start(bf16[144,128]{1,0:T(8,128)(2,1)S(1)} %get-tuple-element.23), channel_id=1, source_target_pairs={{384,0},{448,64},{0,128},{64,192},{128,256},{192,320},{256,384},{3... | collective-permute-start | bytes 110600 | tf_op jit(solution)/shard_map/ppermute | solution.py:26
  65.0 4.6 %collective-permute-start.7 = (bf16[144,128]{1,0:T(8,128)(2,1)S(1)}, bf16[144,128]{1,0:T(8,128)(2,1)S(1)}, u32[]{:S(2)}, u32[]{:S(2)}) collective-permute-start(bf16[144,128]{1,0:T(8,128)(2,1)S(1)} %get-tuple-element.24), channel_id=1, source_target_pairs={{320,0},{384,64},{448,128},{0,192},{64,256},{128,320},{192,384},{2... | collective-permute-start | bytes 110600 | tf_op jit(solution)/shard_map/ppermute | solution.py:26
  69.6 10.2 %collective-permute-start.4 = (bf16[32,1152]{1,0:T(8,128)(2,1)S(1)}, bf16[32,1152]{1,0:T(8,128)(2,1)S(1)}, u32[]{:S(2)}, u32[]{:S(2)}) collective-permute-start(bf16[32,1152]{1,0:T(8,128)(2,1)S(1)} %get-tuple-element.20), channel_id=1, source_target_pairs={{16,0},{24,8},{32,16},{40,24},{48,32},{56,40},{64,48},{72,56},{80,... | collective-permute-start | bytes 221192 | tf_op jit(solution)/shard_map/ppermute | solution.py:26
  79.7 1.9 %collective-permute-start.8 = (bf16[144,128]{1,0:T(8,128)(2,1)S(1)}, bf16[144,128]{1,0:T(8,128)(2,1)S(1)}, u32[]{:S(2)}, u32[]{:S(2)}) collective-permute-start(bf16[144,128]{1,0:T(8,128)(2,1)S(1)} %get-tuple-element.25), channel_id=1, source_target_pairs={{256,0},{320,64},{384,128},{448,192},{0,256},{64,320},{128,384},{1... | collective-permute-start | bytes 110600 | tf_op jit(solution)/shard_map/ppermute | solution.py:26
  81.7 3.4 %collective-permute-start.9 = (bf16[144,128]{1,0:T(8,128)(2,1)S(1)}, bf16[144,128]{1,0:T(8,128)(2,1)S(1)}, u32[]{:S(2)}, u32[]{:S(2)}) collective-permute-start(bf16[144,128]{1,0:T(8,128)(2,1)S(1)} %get-tuple-element.26), channel_id=1, source_target_pairs={{192,0},{256,64},{320,128},{384,192},{448,256},{0,320},{64,384},{1... | collective-permute-start | bytes 110600 | tf_op jit(solution)/shard_map/ppermute | solution.py:26
  85.1 5.6 %collective-permute-start.10 = (bf16[144,128]{1,0:T(8,128)(2,1)S(1)}, bf16[144,128]{1,0:T(8,128)(2,1)S(1)}, u32[]{:S(2)}, u32[]{:S(2)}) collective-permute-start(bf16[144,128]{1,0:T(8,128)(2,1)S(1)} %get-tuple-element.27), channel_id=1, source_target_pairs={{128,0},{192,64},{256,128},{320,192},{384,256},{448,320},{0,384},{... | collective-permute-start | bytes 110600 | tf_op jit(solution)/shard_map/ppermute | solution.py:26
  90.8 3.1 %collective-permute-start.11 = (bf16[144,128]{1,0:T(8,128)(2,1)S(1)}, bf16[144,128]{1,0:T(8,128)(2,1)S(1)}, u32[]{:S(2)}, u32[]{:S(2)}) collective-permute-start(bf16[144,128]{1,0:T(8,128)(2,1)S(1)} %get-tuple-element.28), channel_id=1, source_target_pairs={{64,0},{128,64},{192,128},{256,192},{320,256},{384,320},{448,384},... | collective-permute-start | bytes 110600 | tf_op jit(solution)/shard_map/ppermute | solution.py:26
  94.0 3.3 %collective-permute-done.11.refs_7_ = bf16[144,128]{1,0:T(8,128)(2,1)S(1)} collective-permute-done((bf16[144,128]{1,0:T(8,128)(2,1)S(1)}, bf16[144,128]{1,0:T(8,128)(2,1)S(1)}, u32[]{:S(2)}, u32[]{:S(2)}) %collective-permute-start.11) | collective-permute-done | bytes 36896 | tf_op jit(solution)/shard_map/ppermute | solution.py:26
  97.3 2.8 %head_side.1._parts = bf16[16,54,128]{2,1,0:T(8,128)(2,1)} custom-call(s32[1]{0:T(128)} %bitcast.plane_ref, bf16[8,128,768]{2,1,0:T(8,128)(2,1)} %all-to-all-done.feat_ref, bf16[144,128]{1,0:T(8,128)(2,1)S(1)} %get-tuple-element.21.refs_0_, bf16[144,128]{1,0:T(8,128)(2,1)S(1)} %collective-permute-done.5.refs_1_, ...), custom_call_target="tpu_custom_call" | custom-call | tf_op jit(solution)/shard_map/head_side/pallas_call | solution.py:178
  100.2 4.9 %all-to-all-start.1 = ((bf16[16,54,128]{2,1,0:T(8,128)(2,1)}), bf16[16,54,128]{2,1,0:T(8,128)(2,1)S(1)}, u32[]{:S(2)}, u32[]{:S(2)}) async-start(bf16[16,54,128]{2,1,0:T(8,128)(2,1)} %head_side.1._parts), calls=%async_computation.1 | async-start | bytes 458752 | tf_op jit(solution)/shard_map/all_to_all | solution.py:246
  105.0 11.1 %collective-permute-start.12 = (bf16[16,1152]{1,0:T(8,128)(2,1)S(1)}, bf16[16,1152]{1,0:T(8,128)(2,1)S(1)}, u32[]{:S(2)}, u32[]{:S(2)}) collective-permute-start(bf16[16,1152]{1,0:T(8,128)(2,1)S(1)} %get-tuple-element.30), channel_id=1, source_target_pairs={{8,0},{16,8},{24,16},{32,24},{40,32},{48,40},{56,48},{64,56},{72,6... | collective-permute-start | bytes 110600 | tf_op jit(solution)/shard_map/ppermute | solution.py:26
  116.1 1.6 %collective-permute-done.12.last_ref = bf16[16,1152]{1,0:T(8,128)(2,1)S(1)} collective-permute-done((bf16[16,1152]{1,0:T(8,128)(2,1)S(1)}, bf16[16,1152]{1,0:T(8,128)(2,1)S(1)}, u32[]{:S(2)}, u32[]{:S(2)}) %collective-permute-start.12) | collective-permute-done | bytes 36896 | tf_op jit(solution)/shard_map/ppermute | solution.py:26
  117.7 1.5 %copy-done.4 = bf16[1152,768]{1,0:T(8,128)(2,1)S(1)} copy-done((bf16[1152,768]{1,0:T(8,128)(2,1)S(1)}, bf16[1152,768]{1,0:T(8,128)(2,1)}, u32[]{:S(2)}) %copy-start.4) | copy-done | bytes 1769496
  119.2 1.1 finish.1
  120.3 0.7 head_sum.1
  (17 shorter events, 0.1 us)
Async XLA Ops:
  2.2 32.4 %collective-permute-start.2 = (bf16[16,1280]{1,0:T(8,128)(2,1)}, bf16[16,1280]{1,0:T(8,128)(2,1)S(1)}, u32[]{:S(2)}, u32[]{:S(2)}) collective-permute-start(bf16[16,1280]{1,0:T(8,128)(2,1)} %prepare.1.refs_0_._payload), channel_id=1, source_target_pairs={{1000,0},{1008,8},{1016,16},{0,24},{8,32},{16,40},{24,48},{32,56},... | collective-permute-start | bytes 122888 | tf_op jit(solution)/shard_map/ppermute | solution.py:26
  8.1 26.6 %collective-permute-start.1 = (bf16[16,1280]{1,0:T(8,128)(2,1)}, bf16[16,1280]{1,0:T(8,128)(2,1)S(1)}, u32[]{:S(2)}, u32[]{:S(2)}) collective-permute-start(bf16[16,1280]{1,0:T(8,128)(2,1)} %prepare.1.refs_0_._payload), channel_id=1, source_target_pairs={{1008,0},{1016,8},{0,16},{8,24},{16,32},{24,40},{32,48},{40,56},{4... | collective-permute-start | bytes 122888 | tf_op jit(solution)/shard_map/ppermute | solution.py:26
  13.1 21.5 %collective-permute-start = (bf16[16,1280]{1,0:T(8,128)(2,1)}, bf16[16,1280]{1,0:T(8,128)(2,1)S(1)}, u32[]{:S(2)}, u32[]{:S(2)}) collective-permute-start(bf16[16,1280]{1,0:T(8,128)(2,1)} %prepare.1.refs_0_._payload), channel_id=1, source_target_pairs={{1016,0},{0,8},{8,16},{16,24},{24,32},{32,40},{40,48},{48,56},{56,... | collective-permute-start | bytes 122888 | tf_op jit(solution)/shard_map/ppermute | solution.py:26
  17.9 16.7 %copy-start.1 = (bf16[16,1280]{1,0:T(8,128)(2,1)S(1)}, bf16[16,1280]{1,0:T(8,128)(2,1)}, u32[]{:S(2)}) copy-start(bf16[16,1280]{1,0:T(8,128)(2,1)} %prepare.1.refs_0_._payload) | copy-start | bytes 122884
  18.0 79.4 %all-to-all-start = ((bf16[8,128,768]{2,1,0:T(8,128)(2,1)}), bf16[8,128,768]{2,1,0:T(8,128)(2,1)}, u32[]{:S(2)}, u32[]{:S(2)}) async-start(bf16[8,128,768]{2,1,0:T(8,128)(2,1)} %fan_out.1), calls=%async_computation | async-start | bytes 3145728 | tf_op jit(solution)/shard_map/all_to_all | solution.py:213
  34.7 21.2 %copy-start = (bf16[128,1152]{1,0:T(8,128)(2,1)S(1)}, bf16[128,1152]{1,0:T(8,128)(2,1)}, u32[]{:S(2)}) copy-start(bf16[128,1152]{1,0:T(8,128)(2,1)} %embed_ref.1) | copy-start | bytes 884740
  34.7 21.2 %copy-start.3 = (s32[128]{0:T(128)S(1)}, s32[128]{0:T(128)}, u32[]{:S(2)}) copy-start(s32[128]{0:T(128)} %param.11) | copy-start | bytes 1540
  51.9 4.0 %collective-permute-start.3 = (bf16[256,1280]{1,0:T(8,128)(2,1)S(1)}, bf16[256,1280]{1,0:T(8,128)(2,1)S(1)}, u32[]{:S(2)}, u32[]{:S(2)}) collective-permute-start(bf16[256,1280]{1,0:T(8,128)(2,1)S(1)} %all_gather.3.a_ref), channel_id=1, source_target_pairs={{1,0},{0,1},{3,2},{2,3},{5,4},{4,5},{7,6},{6,7},{9,8},{8,9},{11,10... | collective-permute-start | bytes 1966088 | tf_op jit(solution)/shard_map/ppermute | solution.py:26
  57.3 60.4 %copy-start.2 = (bf16[16,1152]{1,0:T(8,128)(2,1)S(1)}, bf16[16,1152]{1,0:T(8,128)(2,1)}, u32[]{:S(2)}) copy-start(bf16[16,1152]{1,0:T(8,128)(2,1)} %text_ref.1) | copy-start | bytes 110596
  57.3 24.3 %collective-permute-start.5 = (bf16[144,128]{1,0:T(8,128)(2,1)S(1)}, bf16[144,128]{1,0:T(8,128)(2,1)S(1)}, u32[]{:S(2)}, u32[]{:S(2)}) collective-permute-start(bf16[144,128]{1,0:T(8,128)(2,1)S(1)} %get-tuple-element.22), channel_id=1, source_target_pairs={{448,0},{0,64},{64,128},{128,192},{192,256},{256,320},{320,384},{3... | collective-permute-start | bytes 110600 | tf_op jit(solution)/shard_map/ppermute | solution.py:26
  60.5 24.6 %collective-permute-start.6 = (bf16[144,128]{1,0:T(8,128)(2,1)S(1)}, bf16[144,128]{1,0:T(8,128)(2,1)S(1)}, u32[]{:S(2)}, u32[]{:S(2)}) collective-permute-start(bf16[144,128]{1,0:T(8,128)(2,1)S(1)} %get-tuple-element.23), channel_id=1, source_target_pairs={{384,0},{448,64},{0,128},{64,192},{128,256},{192,320},{256,384},{3... | collective-permute-start | bytes 110600 | tf_op jit(solution)/shard_map/ppermute | solution.py:26
  65.0 25.8 %collective-permute-start.7 = (bf16[144,128]{1,0:T(8,128)(2,1)S(1)}, bf16[144,128]{1,0:T(8,128)(2,1)S(1)}, u32[]{:S(2)}, u32[]{:S(2)}) collective-permute-start(bf16[144,128]{1,0:T(8,128)(2,1)S(1)} %get-tuple-element.24), channel_id=1, source_target_pairs={{320,0},{384,64},{448,128},{0,192},{64,256},{128,320},{192,384},{2... | collective-permute-start | bytes 110600 | tf_op jit(solution)/shard_map/ppermute | solution.py:26
  69.6 27.8 %collective-permute-start.4 = (bf16[32,1152]{1,0:T(8,128)(2,1)S(1)}, bf16[32,1152]{1,0:T(8,128)(2,1)S(1)}, u32[]{:S(2)}, u32[]{:S(2)}) collective-permute-start(bf16[32,1152]{1,0:T(8,128)(2,1)S(1)} %get-tuple-element.20), channel_id=1, source_target_pairs={{16,0},{24,8},{32,16},{40,24},{48,32},{56,40},{64,48},{72,56},{80,... | collective-permute-start | bytes 221192 | tf_op jit(solution)/shard_map/ppermute | solution.py:26
  79.7 14.2 %collective-permute-start.8 = (bf16[144,128]{1,0:T(8,128)(2,1)S(1)}, bf16[144,128]{1,0:T(8,128)(2,1)S(1)}, u32[]{:S(2)}, u32[]{:S(2)}) collective-permute-start(bf16[144,128]{1,0:T(8,128)(2,1)S(1)} %get-tuple-element.25), channel_id=1, source_target_pairs={{256,0},{320,64},{384,128},{448,192},{0,256},{64,320},{128,384},{1... | collective-permute-start | bytes 110600 | tf_op jit(solution)/shard_map/ppermute | solution.py:26
  81.7 12.3 %collective-permute-start.9 = (bf16[144,128]{1,0:T(8,128)(2,1)S(1)}, bf16[144,128]{1,0:T(8,128)(2,1)S(1)}, u32[]{:S(2)}, u32[]{:S(2)}) collective-permute-start(bf16[144,128]{1,0:T(8,128)(2,1)S(1)} %get-tuple-element.26), channel_id=1, source_target_pairs={{192,0},{256,64},{320,128},{384,192},{448,256},{0,320},{64,384},{1... | collective-permute-start | bytes 110600 | tf_op jit(solution)/shard_map/ppermute | solution.py:26
  85.1 8.8 %collective-permute-start.10 = (bf16[144,128]{1,0:T(8,128)(2,1)S(1)}, bf16[144,128]{1,0:T(8,128)(2,1)S(1)}, u32[]{:S(2)}, u32[]{:S(2)}) collective-permute-start(bf16[144,128]{1,0:T(8,128)(2,1)S(1)} %get-tuple-element.27), channel_id=1, source_target_pairs={{128,0},{192,64},{256,128},{320,192},{384,256},{448,320},{0,384},{... | collective-permute-start | bytes 110600 | tf_op jit(solution)/shard_map/ppermute | solution.py:26
  90.8 6.5 %collective-permute-start.11 = (bf16[144,128]{1,0:T(8,128)(2,1)S(1)}, bf16[144,128]{1,0:T(8,128)(2,1)S(1)}, u32[]{:S(2)}, u32[]{:S(2)}) collective-permute-start(bf16[144,128]{1,0:T(8,128)(2,1)S(1)} %get-tuple-element.28), channel_id=1, source_target_pairs={{64,0},{128,64},{192,128},{256,192},{320,256},{384,320},{448,384},... | collective-permute-start | bytes 110600 | tf_op jit(solution)/shard_map/ppermute | solution.py:26
  100.2 20.2 %all-to-all-start.1 = ((bf16[16,54,128]{2,1,0:T(8,128)(2,1)}), bf16[16,54,128]{2,1,0:T(8,128)(2,1)S(1)}, u32[]{:S(2)}, u32[]{:S(2)}) async-start(bf16[16,54,128]{2,1,0:T(8,128)(2,1)} %head_side.1._parts), calls=%async_computation.1 | async-start | bytes 458752 | tf_op jit(solution)/shard_map/all_to_all | solution.py:246
  105.0 12.7 %collective-permute-start.12 = (bf16[16,1152]{1,0:T(8,128)(2,1)S(1)}, bf16[16,1152]{1,0:T(8,128)(2,1)S(1)}, u32[]{:S(2)}, u32[]{:S(2)}) collective-permute-start(bf16[16,1152]{1,0:T(8,128)(2,1)S(1)} %get-tuple-element.30), channel_id=1, source_target_pairs={{8,0},{16,8},{24,16},{32,24},{40,32},{48,40},{56,48},{64,56},{72,6... | collective-permute-start | bytes 110600 | tf_op jit(solution)/shard_map/ppermute | solution.py:26
  117.7 1.5 %copy-start.4 = (bf16[1152,768]{1,0:T(8,128)(2,1)S(1)}, bf16[1152,768]{1,0:T(8,128)(2,1)}, u32[]{:S(2)}) copy-start(bf16[1152,768]{1,0:T(8,128)(2,1)} %head_ref.1) | copy-start | bytes 5308420

commit v7 on v6

--- a/solution.py
+++ b/solution.py
@@ -1,5 +1,3 @@
-import functools
-
 import jax
 import jax.numpy as jnp
 from jax import lax
@@ -96,8 +94,7 @@
     return (-signs * jax.nn.sigmoid(-signs * logits)).astype(bf16)
 
 
-def image_side(pieces, plane_ref, a_ref, b_ref, own_ref, embed_ref, ids_ref, grad_ref, kept_ref, far_ref, *rest):
-    turned_refs, turned_f32 = rest[:-1], rest[-1]
+def image_side(a_ref, b_ref, own_ref, embed_ref, ids_ref, grad_ref, kept_ref, far_ref, turned_ref):
     floats = embed_ref[...].astype(f32)
     norms = norms_of(floats)
     units = floats / norms
@@ -111,16 +108,12 @@
     total = SCALE * total
     grad = (total - units * jnp.sum(units * total, -1, keepdims=True)) / norms
     grad_ref[...] = grad.astype(bf16)
-    turned_f32[...] = grad.T
-    planes = len(turned_refs)
-    run = width // (planes * pieces)
-    for ahead, ref in enumerate(turned_refs):
-        plane = lax.rem(plane_ref[0] + ahead, planes)
-        parts = [
-            turned_f32[pl.ds(pl.multiple_of((p * planes + plane) * run, 8), run)]
-            for p in range(pieces)
-        ]
-        ref[...] = jnp.concatenate(parts, 0).astype(bf16)
+    turned = grad.T.astype(bf16)
+    planes, pieces, run = turned_ref.shape[:3]
+    for p in range(pieces):
+        for z in range(planes):
+            start = (p * planes + z) * run
+            turned_ref[z, p] = turned[start : start + run]
     slope = slopes(own_ref[...], rounded, ids_ref[...])
     share = SCALE * jnp.dot(slope, rounded, preferred_element_type=f32)
     half = kept_ref.shape[0]
@@ -135,13 +128,10 @@
     pass_ref[...] = total[count:].astype(bf16)
 
 
-def head_side(plane_ref, feat_ref, *refs):
-    out_ref, planes = refs[-1], feat_ref.shape[0]
-    refs = refs[:planes]
-    part = jnp.zeros((refs[0].shape[0], feat_ref.shape[2]), f32)
-    for behind, ref in enumerate(refs):
-        plane = lax.rem(plane_ref[0] + (planes - behind), planes)
-        part = part + jnp.dot(ref[...], feat_ref[plane], preferred_element_type=f32)
+def head_side(turned_ref, feat_ref, _back, out_ref):
+    part = jnp.zeros((turned_ref.shape[1], feat_ref.shape[2]), f32)
+    for k in range(turned_ref.shape[0]):
+        part = part + jnp.dot(turned_ref[k], feat_ref[k], preferred_element_type=f32)
     targets, groups = out_ref.shape[0], part.shape[1] // 128
     run = part.shape[0] // targets
     for c in range(targets):
@@ -158,8 +148,7 @@
         out_ref[:, g * 128 : (g + 1) * 128] = total[g * run : (g + 1) * run]
 
 
-def finish(grad_ref, head_ref, stay_ref, last_ref, text_ref, image_ref, out_ref):
-    image_ref[...] = jnp.dot(grad_ref[...], head_ref[...], preferred_element_type=f32).astype(bf16)
+def text_back(stay_ref, last_ref, text_ref, out_ref):
     floats = text_ref[...].astype(f32)
     norms = norms_of(floats)
     units = floats / norms
@@ -183,7 +172,7 @@
         scratch_shapes=list(scratch),
         compiler_params=pltpu.CompilerParams(vmem_limit_bytes=room),
         cost_estimate=cost,
-        name=getattr(kernel, "func", kernel).__name__,
+        name=kernel.__name__,
     )(*args)
 
 
@@ -208,35 +197,36 @@
     )
     feats = call(
         fan_out, [((planes, images, features), bf16)], image_feat, payload,
-        after=1, out_hbm=1, scratch=[pltpu.SemaphoreType.DMA], cost=lasting(20),
+        after=1, out_hbm=1, scratch=[pltpu.SemaphoreType.DMA],
     )
     feats = lax.all_to_all(feats, "z", 0, 0, tiled=True)
 
     window = [payload] + [shifted(payload, BLK, d) for d in (1, 2, 3)]
     own = call(
         assemble, [((len(window) * texts, width + TAIL), bf16)], *window,
-        cost=lasting(400), room=ROOM,
+        room=ROOM,
     )
 
     here = lax.all_gather(own, "xl", axis=0, tiled=True)
     there = shifted(here, "core", 1)
 
-    plane = lax.axis_index("z").astype(i32).reshape(1)
-    embed_grad, kept, far, *turned = call(
-        functools.partial(image_side, lax.axis_size("xh")),
-        [((images, width), bf16), ((2 * texts, width), f32), ((2 * texts, width), bf16)]
-        + [((own_width, images), bf16)] * planes,
-        plane, here, there, own, image_embed, ids, smem=1, room=ROOM,
-        scratch=[pltpu.VMEM((width, images), f32)],
-    )
-    came = turned[:1] + [shifted(turned[d], "z", d) for d in range(1, planes)]
+    pieces = lax.axis_size("xh")
+    run = width // (planes * pieces)
+    embed_grad, kept, far, turned = call(
+        image_side,
+        [((images, width), bf16), ((2 * texts, width), f32), ((2 * texts, width), bf16),
+         ((planes, pieces, run, images), bf16)],
+        here, there, own, image_embed, ids, room=ROOM,
+    )
+    turned, feats = lax.optimization_barrier((turned, feats))
+    plane = lax.all_to_all(turned.reshape(planes, own_width, images), "z", 0, 0, tiled=True)
 
     back = shifted(far, BLK, -2)
 
     rows = own_width // across
     parts = call(
         head_side, [((across, rows * features // 128, 128), bf16)],
-        plane, feats, *came, back, smem=1, after=1, room=ROOM,
+        plane, feats, back, after=1,
     )
     stay, passed = call(
         text_middle, [((texts, width), f32), ((texts, width), bf16)],
@@ -244,9 +234,9 @@
     )
     last = shifted(passed, BLK, -1)
     parts = lax.all_to_all(parts, ("xh", "y"), 0, 0, tiled=True)
-    image_grad, text_grad = call(
-        finish, [((images, features), bf16), ((texts, width), f32)],
-        embed_grad, head, stay, last, text_embed, cost=lasting(1), room=ROOM,
+    image_grad = jnp.dot(embed_grad, head, preferred_element_type=f32).astype(bf16)
+    text_grad = call(
+        text_back, [((texts, width), f32)], stay, last, text_embed, cost=lasting(1), room=ROOM
     )
     head_grad = call(head_sum, [((rows, features), f32)], parts, room=ROOM)
     return (image_grad, text_grad, head_grad)

time: 122 us -> 114 us (0.934)
  the two profiles are of different devices: /device:TPU:6 before, /device:TPU:2 now
where the time goes in v7:
time: 114 us; the launch traced here: 113 us
  starting transfers between devices  61.4 us (54%)
  waiting for transfers between devices  21.2 us (19%)
  blocking collectives  15.9 us (14%)
  Pallas kernels  10.3 us (9%)
  local copies, waits for them, and re-layouts  2.61 us (2%)
    ppermute x6, starting transfers between devices, shifted(): lax.ppermute(block, axis, [((i - distance) % size, i) for i in range(size)])  36.5 us
    ppermute x6, waiting for transfers between devices, shifted(): lax.ppermute(block, axis, [((i - distance) % size, i) for i in range(size)])  17 us
    all_to_all x1, starting transfers between devices, local(): feats = lax.all_to_all(feats, 'z', 0, 0, tiled=True)  16.8 us
    all_gather x1, blocking collectives, local(): here = lax.all_gather(own, 'xl', axis=0, tiled=True)  15.9 us
    pallas_call x8, Pallas kernels, call(): pl.pallas_call(kernel, out_shape=outs[0] if single else outs, in_specs=sp...  10.3 us
    all_to_all x1, starting transfers between devices, local(): parts = lax.all_to_all(parts, ('xh', 'y'), 0, 0, tiled=True)  4.71 us
    all_to_all x1, waiting for transfers between devices, local(): lax.all_to_all(turned.reshape(planes, own_width, images), 'z', 0, 0, tile...  4.2 us
    all_to_all x1, starting transfers between devices, local(): lax.all_to_all(turned.reshape(planes, own_width, images), 'z', 0, 0, tile...  3.42 us
  transfers between devices with their start and end apart: 9, of which 7 were waited for; matrix products, arithmetic and copies ran while one was open for 1% of the time, Pallas kernels for 3%

profile of v7, /device:TPU:2, one launch (start us, length us, event | category | flops | bytes accessed | tf_op | source)
XLA Modules:
  0.0 113.3 jit_solution(6133903643647660460)
XLA Ops:
  0.6 0.0 copy-start
  0.7 1.7 %prepare.1.refs_0_._payload = bf16[16,1280]{1,0:T(8,128)(2,1)} custom-call(s32[1]{0:T(128)} %bitcast.pos_ref, bf16[16,1152]{1,0:T(8,128)(2,1)} %text_ref.1, s32[1,128]{1,0:T(1,128)} %bitcast.7, s32[1,128]{1,0:T(1,128)} %bitcast.9, f32[1,8]{1,0:T(1,128)} %bitcast.10), custom_call_target="tpu_custom_call" | custom-call | tf_op jit(solution)/shard_map/prepare/pallas_call | solution.py:167
  2.4 2.1 %fan_out.1 = bf16[8,128,768]{2,1,0:T(8,128)(2,1)} custom-call(bf16[128,768]{1,0:T(8,128)(2,1)} %feat_ref.1, bf16[16,1280]{1,0:T(8,128)(2,1)} %prepare.1.refs_0_._payload), custom_call_target="tpu_custom_call" | custom-call | tf_op jit(solution)/shard_map/fan_out/pallas_call | solution.py:167
  4.5 0.0 copy-start.2
  4.5 0.0 copy-start.5
  4.5 0.0 copy-start.7
  4.5 16.8 %all-to-all-start = ((bf16[8,128,768]{2,1,0:T(8,128)(2,1)}), bf16[8,128,768]{2,1,0:T(8,128)(2,1)}, u32[]{:S(2)}, u32[]{:S(2)}) async-start(bf16[8,128,768]{2,1,0:T(8,128)(2,1)} %fan_out.1), calls=%async_computation | async-start | bytes 3145728 | tf_op jit(solution)/shard_map/all_to_all | solution.py:202
  21.3 5.9 %collective-permute-start.2 = (bf16[16,1280]{1,0:T(8,128)(2,1)S(1)}, bf16[16,1280]{1,0:T(8,128)(2,1)S(1)}, u32[]{:S(2)}, u32[]{:S(2)}) collective-permute-start(bf16[16,1280]{1,0:T(8,128)(2,1)S(1)} %copy-done.2), channel_id=1, source_target_pairs={{1000,0},{1008,8},{1016,16},{0,24},{8,32},{16,40},{24,48},{32,56},... | collective-permute-start | bytes 122888 | tf_op jit(solution)/shard_map/ppermute | solution.py:24
  27.2 5.0 %collective-permute-start.1 = (bf16[16,1280]{1,0:T(8,128)(2,1)S(1)}, bf16[16,1280]{1,0:T(8,128)(2,1)S(1)}, u32[]{:S(2)}, u32[]{:S(2)}) collective-permute-start(bf16[16,1280]{1,0:T(8,128)(2,1)S(1)} %copy-done.2), channel_id=1, source_target_pairs={{1008,0},{1016,8},{0,16},{8,24},{16,32},{24,40},{32,48},{40,56},{4... | collective-permute-start | bytes 122888 | tf_op jit(solution)/shard_map/ppermute | solution.py:24
  32.2 2.7 %collective-permute-start = (bf16[16,1280]{1,0:T(8,128)(2,1)S(1)}, bf16[16,1280]{1,0:T(8,128)(2,1)S(1)}, u32[]{:S(2)}, u32[]{:S(2)}) collective-permute-start(bf16[16,1280]{1,0:T(8,128)(2,1)S(1)} %copy-done.2), channel_id=1, source_target_pairs={{1016,0},{0,8},{8,16},{16,24},{24,32},{32,40},{40,48},{48,56},{56,... | collective-permute-start | bytes 122888 | tf_op jit(solution)/shard_map/ppermute | solution.py:24
  34.9 3.3 %collective-permute-done.2.refs_3_ = bf16[16,1280]{1,0:T(8,128)(2,1)S(1)} collective-permute-done((bf16[16,1280]{1,0:T(8,128)(2,1)S(1)}, bf16[16,1280]{1,0:T(8,128)(2,1)S(1)}, u32[]{:S(2)}, u32[]{:S(2)}) %collective-permute-start.2) | collective-permute-done | bytes 40992 | tf_op jit(solution)/shard_map/ppermute | solution.py:24
  38.3 4.3 %collective-permute-done.1.refs_2_ = bf16[16,1280]{1,0:T(8,128)(2,1)S(1)} collective-permute-done((bf16[16,1280]{1,0:T(8,128)(2,1)S(1)}, bf16[16,1280]{1,0:T(8,128)(2,1)S(1)}, u32[]{:S(2)}, u32[]{:S(2)}) %collective-permute-start.1) | collective-permute-done | bytes 40992 | tf_op jit(solution)/shard_map/ppermute | solution.py:24
  42.6 4.2 %collective-permute-done.refs_1_ = bf16[16,1280]{1,0:T(8,128)(2,1)S(1)} collective-permute-done((bf16[16,1280]{1,0:T(8,128)(2,1)S(1)}, bf16[16,1280]{1,0:T(8,128)(2,1)S(1)}, u32[]{:S(2)}, u32[]{:S(2)}) %collective-permute-start) | collective-permute-done | bytes 40992 | tf_op jit(solution)/shard_map/ppermute | solution.py:24
  46.8 15.9 %all_gather.3.a_ref = bf16[256,1280]{1,0:T(8,128)(2,1)S(1)} all-gather(bf16[64,1280]{1,0:T(8,128)(2,1)S(1)} %assemble.1.own_ref), channel_id=1, replica_groups=mesh['xh'=2,'z'=8,'y'=8,'xl'=4,'core'=2] {'xl'}, dimensions={0}, use_global_device_ids=true | all-gather | bytes 819200 | tf_op jit(solution)/shard_map/all_gather | solution.py:210
  62.6 1.9 %collective-permute-start.3 = (bf16[256,1280]{1,0:T(8,128)(2,1)S(1)}, bf16[256,1280]{1,0:T(8,128)(2,1)S(1)}, u32[]{:S(2)}, u32[]{:S(2)}) collective-permute-start(bf16[256,1280]{1,0:T(8,128)(2,1)S(1)} %all_gather.3.a_ref), channel_id=1, source_target_pairs={{1,0},{0,1},{3,2},{2,3},{5,4},{4,5},{7,6},{6,7},{9,8},{8,9},{11,10... | collective-permute-start | bytes 1966088 | tf_op jit(solution)/shard_map/ppermute | solution.py:24
  64.6 2.1 %collective-permute-done.3.b_ref = bf16[256,1280]{1,0:T(8,128)(2,1)S(1)} collective-permute-done((bf16[256,1280]{1,0:T(8,128)(2,1)S(1)}, bf16[256,1280]{1,0:T(8,128)(2,1)S(1)}, u32[]{:S(2)}, u32[]{:S(2)}) %collective-permute-start.3) | collective-permute-done | bytes 655392 | tf_op jit(solution)/shard_map/ppermute | solution.py:24
  66.6 2.0 %image_side.1 = (bf16[128,1152]{1,0:T(8,128)(2,1)S(1)}, f32[32,1152]{1,0:T(8,128)S(1)}, bf16[32,1152]{1,0:T(8,128)(2,1)S(1)}, bf16[8,2,72,128]{3,2,1,0:T(8,128)(2,1)}) custom-call(bf16[256,1280]{1,0:T(8,128)(2,1)S(1)} %all_gather.3.a_ref, bf16[256,1280]{1,0:T(8,128)(2,1)S(1)} %collective-permute-done.3.b_ref, bf16[64,1280]{1,0:T(8,128)(2,1)S(1)} %assemble.1.own_ref, ...), custom_call_target="tpu_custom_call" | custom-call | tf_op jit(solution)/shard_map/image_side/pallas_call | solution.py:167
  68.6 3.4 %all-to-all-start.1 = ((bf16[8,144,128]{2,1,0:T(8,128)(2,1)}), bf16[8,144,128]{2,1,0:T(8,128)(2,1)S(1)}, u32[]{:S(2)}, u32[]{:S(2)}) async-start(bf16[8,144,128]{2,1,0:T(8,128)(2,1)} %bitcast.4), calls=%async_computation.1 | async-start | bytes 589824 | tf_op jit(solution)/shard_map/all_to_all | solution.py:222
  72.1 6.2 %collective-permute-start.4 = (bf16[32,1152]{1,0:T(8,128)(2,1)S(1)}, bf16[32,1152]{1,0:T(8,128)(2,1)S(1)}, u32[]{:S(2)}, u32[]{:S(2)}) collective-permute-start(bf16[32,1152]{1,0:T(8,128)(2,1)S(1)} %get-tuple-element.13), channel_id=1, source_target_pairs={{16,0},{24,8},{32,16},{40,24},{48,32},{56,40},{64,48},{72,56},{80,... | collective-permute-start | bytes 221192 | tf_op jit(solution)/shard_map/ppermute | solution.py:24
  78.3 2.6 %collective-permute-done.4._back.back_ref = bf16[32,1152]{1,0:T(8,128)(2,1)S(1)} collective-permute-done((bf16[32,1152]{1,0:T(8,128)(2,1)S(1)}, bf16[32,1152]{1,0:T(8,128)(2,1)S(1)}, u32[]{:S(2)}, u32[]{:S(2)}) %collective-permute-start.4) | collective-permute-done | bytes 73760 | tf_op jit(solution)/shard_map/ppermute | solution.py:24
  80.9 4.2 %all-to-all-done.1.turned_ref = bf16[8,144,128]{2,1,0:T(8,128)(2,1)S(1)} async-done(((bf16[8,144,128]{2,1,0:T(8,128)(2,1)}), bf16[8,144,128]{2,1,0:T(8,128)(2,1)S(1)}, u32[]{:S(2)}, u32[]{:S(2)}) %all-to-all-start.1) | async-done | bytes 294944 | tf_op jit(solution)/shard_map/all_to_all | solution.py:222
  85.1 0.7 copy-done.8
  85.9 2.9 %head_side.1._parts = bf16[16,54,128]{2,1,0:T(8,128)(2,1)} custom-call(bf16[8,144,128]{2,1,0:T(8,128)(2,1)} %copy-done.8, bf16[8,128,768]{2,1,0:T(8,128)(2,1)} %all-to-all-done.feat_ref, bf16[32,1152]{1,0:T(8,128)(2,1)} %copy-done.3), custom_call_target="tpu_custom_call" | custom-call | tf_op jit(solution)/shard_map/head_side/pallas_call | solution.py:167
  88.8 4.7 %all-to-all-start.2 = ((bf16[16,54,128]{2,1,0:T(8,128)(2,1)}), bf16[16,54,128]{2,1,0:T(8,128)(2,1)S(1)}, u32[]{:S(2)}, u32[]{:S(2)}) async-start(bf16[16,54,128]{2,1,0:T(8,128)(2,1)} %head_side.1._parts), calls=%async_computation.2 | async-start | bytes 458752 | tf_op jit(solution)/shard_map/all_to_all | solution.py:236
  93.5 1.0 copy-done.1
  94.5 0.9 copy-done.4
  95.4 14.8 %collective-permute-start.5 = (bf16[16,1152]{1,0:T(8,128)(2,1)S(1)}, bf16[16,1152]{1,0:T(8,128)(2,1)S(1)}, u32[]{:S(2)}, u32[]{:S(2)}) collective-permute-start(bf16[16,1152]{1,0:T(8,128)(2,1)S(1)} %get-tuple-element.18), channel_id=1, source_target_pairs={{8,0},{16,8},{24,16},{32,24},{40,32},{48,40},{56,48},{64,56},{72,6... | collective-permute-start | bytes 110600 | tf_op jit(solution)/shard_map/ppermute | solution.py:24
  110.2 1.1 convolution_convert_fusion
  111.3 0.5 collective-permute-done.5.last_ref
  111.8 0.8 text_back.1
  112.6 0.0 all-to-all-done.2.parts_ref
  112.6 0.7 head_sum.1
  (14 shorter events, 0.1 us)
Async XLA Ops:
  0.6 109.5 %copy-start = (bf16[1152,768]{1,0:T(8,128)(2,1)S(1)}, bf16[1152,768]{1,0:T(8,128)(2,1)}, u32[]{:S(2)}) copy-start(bf16[1152,768]{1,0:T(8,128)(2,1)} %param.10) | copy-start | bytes 5308420
  4.5 16.9 %copy-start.2 = (bf16[16,1280]{1,0:T(8,128)(2,1)S(1)}, bf16[16,1280]{1,0:T(8,128)(2,1)}, u32[]{:S(2)}) copy-start(bf16[16,1280]{1,0:T(8,128)(2,1)} %prepare.1.refs_0_._payload) | copy-start | bytes 122884
  4.5 62.1 %copy-start.5 = (bf16[128,1152]{1,0:T(8,128)(2,1)S(1)}, bf16[128,1152]{1,0:T(8,128)(2,1)}, u32[]{:S(2)}) copy-start(bf16[128,1152]{1,0:T(8,128)(2,1)} %embed_ref.1) | copy-start | bytes 884740
  4.5 62.1 %copy-start.7 = (s32[128]{0:T(128)S(1)}, s32[128]{0:T(128)}, u32[]{:S(2)}) copy-start(s32[128]{0:T(128)} %param.11) | copy-start | bytes 1540
  4.5 64.1 %all-to-all-start = ((bf16[8,128,768]{2,1,0:T(8,128)(2,1)}), bf16[8,128,768]{2,1,0:T(8,128)(2,1)}, u32[]{:S(2)}, u32[]{:S(2)}) async-start(bf16[8,128,768]{2,1,0:T(8,128)(2,1)} %fan_out.1), calls=%async_computation | async-start | bytes 3145728 | tf_op jit(solution)/shard_map/all_to_all | solution.py:202
  21.3 16.9 %collective-permute-start.2 = (bf16[16,1280]{1,0:T(8,128)(2,1)S(1)}, bf16[16,1280]{1,0:T(8,128)(2,1)S(1)}, u32[]{:S(2)}, u32[]{:S(2)}) collective-permute-start(bf16[16,1280]{1,0:T(8,128)(2,1)S(1)} %copy-done.2), channel_id=1, source_target_pairs={{1000,0},{1008,8},{1016,16},{0,24},{8,32},{16,40},{24,48},{32,56},... | collective-permute-start | bytes 122888 | tf_op jit(solution)/shard_map/ppermute | solution.py:24
  27.2 15.4 %collective-permute-start.1 = (bf16[16,1280]{1,0:T(8,128)(2,1)S(1)}, bf16[16,1280]{1,0:T(8,128)(2,1)S(1)}, u32[]{:S(2)}, u32[]{:S(2)}) collective-permute-start(bf16[16,1280]{1,0:T(8,128)(2,1)S(1)} %copy-done.2), channel_id=1, source_target_pairs={{1008,0},{1016,8},{0,16},{8,24},{16,32},{24,40},{32,48},{40,56},{4... | collective-permute-start | bytes 122888 | tf_op jit(solution)/shard_map/ppermute | solution.py:24
  32.2 14.5 %collective-permute-start = (bf16[16,1280]{1,0:T(8,128)(2,1)S(1)}, bf16[16,1280]{1,0:T(8,128)(2,1)S(1)}, u32[]{:S(2)}, u32[]{:S(2)}) collective-permute-start(bf16[16,1280]{1,0:T(8,128)(2,1)S(1)} %copy-done.2), channel_id=1, source_target_pairs={{1016,0},{0,8},{8,16},{16,24},{24,32},{32,40},{40,48},{48,56},{56,... | collective-permute-start | bytes 122888 | tf_op jit(solution)/shard_map/ppermute | solution.py:24
  62.6 4.0 %collective-permute-start.3 = (bf16[256,1280]{1,0:T(8,128)(2,1)S(1)}, bf16[256,1280]{1,0:T(8,128)(2,1)S(1)}, u32[]{:S(2)}, u32[]{:S(2)}) collective-permute-start(bf16[256,1280]{1,0:T(8,128)(2,1)S(1)} %all_gather.3.a_ref), channel_id=1, source_target_pairs={{1,0},{0,1},{3,2},{2,3},{5,4},{4,5},{7,6},{6,7},{9,8},{8,9},{11,10... | collective-permute-start | bytes 1966088 | tf_op jit(solution)/shard_map/ppermute | solution.py:24
  68.6 16.5 %all-to-all-start.1 = ((bf16[8,144,128]{2,1,0:T(8,128)(2,1)}), bf16[8,144,128]{2,1,0:T(8,128)(2,1)S(1)}, u32[]{:S(2)}, u32[]{:S(2)}) async-start(bf16[8,144,128]{2,1,0:T(8,128)(2,1)} %bitcast.4), calls=%async_computation.1 | async-start | bytes 589824 | tf_op jit(solution)/shard_map/all_to_all | solution.py:222
  72.1 8.9 %collective-permute-start.4 = (bf16[32,1152]{1,0:T(8,128)(2,1)S(1)}, bf16[32,1152]{1,0:T(8,128)(2,1)S(1)}, u32[]{:S(2)}, u32[]{:S(2)}) collective-permute-start(bf16[32,1152]{1,0:T(8,128)(2,1)S(1)} %get-tuple-element.13), channel_id=1, source_target_pairs={{16,0},{24,8},{32,16},{40,24},{48,32},{56,40},{64,48},{72,56},{80,... | collective-permute-start | bytes 221192 | tf_op jit(solution)/shard_map/ppermute | solution.py:24
  80.9 4.2 %copy-start.3 = (bf16[32,1152]{1,0:T(8,128)(2,1)}, bf16[32,1152]{1,0:T(8,128)(2,1)S(1)}, u32[]{:S(2)}) copy-start(bf16[32,1152]{1,0:T(8,128)(2,1)S(1)} %collective-permute-done.4._back.back_ref) | copy-start | bytes 221188
  85.1 0.7 copy-start.8
  88.8 23.0 %copy-start.6 = (bf16[16,1152]{1,0:T(8,128)(2,1)S(1)}, bf16[16,1152]{1,0:T(8,128)(2,1)}, u32[]{:S(2)}) copy-start(bf16[16,1152]{1,0:T(8,128)(2,1)} %text_ref.1) | copy-start | bytes 110596
  88.8 23.8 %all-to-all-start.2 = ((bf16[16,54,128]{2,1,0:T(8,128)(2,1)}), bf16[16,54,128]{2,1,0:T(8,128)(2,1)S(1)}, u32[]{:S(2)}, u32[]{:S(2)}) async-start(bf16[16,54,128]{2,1,0:T(8,128)(2,1)} %head_side.1._parts), calls=%async_computation.2 | async-start | bytes 458752 | tf_op jit(solution)/shard_map/all_to_all | solution.py:236
  93.5 1.0 copy-start.1
  94.5 0.9 copy-start.4
  95.4 16.4 %collective-permute-start.5 = (bf16[16,1152]{1,0:T(8,128)(2,1)S(1)}, bf16[16,1152]{1,0:T(8,128)(2,1)S(1)}, u32[]{:S(2)}, u32[]{:S(2)}) collective-permute-start(bf16[16,1152]{1,0:T(8,128)(2,1)S(1)} %get-tuple-element.18), channel_id=1, source_target_pairs={{8,0},{16,8},{24,16},{32,24},{40,32},{48,40},{56,48},{64,56},{72,6... | collective-permute-start | bytes 110600 | tf_op jit(solution)/shard_map/ppermute | solution.py:24

commit v8 on v7

--- a/solution.py
+++ b/solution.py
@@ -94,7 +94,7 @@
     return (-signs * jax.nn.sigmoid(-signs * logits)).astype(bf16)
 
 
-def image_side(a_ref, b_ref, own_ref, embed_ref, ids_ref, grad_ref, kept_ref, far_ref, turned_ref):
+def image_side(a_ref, b_ref, own_ref, embed_ref, ids_ref, grad_ref, turned_ref, *share_refs):
     floats = embed_ref[...].astype(f32)
     norms = norms_of(floats)
     units = floats / norms
@@ -116,19 +116,12 @@
             turned_ref[z, p] = turned[start : start + run]
     slope = slopes(own_ref[...], rounded, ids_ref[...])
     share = SCALE * jnp.dot(slope, rounded, preferred_element_type=f32)
-    half = kept_ref.shape[0]
-    kept_ref[...] = share[:half]
-    far_ref[...] = share[half:].astype(bf16)
-
-
-def text_middle(kept_ref, back_ref, _parts, stay_ref, pass_ref):
-    count = stay_ref.shape[0]
-    total = kept_ref[...] + back_ref[...].astype(f32)
-    stay_ref[...] = total[:count]
-    pass_ref[...] = total[count:].astype(bf16)
-
-
-def head_side(turned_ref, feat_ref, _back, out_ref):
+    count = share_refs[0].shape[0]
+    for k, ref in enumerate(share_refs):
+        ref[...] = share[k * count : (k + 1) * count].astype(ref.dtype)
+
+
+def head_side(feat_ref, turned_ref, out_ref):
     part = jnp.zeros((turned_ref.shape[1], feat_ref.shape[2]), f32)
     for k in range(turned_ref.shape[0]):
         part = part + jnp.dot(turned_ref[k], feat_ref[k], preferred_element_type=f32)
@@ -148,11 +141,14 @@
         out_ref[:, g * 128 : (g + 1) * 128] = total[g * run : (g + 1) * run]
 
 
-def text_back(stay_ref, last_ref, text_ref, out_ref):
+def finish(grad_ref, head_ref, text_ref, kept_ref, one_ref, two_ref, three_ref, image_ref, out_ref):
+    image_ref[...] = jnp.dot(grad_ref[...], head_ref[...], preferred_element_type=f32).astype(bf16)
     floats = text_ref[...].astype(f32)
     norms = norms_of(floats)
     units = floats / norms
-    total = stay_ref[...] + last_ref[...].astype(f32)
+    total = kept_ref[...]
+    for ref in (one_ref, two_ref, three_ref):
+        total = total + ref[...].astype(f32)
     out_ref[...] = (total - units * jnp.sum(units * total, -1, keepdims=True)) / norms
 
 
@@ -212,31 +208,25 @@
 
     pieces = lax.axis_size("xh")
     run = width // (planes * pieces)
-    embed_grad, kept, far, turned = call(
+    embed_grad, turned, kept, *aways = call(
         image_side,
-        [((images, width), bf16), ((2 * texts, width), f32), ((2 * texts, width), bf16),
-         ((planes, pieces, run, images), bf16)],
+        [((images, width), bf16), ((planes, pieces, run, images), bf16), ((texts, width), f32)]
+        + [((texts, width), bf16)] * 3,
         here, there, own, image_embed, ids, room=ROOM,
     )
     turned, feats = lax.optimization_barrier((turned, feats))
     plane = lax.all_to_all(turned.reshape(planes, own_width, images), "z", 0, 0, tiled=True)
 
-    back = shifted(far, BLK, -2)
+    backs = [shifted(away, BLK, -d) for d, away in zip((1, 2, 3), aways)]
 
     rows = own_width // across
     parts = call(
-        head_side, [((across, rows * features // 128, 128), bf16)],
-        plane, feats, back, after=1,
-    )
-    stay, passed = call(
-        text_middle, [((texts, width), f32), ((texts, width), bf16)],
-        kept, back, parts, after=1, room=ROOM,
-    )
-    last = shifted(passed, BLK, -1)
+        head_side, [((across, rows * features // 128, 128), bf16)], feats, plane, room=ROOM,
+    )
     parts = lax.all_to_all(parts, ("xh", "y"), 0, 0, tiled=True)
-    image_grad = jnp.dot(embed_grad, head, preferred_element_type=f32).astype(bf16)
-    text_grad = call(
-        text_back, [((texts, width), f32)], stay, last, text_embed, cost=lasting(1), room=ROOM
+    image_grad, text_grad = call(
+        finish, [((images, features), bf16), ((texts, width), f32)],
+        embed_grad, head, text_embed, kept, *backs, cost=lasting(60), room=ROOM,
     )
     head_grad = call(head_sum, [((rows, features), f32)], parts, room=ROOM)
     return (image_grad, text_grad, head_grad)

time: 114 us -> 108 us (0.947)
  the two profiles are of different devices: /device:TPU:2 before, /device:TPU:16 now
where the time goes in v8:
time: 108 us; the launch traced here: 107 us
  starting transfers between devices  57.4 us (53%)
  waiting for transfers between devices  21.1 us (20%)
  blocking collectives  17.6 us (16%)
  Pallas kernels  8.9 us (8%)
  local copies, waits for them, and re-layouts  1.49 us (1%)
    ppermute x7, starting transfers between devices, shifted(): lax.ppermute(block, axis, [((i - distance) % size, i) for i in range(size)])  28.8 us
    all_gather x1, blocking collectives, local(): here = lax.all_gather(own, 'xl', axis=0, tiled=True)  17.6 us
    all_to_all x1, starting transfers between devices, local(): feats = lax.all_to_all(feats, 'z', 0, 0, tiled=True)  16.8 us
    ppermute x7, waiting for transfers between devices, shifted(): lax.ppermute(block, axis, [((i - distance) % size, i) for i in range(size)])  11.7 us
    all_to_all x1, waiting for transfers between devices, local(): parts = lax.all_to_all(parts, ('xh', 'y'), 0, 0, tiled=True)  9.41 us
    pallas_call x7, Pallas kernels, call(): pl.pallas_call(kernel, out_shape=outs[0] if single else outs, in_specs=sp...  8.9 us
    all_to_all x1, starting transfers between devices, local(): parts = lax.all_to_all(parts, ('xh', 'y'), 0, 0, tiled=True)  8.15 us
    all_to_all x1, starting transfers between devices, local(): lax.all_to_all(turned.reshape(planes, own_width, images), 'z', 0, 0, tile...  3.55 us
  transfers between devices with their start and end apart: 10, of which 4 were waited for; matrix products, arithmetic and copies ran while one was open for 0% of the time, Pallas kernels for 4%

profile of v8, /device:TPU:16, one launch (start us, length us, event | category | flops | bytes accessed | tf_op | source)
XLA Modules:
  0.0 107.2 jit_solution(16125483645903900335)
XLA Ops:
  0.6 1.6 %prepare.1.refs_0_._payload = bf16[16,1280]{1,0:T(8,128)(2,1)} custom-call(s32[1]{0:T(128)} %bitcast.pos_ref, bf16[16,1152]{1,0:T(8,128)(2,1)} %text_ref.1, s32[1,128]{1,0:T(1,128)} %bitcast.5, s32[1,128]{1,0:T(1,128)} %bitcast.7, f32[1,8]{1,0:T(1,128)} %bitcast.8), custom_call_target="tpu_custom_call" | custom-call | tf_op jit(solution)/shard_map/prepare/pallas_call | solution.py:163
  2.2 2.1 %fan_out.1 = bf16[8,128,768]{2,1,0:T(8,128)(2,1)} custom-call(bf16[128,768]{1,0:T(8,128)(2,1)} %feat_ref.1, bf16[16,1280]{1,0:T(8,128)(2,1)} %prepare.1.refs_0_._payload), custom_call_target="tpu_custom_call" | custom-call | tf_op jit(solution)/shard_map/fan_out/pallas_call | solution.py:163
  4.4 0.0 copy-start
  4.4 0.0 copy-start.1
  4.4 0.0 copy-start.3
  4.4 16.8 %all-to-all-start = ((bf16[8,128,768]{2,1,0:T(8,128)(2,1)}), bf16[8,128,768]{2,1,0:T(8,128)(2,1)S(1)}, u32[]{:S(2)}, u32[]{:S(2)}) async-start(bf16[8,128,768]{2,1,0:T(8,128)(2,1)} %fan_out.1), calls=%async_computation | async-start | bytes 3145728 | tf_op jit(solution)/shard_map/all_to_all | solution.py:198
  21.2 7.1 %collective-permute-start.2 = (bf16[16,1280]{1,0:T(8,128)(2,1)S(1)}, bf16[16,1280]{1,0:T(8,128)(2,1)S(1)}, u32[]{:S(2)}, u32[]{:S(2)}) collective-permute-start(bf16[16,1280]{1,0:T(8,128)(2,1)S(1)} %copy-done), channel_id=1, source_target_pairs={{1000,0},{1008,8},{1016,16},{0,24},{8,32},{16,40},{24,48},{32,56},... | collective-permute-start | bytes 122888 | tf_op jit(solution)/shard_map/ppermute | solution.py:24
  28.3 2.9 %collective-permute-start.1 = (bf16[16,1280]{1,0:T(8,128)(2,1)S(1)}, bf16[16,1280]{1,0:T(8,128)(2,1)S(1)}, u32[]{:S(2)}, u32[]{:S(2)}) collective-permute-start(bf16[16,1280]{1,0:T(8,128)(2,1)S(1)} %copy-done), channel_id=1, source_target_pairs={{1008,0},{1016,8},{0,16},{8,24},{16,32},{24,40},{32,48},{40,56},{4... | collective-permute-start | bytes 122888 | tf_op jit(solution)/shard_map/ppermute | solution.py:24
  31.2 2.7 %collective-permute-start = (bf16[16,1280]{1,0:T(8,128)(2,1)S(1)}, bf16[16,1280]{1,0:T(8,128)(2,1)S(1)}, u32[]{:S(2)}, u32[]{:S(2)}) collective-permute-start(bf16[16,1280]{1,0:T(8,128)(2,1)S(1)} %copy-done), channel_id=1, source_target_pairs={{1016,0},{0,8},{8,16},{16,24},{24,32},{32,40},{40,48},{48,56},{56,... | collective-permute-start | bytes 122888 | tf_op jit(solution)/shard_map/ppermute | solution.py:24
  33.9 3.9 %collective-permute-done.2.refs_3_ = bf16[16,1280]{1,0:T(8,128)(2,1)S(1)} collective-permute-done((bf16[16,1280]{1,0:T(8,128)(2,1)S(1)}, bf16[16,1280]{1,0:T(8,128)(2,1)S(1)}, u32[]{:S(2)}, u32[]{:S(2)}) %collective-permute-start.2) | collective-permute-done | bytes 40992 | tf_op jit(solution)/shard_map/ppermute | solution.py:24
  37.8 5.8 %collective-permute-done.1.refs_2_ = bf16[16,1280]{1,0:T(8,128)(2,1)S(1)} collective-permute-done((bf16[16,1280]{1,0:T(8,128)(2,1)S(1)}, bf16[16,1280]{1,0:T(8,128)(2,1)S(1)}, u32[]{:S(2)}, u32[]{:S(2)}) %collective-permute-start.1) | collective-permute-done | bytes 40992 | tf_op jit(solution)/shard_map/ppermute | solution.py:24
  43.6 0.0 collective-permute-done.refs_1_
  43.6 17.6 %all_gather.3.a_ref = bf16[256,1280]{1,0:T(8,128)(2,1)S(1)} all-gather(bf16[64,1280]{1,0:T(8,128)(2,1)S(1)} %assemble.1.own_ref), channel_id=1, replica_groups=mesh['xh'=2,'z'=8,'y'=8,'xl'=4,'core'=2] {'xl'}, dimensions={0}, use_global_device_ids=true | all-gather | bytes 819200 | tf_op jit(solution)/shard_map/all_gather | solution.py:206
  61.2 1.9 %collective-permute-start.3 = (bf16[256,1280]{1,0:T(8,128)(2,1)S(1)}, bf16[256,1280]{1,0:T(8,128)(2,1)S(1)}, u32[]{:S(2)}, u32[]{:S(2)}) collective-permute-start(bf16[256,1280]{1,0:T(8,128)(2,1)S(1)} %all_gather.3.a_ref), channel_id=1, source_target_pairs={{1,0},{0,1},{3,2},{2,3},{5,4},{4,5},{7,6},{6,7},{9,8},{8,9},{11,10... | collective-permute-start | bytes 1966088 | tf_op jit(solution)/shard_map/ppermute | solution.py:24
  63.1 2.1 %collective-permute-done.3.b_ref = bf16[256,1280]{1,0:T(8,128)(2,1)S(1)} collective-permute-done((bf16[256,1280]{1,0:T(8,128)(2,1)S(1)}, bf16[256,1280]{1,0:T(8,128)(2,1)S(1)}, u32[]{:S(2)}, u32[]{:S(2)}) %collective-permute-start.3) | collective-permute-done | bytes 655392 | tf_op jit(solution)/shard_map/ppermute | solution.py:24
  65.1 2.0 %image_side.1 = (bf16[128,1152]{1,0:T(8,128)(2,1)S(1)}, bf16[8,2,72,128]{3,2,1,0:T(8,128)(2,1)}, f32[16,1152]{1,0:T(8,128)S(1)}, bf16[16,1152]{1,0:T(8,128)(2,1)...) custom-call(bf16[256,1280]{1,0:T(8,128)(2,1)S(1)} %all_gather.3.a_ref, ...), custom_call_target="tpu_custom_call" | custom-call | tf_op jit(solution)/shard_map/image_side/pallas_call | solution.py:163
  67.1 0.0 all-to-all-done.feat_ref
  67.1 3.6 %all-to-all-start.1 = ((bf16[8,144,128]{2,1,0:T(8,128)(2,1)}), bf16[8,144,128]{2,1,0:T(8,128)(2,1)S(1)}, u32[]{:S(2)}, u32[]{:S(2)}) async-start(bf16[8,144,128]{2,1,0:T(8,128)(2,1)} %bitcast.4), calls=%async_computation.1 | async-start | bytes 589824 | tf_op jit(solution)/shard_map/all_to_all | solution.py:218
  70.7 4.4 %collective-permute-start.4 = (bf16[16,1152]{1,0:T(8,128)(2,1)S(1)}, bf16[16,1152]{1,0:T(8,128)(2,1)S(1)}, u32[]{:S(2)}, u32[]{:S(2)}) collective-permute-start(bf16[16,1152]{1,0:T(8,128)(2,1)S(1)} %get-tuple-element.15), channel_id=1, source_target_pairs={{8,0},{16,8},{24,16},{32,24},{40,32},{48,40},{56,48},{64,56},{72,6... | collective-permute-start | bytes 110600 | tf_op jit(solution)/shard_map/ppermute | solution.py:24
  75.1 6.3 %collective-permute-start.5 = (bf16[16,1152]{1,0:T(8,128)(2,1)S(1)}, bf16[16,1152]{1,0:T(8,128)(2,1)S(1)}, u32[]{:S(2)}, u32[]{:S(2)}) collective-permute-start(bf16[16,1152]{1,0:T(8,128)(2,1)S(1)} %get-tuple-element.16), channel_id=1, source_target_pairs={{16,0},{24,8},{32,16},{40,24},{48,32},{56,40},{64,48},{72,56},{80,... | collective-permute-start | bytes 110600 | tf_op jit(solution)/shard_map/ppermute | solution.py:24
  81.4 3.6 %collective-permute-start.6 = (bf16[16,1152]{1,0:T(8,128)(2,1)S(1)}, bf16[16,1152]{1,0:T(8,128)(2,1)S(1)}, u32[]{:S(2)}, u32[]{:S(2)}) collective-permute-start(bf16[16,1152]{1,0:T(8,128)(2,1)S(1)} %get-tuple-element.17), channel_id=1, source_target_pairs={{24,0},{32,8},{40,16},{48,24},{56,32},{64,40},{72,48},{80,56},{88,... | collective-permute-start | bytes 110600 | tf_op jit(solution)/shard_map/ppermute | solution.py:24
  85.0 0.0 all-to-all-done.1.turned_ref
  85.0 1.4 %head_side.1 = bf16[16,54,128]{2,1,0:T(8,128)(2,1)} custom-call(bf16[8,128,768]{2,1,0:T(8,128)(2,1)S(1)} %all-to-all-done.feat_ref, bf16[8,144,128]{2,1,0:T(8,128)(2,1)S(1)} %all-to-all-done.1.turned_ref), custom_call_target="tpu_custom_call" | custom-call | tf_op jit(solution)/shard_map/head_side/pallas_call | solution.py:163
  86.4 8.1 %all-to-all-start.2 = ((bf16[16,54,128]{2,1,0:T(8,128)(2,1)}), bf16[16,54,128]{2,1,0:T(8,128)(2,1)S(1)}, u32[]{:S(2)}, u32[]{:S(2)}) async-start(bf16[16,54,128]{2,1,0:T(8,128)(2,1)} %head_side.1), calls=%async_computation.2 | async-start | bytes 458752 | tf_op jit(solution)/shard_map/all_to_all | solution.py:226
  94.5 0.0 collective-permute-done.4.one_ref
  94.5 0.0 collective-permute-done.5.two_ref
  94.6 0.0 collective-permute-done.6.three_ref
  94.6 0.0 copy-start.4
  94.6 1.5 %copy-done.4 = bf16[1152,768]{1,0:T(8,128)(2,1)S(1)} copy-done((bf16[1152,768]{1,0:T(8,128)(2,1)S(1)}, bf16[1152,768]{1,0:T(8,128)(2,1)}, u32[]{:S(2)}) %copy-start.4) | copy-done | bytes 1769496
  96.1 1.1 %finish.1 = (bf16[128,768]{1,0:T(8,128)(2,1)}, f32[16,1152]{1,0:T(8,128)}) custom-call(bf16[128,1152]{1,0:T(8,128)(2,1)S(1)} %get-tuple-element.13.grad_ref, bf16[1152,768]{1,0:T(8,128)(2,1)S(1)} %copy-done.4, bf16[16,1152]{1,0:T(8,128)(2,1)S(1)} %copy-done.2, f32[16,1152]{1,0:T(8,128)S(1)} %get-tuple-element.14.kept_ref, ...), custom_call_target="tpu_custom_call" | custom-call | flops 60000002048 | tf_op jit(solution)/shard_map/finish/pallas_call | solution.py:163
  97.2 9.4 %all-to-all-done.2.parts_ref = bf16[16,54,128]{2,1,0:T(8,128)(2,1)S(1)} async-done(((bf16[16,54,128]{2,1,0:T(8,128)(2,1)}), bf16[16,54,128]{2,1,0:T(8,128)(2,1)S(1)}, u32[]{:S(2)}, u32[]{:S(2)}) %all-to-all-start.2) | async-done | bytes 221216 | tf_op jit(solution)/shard_map/all_to_all | solution.py:226
  106.6 0.7 head_sum.1
  (6 shorter events, 0.0 us)
Async XLA Ops:
  4.4 16.9 %copy-start = (bf16[16,1280]{1,0:T(8,128)(2,1)S(1)}, bf16[16,1280]{1,0:T(8,128)(2,1)}, u32[]{:S(2)}) copy-start(bf16[16,1280]{1,0:T(8,128)(2,1)} %prepare.1.refs_0_._payload) | copy-start | bytes 122884
  4.4 60.8 %copy-start.1 = (bf16[128,1152]{1,0:T(8,128)(2,1)S(1)}, bf16[128,1152]{1,0:T(8,128)(2,1)}, u32[]{:S(2)}) copy-start(bf16[128,1152]{1,0:T(8,128)(2,1)} %embed_ref.1) | copy-start | bytes 884740
  4.4 60.8 %copy-start.3 = (s32[128]{0:T(128)S(1)}, s32[128]{0:T(128)}, u32[]{:S(2)}) copy-start(s32[128]{0:T(128)} %param.11) | copy-start | bytes 1540
  4.4 62.7 %all-to-all-start = ((bf16[8,128,768]{2,1,0:T(8,128)(2,1)}), bf16[8,128,768]{2,1,0:T(8,128)(2,1)S(1)}, u32[]{:S(2)}, u32[]{:S(2)}) async-start(bf16[8,128,768]{2,1,0:T(8,128)(2,1)} %fan_out.1), calls=%async_computation | async-start | bytes 3145728 | tf_op jit(solution)/shard_map/all_to_all | solution.py:198
  21.2 16.6 %collective-permute-start.2 = (bf16[16,1280]{1,0:T(8,128)(2,1)S(1)}, bf16[16,1280]{1,0:T(8,128)(2,1)S(1)}, u32[]{:S(2)}, u32[]{:S(2)}) collective-permute-start(bf16[16,1280]{1,0:T(8,128)(2,1)S(1)} %copy-done), channel_id=1, source_target_pairs={{1000,0},{1008,8},{1016,16},{0,24},{8,32},{16,40},{24,48},{32,56},... | collective-permute-start | bytes 122888 | tf_op jit(solution)/shard_map/ppermute | solution.py:24
  28.3 15.3 %collective-permute-start.1 = (bf16[16,1280]{1,0:T(8,128)(2,1)S(1)}, bf16[16,1280]{1,0:T(8,128)(2,1)S(1)}, u32[]{:S(2)}, u32[]{:S(2)}) collective-permute-start(bf16[16,1280]{1,0:T(8,128)(2,1)S(1)} %copy-done), channel_id=1, source_target_pairs={{1008,0},{1016,8},{0,16},{8,24},{16,32},{24,40},{32,48},{40,56},{4... | collective-permute-start | bytes 122888 | tf_op jit(solution)/shard_map/ppermute | solution.py:24
  31.2 12.4 %collective-permute-start = (bf16[16,1280]{1,0:T(8,128)(2,1)S(1)}, bf16[16,1280]{1,0:T(8,128)(2,1)S(1)}, u32[]{:S(2)}, u32[]{:S(2)}) collective-permute-start(bf16[16,1280]{1,0:T(8,128)(2,1)S(1)} %copy-done), channel_id=1, source_target_pairs={{1016,0},{0,8},{8,16},{16,24},{24,32},{32,40},{40,48},{48,56},{56,... | collective-permute-start | bytes 122888 | tf_op jit(solution)/shard_map/ppermute | solution.py:24
  61.2 4.0 %collective-permute-start.3 = (bf16[256,1280]{1,0:T(8,128)(2,1)S(1)}, bf16[256,1280]{1,0:T(8,128)(2,1)S(1)}, u32[]{:S(2)}, u32[]{:S(2)}) collective-permute-start(bf16[256,1280]{1,0:T(8,128)(2,1)S(1)} %all_gather.3.a_ref), channel_id=1, source_target_pairs={{1,0},{0,1},{3,2},{2,3},{5,4},{4,5},{7,6},{6,7},{9,8},{8,9},{11,10... | collective-permute-start | bytes 1966088 | tf_op jit(solution)/shard_map/ppermute | solution.py:24
  67.1 27.4 %copy-start.2 = (bf16[16,1152]{1,0:T(8,128)(2,1)S(1)}, bf16[16,1152]{1,0:T(8,128)(2,1)}, u32[]{:S(2)}) copy-start(bf16[16,1152]{1,0:T(8,128)(2,1)} %text_ref.1) | copy-start | bytes 110596
  67.1 17.8 %all-to-all-start.1 = ((bf16[8,144,128]{2,1,0:T(8,128)(2,1)}), bf16[8,144,128]{2,1,0:T(8,128)(2,1)S(1)}, u32[]{:S(2)}, u32[]{:S(2)}) async-start(bf16[8,144,128]{2,1,0:T(8,128)(2,1)} %bitcast.4), calls=%async_computation.1 | async-start | bytes 589824 | tf_op jit(solution)/shard_map/all_to_all | solution.py:218
  70.7 23.8 %collective-permute-start.4 = (bf16[16,1152]{1,0:T(8,128)(2,1)S(1)}, bf16[16,1152]{1,0:T(8,128)(2,1)S(1)}, u32[]{:S(2)}, u32[]{:S(2)}) collective-permute-start(bf16[16,1152]{1,0:T(8,128)(2,1)S(1)} %get-tuple-element.15), channel_id=1, source_target_pairs={{8,0},{16,8},{24,16},{32,24},{40,32},{48,40},{56,48},{64,56},{72,6... | collective-permute-start | bytes 110600 | tf_op jit(solution)/shard_map/ppermute | solution.py:24
  75.1 19.4 %collective-permute-start.5 = (bf16[16,1152]{1,0:T(8,128)(2,1)S(1)}, bf16[16,1152]{1,0:T(8,128)(2,1)S(1)}, u32[]{:S(2)}, u32[]{:S(2)}) collective-permute-start(bf16[16,1152]{1,0:T(8,128)(2,1)S(1)} %get-tuple-element.16), channel_id=1, source_target_pairs={{16,0},{24,8},{32,16},{40,24},{48,32},{56,40},{64,48},{72,56},{80,... | collective-permute-start | bytes 110600 | tf_op jit(solution)/shard_map/ppermute | solution.py:24
  81.4 13.2 %collective-permute-start.6 = (bf16[16,1152]{1,0:T(8,128)(2,1)S(1)}, bf16[16,1152]{1,0:T(8,128)(2,1)S(1)}, u32[]{:S(2)}, u32[]{:S(2)}) collective-permute-start(bf16[16,1152]{1,0:T(8,128)(2,1)S(1)} %get-tuple-element.17), channel_id=1, source_target_pairs={{24,0},{32,8},{40,16},{48,24},{56,32},{64,40},{72,48},{80,56},{88,... | collective-permute-start | bytes 110600 | tf_op jit(solution)/shard_map/ppermute | solution.py:24
  86.4 20.2 %all-to-all-start.2 = ((bf16[16,54,128]{2,1,0:T(8,128)(2,1)}), bf16[16,54,128]{2,1,0:T(8,128)(2,1)S(1)}, u32[]{:S(2)}, u32[]{:S(2)}) async-start(bf16[16,54,128]{2,1,0:T(8,128)(2,1)} %head_side.1), calls=%async_computation.2 | async-start | bytes 458752 | tf_op jit(solution)/shard_map/all_to_all | solution.py:226
  94.6 1.5 %copy-start.4 = (bf16[1152,768]{1,0:T(8,128)(2,1)S(1)}, bf16[1152,768]{1,0:T(8,128)(2,1)}, u32[]{:S(2)}) copy-start(bf16[1152,768]{1,0:T(8,128)(2,1)} %head_ref.1) | copy-start | bytes 5308420

commit v9 on v8

--- a/solution.py
+++ b/solution.py
@@ -36,12 +36,17 @@
     return lax.broadcasted_iota(i32, shape, dim)
 
 
-def prepare(pos_ref, text_hbm, ids_hbm, domain_hbm, bias_hbm, out_ref, text_ref, ids_ref, domain_ref, bias_ref, sems):
-    pairs = ((text_hbm, text_ref), (ids_hbm, ids_ref), (domain_hbm, domain_ref), (bias_hbm, bias_ref))
-    copies = [pltpu.make_async_copy(src, dst, sems.at[k]) for k, (src, dst) in enumerate(pairs)]
+def prepare(pos_ref, *refs):
+    sources, (out_ref, feats_hbm), held, sems, sem = refs[:5], refs[5:7], refs[7:12], refs[12], refs[13]
+    copies = [pltpu.make_async_copy(src, dst, sems.at[k]) for k, (src, dst) in enumerate(zip(sources, held))]
     for copy in copies:
         copy.start()
-    for copy in copies:
+    text_ref, ids_ref, domain_ref, bias_ref, feat_ref = held
+    fans = [pltpu.make_async_copy(feat_ref, feats_hbm.at[k], sem.at[k]) for k in range(feats_hbm.shape[0])]
+    copies[4].wait()
+    for fan in fans:
+        fan.start()
+    for copy in copies[:4]:
         copy.wait()
     rows, width = text_ref.shape
     floats = text_ref[...].astype(f32)
@@ -64,14 +69,8 @@
     for k, part in enumerate((high, low, first, second, third)):
         tail = jnp.where(lane == k, part, tail)
     out_ref[:, width:] = tail.astype(bf16)
-
-
-def fan_out(feat_ref, _payload, feats_hbm, sem):
-    copies = [pltpu.make_async_copy(feat_ref, feats_hbm.at[k], sem) for k in range(feats_hbm.shape[0])]
-    for copy in copies:
-        copy.start()
-    for copy in copies:
-        copy.wait()
+    for fan in fans:
+        fan.wait()
 
 
 def assemble(*refs):
@@ -186,14 +185,12 @@
     across = lax.axis_size("xh") * lax.axis_size("y")
     own_width = width // planes
 
-    inputs = (text_embed, ids, domain.reshape(1, images), domain_bias.reshape(1, -1))
-    payload = call(
-        prepare, [((texts, width + TAIL), bf16)], position, *inputs, smem=1, hbm=4,
-        scratch=[pltpu.VMEM(v.shape, v.dtype) for v in inputs] + [pltpu.SemaphoreType.DMA((4,))],
-    )
-    feats = call(
-        fan_out, [((planes, images, features), bf16)], image_feat, payload,
-        after=1, out_hbm=1, scratch=[pltpu.SemaphoreType.DMA],
+    inputs = (text_embed, ids, domain.reshape(1, images), domain_bias.reshape(1, -1), image_feat)
+    payload, feats = call(
+        prepare, [((texts, width + TAIL), bf16), ((planes, images, features), bf16)],
+        position, *inputs, smem=1, hbm=5, out_hbm=1,
+        scratch=[pltpu.VMEM(v.shape, v.dtype) for v in inputs]
+        + [pltpu.SemaphoreType.DMA((5,)), pltpu.SemaphoreType.DMA((planes,))],
     )
     feats = lax.all_to_all(feats, "z", 0, 0, tiled=True)
 

time: 108 us -> 107 us (level)
    pallas_call x7 -> x6, Pallas kernels: 8.9 us -> 8.12 us  [call(): pl.pallas_call(kernel, out_shape=outs[0] if single else outs, in_specs=sp...]
where the time goes in v9:
time: 107 us; the launch traced here: 106 us
  starting transfers between devices  57.4 us (54%)
  waiting for transfers between devices  21.1 us (20%)
  blocking collectives  17.6 us (16%)
  Pallas kernels  8.12 us (8%)
  local copies, waits for them, and re-layouts  1.49 us (1%)
    ppermute x7, starting transfers between devices, shifted(): lax.ppermute(block, axis, [((i - distance) % size, i) for i in range(size)])  28.8 us
    all_gather x1, blocking collectives, local(): here = lax.all_gather(own, 'xl', axis=0, tiled=True)  17.6 us
    all_to_all x1, starting transfers between devices, local(): feats = lax.all_to_all(feats, 'z', 0, 0, tiled=True)  16.8 us
    ppermute x7, waiting for transfers between devices, shifted(): lax.ppermute(block, axis, [((i - distance) % size, i) for i in range(size)])  11.7 us
    all_to_all x1, waiting for transfers between devices, local(): parts = lax.all_to_all(parts, ('xh', 'y'), 0, 0, tiled=True)  9.41 us
    all_to_all x1, starting transfers between devices, local(): parts = lax.all_to_all(parts, ('xh', 'y'), 0, 0, tiled=True)  8.17 us
    pallas_call x6, Pallas kernels, call(): pl.pallas_call(kernel, out_shape=outs[0] if single else outs, in_specs=sp...  8.12 us
    all_to_all x1, starting transfers between devices, local(): lax.all_to_all(turned.reshape(planes, own_width, images), 'z', 0, 0, tile...  3.55 us
  transfers between devices with their start and end apart: 10, of which 4 were waited for; matrix products, arithmetic and copies ran while one was open for 0% of the time, Pallas kernels for 4%

profile of v9, /device:TPU:16, one launch (start us, length us, event | category | flops | bytes accessed | tf_op | source)
XLA Modules:
  0.0 106.5 jit_solution(11102412729578499050)
XLA Ops:
  0.6 2.9 %prepare.1 = (bf16[16,1280]{1,0:T(8,128)(2,1)}, bf16[8,128,768]{2,1,0:T(8,128)(2,1)}) custom-call(s32[1]{0:T(128)} %bitcast.pos_ref, bf16[16,1152]{1,0:T(8,128)(2,1)} %text_ref.1, s32[1,128]{1,0:T(1,128)} %bitcast.5, s32[1,128]{1,0:T(1,128)} %bitcast.7, f32[1,8]{1,0:T(1,128)} %bitcast.8, bf16[128,768]{1,0:T(8,128)(2,1)} %refs_4_.1), custom_call_target="tpu_custom_call" | custom-call | tf_op jit(solution)/shard_map/prepare/pallas_call | solution.py:162
  3.5 0.0 copy-start.1
  3.6 0.0 copy-start
  3.6 0.0 copy-start.3
  3.6 16.8 %all-to-all-start = ((bf16[8,128,768]{2,1,0:T(8,128)(2,1)}), bf16[8,128,768]{2,1,0:T(8,128)(2,1)S(1)}, u32[]{:S(2)}, u32[]{:S(2)}) async-start(bf16[8,128,768]{2,1,0:T(8,128)(2,1)} %get-tuple-element.24), calls=%async_computation | async-start | bytes 3145728 | tf_op jit(solution)/shard_map/all_to_all | solution.py:195
  20.4 0.0 copy-done.1
  20.4 7.1 %collective-permute-start.2 = (bf16[16,1280]{1,0:T(8,128)(2,1)S(1)}, bf16[16,1280]{1,0:T(8,128)(2,1)S(1)}, u32[]{:S(2)}, u32[]{:S(2)}) collective-permute-start(bf16[16,1280]{1,0:T(8,128)(2,1)S(1)} %copy-done.1), channel_id=1, source_target_pairs={{1000,0},{1008,8},{1016,16},{0,24},{8,32},{16,40},{24,48},{32,56},... | collective-permute-start | bytes 122888 | tf_op jit(solution)/shard_map/ppermute | solution.py:24
  27.5 2.9 %collective-permute-start.1 = (bf16[16,1280]{1,0:T(8,128)(2,1)S(1)}, bf16[16,1280]{1,0:T(8,128)(2,1)S(1)}, u32[]{:S(2)}, u32[]{:S(2)}) collective-permute-start(bf16[16,1280]{1,0:T(8,128)(2,1)S(1)} %copy-done.1), channel_id=1, source_target_pairs={{1008,0},{1016,8},{0,16},{8,24},{16,32},{24,40},{32,48},{40,56},{4... | collective-permute-start | bytes 122888 | tf_op jit(solution)/shard_map/ppermute | solution.py:24
  30.4 2.7 %collective-permute-start = (bf16[16,1280]{1,0:T(8,128)(2,1)S(1)}, bf16[16,1280]{1,0:T(8,128)(2,1)S(1)}, u32[]{:S(2)}, u32[]{:S(2)}) collective-permute-start(bf16[16,1280]{1,0:T(8,128)(2,1)S(1)} %copy-done.1), channel_id=1, source_target_pairs={{1016,0},{0,8},{8,16},{16,24},{24,32},{32,40},{40,48},{48,56},{56,... | collective-permute-start | bytes 122888 | tf_op jit(solution)/shard_map/ppermute | solution.py:24
  33.1 3.9 %collective-permute-done.2.refs_3_ = bf16[16,1280]{1,0:T(8,128)(2,1)S(1)} collective-permute-done((bf16[16,1280]{1,0:T(8,128)(2,1)S(1)}, bf16[16,1280]{1,0:T(8,128)(2,1)S(1)}, u32[]{:S(2)}, u32[]{:S(2)}) %collective-permute-start.2) | collective-permute-done | bytes 40992 | tf_op jit(solution)/shard_map/ppermute | solution.py:24
  37.0 5.8 %collective-permute-done.1.refs_2_ = bf16[16,1280]{1,0:T(8,128)(2,1)S(1)} collective-permute-done((bf16[16,1280]{1,0:T(8,128)(2,1)S(1)}, bf16[16,1280]{1,0:T(8,128)(2,1)S(1)}, u32[]{:S(2)}, u32[]{:S(2)}) %collective-permute-start.1) | collective-permute-done | bytes 40992 | tf_op jit(solution)/shard_map/ppermute | solution.py:24
  42.8 0.0 collective-permute-done.refs_1_
  42.8 17.6 %all_gather.3.a_ref = bf16[256,1280]{1,0:T(8,128)(2,1)S(1)} all-gather(bf16[64,1280]{1,0:T(8,128)(2,1)S(1)} %assemble.1.own_ref), channel_id=1, replica_groups=mesh['xh'=2,'z'=8,'y'=8,'xl'=4,'core'=2] {'xl'}, dimensions={0}, use_global_device_ids=true | all-gather | bytes 819200 | tf_op jit(solution)/shard_map/all_gather | solution.py:203
  60.3 1.9 %collective-permute-start.3 = (bf16[256,1280]{1,0:T(8,128)(2,1)S(1)}, bf16[256,1280]{1,0:T(8,128)(2,1)S(1)}, u32[]{:S(2)}, u32[]{:S(2)}) collective-permute-start(bf16[256,1280]{1,0:T(8,128)(2,1)S(1)} %all_gather.3.a_ref), channel_id=1, source_target_pairs={{1,0},{0,1},{3,2},{2,3},{5,4},{4,5},{7,6},{6,7},{9,8},{8,9},{11,10... | collective-permute-start | bytes 1966088 | tf_op jit(solution)/shard_map/ppermute | solution.py:24
  62.3 2.1 %collective-permute-done.3.b_ref = bf16[256,1280]{1,0:T(8,128)(2,1)S(1)} collective-permute-done((bf16[256,1280]{1,0:T(8,128)(2,1)S(1)}, bf16[256,1280]{1,0:T(8,128)(2,1)S(1)}, u32[]{:S(2)}, u32[]{:S(2)}) %collective-permute-start.3) | collective-permute-done | bytes 655392 | tf_op jit(solution)/shard_map/ppermute | solution.py:24
  64.3 2.0 %image_side.1 = (bf16[128,1152]{1,0:T(8,128)(2,1)S(1)}, bf16[8,2,72,128]{3,2,1,0:T(8,128)(2,1)}, f32[16,1152]{1,0:T(8,128)S(1)}, bf16[16,1152]{1,0:T(8,128)(2,1)...) custom-call(bf16[256,1280]{1,0:T(8,128)(2,1)S(1)} %all_gather.3.a_ref, ...), custom_call_target="tpu_custom_call" | custom-call | tf_op jit(solution)/shard_map/image_side/pallas_call | solution.py:162
  66.3 0.0 all-to-all-done.feat_ref
  66.3 3.6 %all-to-all-start.1 = ((bf16[8,144,128]{2,1,0:T(8,128)(2,1)}), bf16[8,144,128]{2,1,0:T(8,128)(2,1)S(1)}, u32[]{:S(2)}, u32[]{:S(2)}) async-start(bf16[8,144,128]{2,1,0:T(8,128)(2,1)} %bitcast.4), calls=%async_computation.1 | async-start | bytes 589824 | tf_op jit(solution)/shard_map/all_to_all | solution.py:215
  69.9 4.4 %collective-permute-start.4 = (bf16[16,1152]{1,0:T(8,128)(2,1)S(1)}, bf16[16,1152]{1,0:T(8,128)(2,1)S(1)}, u32[]{:S(2)}, u32[]{:S(2)}) collective-permute-start(bf16[16,1152]{1,0:T(8,128)(2,1)S(1)} %get-tuple-element.18), channel_id=1, source_target_pairs={{8,0},{16,8},{24,16},{32,24},{40,32},{48,40},{56,48},{64,56},{72,6... | collective-permute-start | bytes 110600 | tf_op jit(solution)/shard_map/ppermute | solution.py:24
  74.3 6.2 %collective-permute-start.5 = (bf16[16,1152]{1,0:T(8,128)(2,1)S(1)}, bf16[16,1152]{1,0:T(8,128)(2,1)S(1)}, u32[]{:S(2)}, u32[]{:S(2)}) collective-permute-start(bf16[16,1152]{1,0:T(8,128)(2,1)S(1)} %get-tuple-element.19), channel_id=1, source_target_pairs={{16,0},{24,8},{32,16},{40,24},{48,32},{56,40},{64,48},{72,56},{80,... | collective-permute-start | bytes 110600 | tf_op jit(solution)/shard_map/ppermute | solution.py:24
  80.6 3.6 %collective-permute-start.6 = (bf16[16,1152]{1,0:T(8,128)(2,1)S(1)}, bf16[16,1152]{1,0:T(8,128)(2,1)S(1)}, u32[]{:S(2)}, u32[]{:S(2)}) collective-permute-start(bf16[16,1152]{1,0:T(8,128)(2,1)S(1)} %get-tuple-element.20), channel_id=1, source_target_pairs={{24,0},{32,8},{40,16},{48,24},{56,32},{64,40},{72,48},{80,56},{88,... | collective-permute-start | bytes 110600 | tf_op jit(solution)/shard_map/ppermute | solution.py:24
  84.2 0.0 all-to-all-done.1.turned_ref
  84.2 1.4 %head_side.1 = bf16[16,54,128]{2,1,0:T(8,128)(2,1)} custom-call(bf16[8,128,768]{2,1,0:T(8,128)(2,1)S(1)} %all-to-all-done.feat_ref, bf16[8,144,128]{2,1,0:T(8,128)(2,1)S(1)} %all-to-all-done.1.turned_ref), custom_call_target="tpu_custom_call" | custom-call | tf_op jit(solution)/shard_map/head_side/pallas_call | solution.py:162
  85.6 8.2 %all-to-all-start.2 = ((bf16[16,54,128]{2,1,0:T(8,128)(2,1)}), bf16[16,54,128]{2,1,0:T(8,128)(2,1)S(1)}, u32[]{:S(2)}, u32[]{:S(2)}) async-start(bf16[16,54,128]{2,1,0:T(8,128)(2,1)} %head_side.1), calls=%async_computation.2 | async-start | bytes 458752 | tf_op jit(solution)/shard_map/all_to_all | solution.py:223
  93.8 0.0 collective-permute-done.4.one_ref
  93.8 0.0 collective-permute-done.5.two_ref
  93.8 0.0 collective-permute-done.6.three_ref
  93.8 0.0 copy-start.4
  93.8 1.5 %copy-done.4 = bf16[1152,768]{1,0:T(8,128)(2,1)S(1)} copy-done((bf16[1152,768]{1,0:T(8,128)(2,1)S(1)}, bf16[1152,768]{1,0:T(8,128)(2,1)}, u32[]{:S(2)}) %copy-start.4) | copy-done | bytes 1769496
  95.3 1.1 %finish.1 = (bf16[128,768]{1,0:T(8,128)(2,1)}, f32[16,1152]{1,0:T(8,128)}) custom-call(bf16[128,1152]{1,0:T(8,128)(2,1)S(1)} %get-tuple-element.16.grad_ref, bf16[1152,768]{1,0:T(8,128)(2,1)S(1)} %copy-done.4, bf16[16,1152]{1,0:T(8,128)(2,1)S(1)} %copy-done.2, f32[16,1152]{1,0:T(8,128)S(1)} %get-tuple-element.17.kept_ref, ...), custom_call_target="tpu_custom_call" | custom-call | flops 60000002048 | tf_op jit(solution)/shard_map/finish/pallas_call | solution.py:162
  96.4 9.4 %all-to-all-done.2.parts_ref = bf16[16,54,128]{2,1,0:T(8,128)(2,1)S(1)} async-done(((bf16[16,54,128]{2,1,0:T(8,128)(2,1)}), bf16[16,54,128]{2,1,0:T(8,128)(2,1)S(1)}, u32[]{:S(2)}, u32[]{:S(2)}) %all-to-all-start.2) | async-done | bytes 221216 | tf_op jit(solution)/shard_map/all_to_all | solution.py:223
  105.8 0.7 head_sum.1
  (5 shorter events, 0.0 us)
Async XLA Ops:
  3.5 16.9 %copy-start.1 = (bf16[16,1280]{1,0:T(8,128)(2,1)S(1)}, bf16[16,1280]{1,0:T(8,128)(2,1)}, u32[]{:S(2)}) copy-start(bf16[16,1280]{1,0:T(8,128)(2,1)} %get-tuple-element.15.refs_0_) | copy-start | bytes 122884
  3.6 60.8 %copy-start = (bf16[128,1152]{1,0:T(8,128)(2,1)S(1)}, bf16[128,1152]{1,0:T(8,128)(2,1)}, u32[]{:S(2)}) copy-start(bf16[128,1152]{1,0:T(8,128)(2,1)} %embed_ref.1) | copy-start | bytes 884740
  3.6 60.8 %copy-start.3 = (s32[128]{0:T(128)S(1)}, s32[128]{0:T(128)}, u32[]{:S(2)}) copy-start(s32[128]{0:T(128)} %param.11) | copy-start | bytes 1540
  3.6 62.8 %all-to-all-start = ((bf16[8,128,768]{2,1,0:T(8,128)(2,1)}), bf16[8,128,768]{2,1,0:T(8,128)(2,1)S(1)}, u32[]{:S(2)}, u32[]{:S(2)}) async-start(bf16[8,128,768]{2,1,0:T(8,128)(2,1)} %get-tuple-element.24), calls=%async_computation | async-start | bytes 3145728 | tf_op jit(solution)/shard_map/all_to_all | solution.py:195
  20.4 16.6 %collective-permute-start.2 = (bf16[16,1280]{1,0:T(8,128)(2,1)S(1)}, bf16[16,1280]{1,0:T(8,128)(2,1)S(1)}, u32[]{:S(2)}, u32[]{:S(2)}) collective-permute-start(bf16[16,1280]{1,0:T(8,128)(2,1)S(1)} %copy-done.1), channel_id=1, source_target_pairs={{1000,0},{1008,8},{1016,16},{0,24},{8,32},{16,40},{24,48},{32,56},... | collective-permute-start | bytes 122888 | tf_op jit(solution)/shard_map/ppermute | solution.py:24
  27.5 15.3 %collective-permute-start.1 = (bf16[16,1280]{1,0:T(8,128)(2,1)S(1)}, bf16[16,1280]{1,0:T(8,128)(2,1)S(1)}, u32[]{:S(2)}, u32[]{:S(2)}) collective-permute-start(bf16[16,1280]{1,0:T(8,128)(2,1)S(1)} %copy-done.1), channel_id=1, source_target_pairs={{1008,0},{1016,8},{0,16},{8,24},{16,32},{24,40},{32,48},{40,56},{4... | collective-permute-start | bytes 122888 | tf_op jit(solution)/shard_map/ppermute | solution.py:24
  30.4 12.4 %collective-permute-start = (bf16[16,1280]{1,0:T(8,128)(2,1)S(1)}, bf16[16,1280]{1,0:T(8,128)(2,1)S(1)}, u32[]{:S(2)}, u32[]{:S(2)}) collective-permute-start(bf16[16,1280]{1,0:T(8,128)(2,1)S(1)} %copy-done.1), channel_id=1, source_target_pairs={{1016,0},{0,8},{8,16},{16,24},{24,32},{32,40},{40,48},{48,56},{56,... | collective-permute-start | bytes 122888 | tf_op jit(solution)/shard_map/ppermute | solution.py:24
  60.3 4.0 %collective-permute-start.3 = (bf16[256,1280]{1,0:T(8,128)(2,1)S(1)}, bf16[256,1280]{1,0:T(8,128)(2,1)S(1)}, u32[]{:S(2)}, u32[]{:S(2)}) collective-permute-start(bf16[256,1280]{1,0:T(8,128)(2,1)S(1)} %all_gather.3.a_ref), channel_id=1, source_target_pairs={{1,0},{0,1},{3,2},{2,3},{5,4},{4,5},{7,6},{6,7},{9,8},{8,9},{11,10... | collective-permute-start | bytes 1966088 | tf_op jit(solution)/shard_map/ppermute | solution.py:24
  66.3 27.4 %copy-start.2 = (bf16[16,1152]{1,0:T(8,128)(2,1)S(1)}, bf16[16,1152]{1,0:T(8,128)(2,1)}, u32[]{:S(2)}) copy-start(bf16[16,1152]{1,0:T(8,128)(2,1)} %text_ref.1) | copy-start | bytes 110596
  66.3 17.8 %all-to-all-start.1 = ((bf16[8,144,128]{2,1,0:T(8,128)(2,1)}), bf16[8,144,128]{2,1,0:T(8,128)(2,1)S(1)}, u32[]{:S(2)}, u32[]{:S(2)}) async-start(bf16[8,144,128]{2,1,0:T(8,128)(2,1)} %bitcast.4), calls=%async_computation.1 | async-start | bytes 589824 | tf_op jit(solution)/shard_map/all_to_all | solution.py:215
  69.9 23.8 %collective-permute-start.4 = (bf16[16,1152]{1,0:T(8,128)(2,1)S(1)}, bf16[16,1152]{1,0:T(8,128)(2,1)S(1)}, u32[]{:S(2)}, u32[]{:S(2)}) collective-permute-start(bf16[16,1152]{1,0:T(8,128)(2,1)S(1)} %get-tuple-element.18), channel_id=1, source_target_pairs={{8,0},{16,8},{24,16},{32,24},{40,32},{48,40},{56,48},{64,56},{72,6... | collective-permute-start | bytes 110600 | tf_op jit(solution)/shard_map/ppermute | solution.py:24
  74.3 19.4 %collective-permute-start.5 = (bf16[16,1152]{1,0:T(8,128)(2,1)S(1)}, bf16[16,1152]{1,0:T(8,128)(2,1)S(1)}, u32[]{:S(2)}, u32[]{:S(2)}) collective-permute-start(bf16[16,1152]{1,0:T(8,128)(2,1)S(1)} %get-tuple-element.19), channel_id=1, source_target_pairs={{16,0},{24,8},{32,16},{40,24},{48,32},{56,40},{64,48},{72,56},{80,... | collective-permute-start | bytes 110600 | tf_op jit(solution)/shard_map/ppermute | solution.py:24
  80.6 13.2 %collective-permute-start.6 = (bf16[16,1152]{1,0:T(8,128)(2,1)S(1)}, bf16[16,1152]{1,0:T(8,128)(2,1)S(1)}, u32[]{:S(2)}, u32[]{:S(2)}) collective-permute-start(bf16[16,1152]{1,0:T(8,128)(2,1)S(1)} %get-tuple-element.20), channel_id=1, source_target_pairs={{24,0},{32,8},{40,16},{48,24},{56,32},{64,40},{72,48},{80,56},{88,... | collective-permute-start | bytes 110600 | tf_op jit(solution)/shard_map/ppermute | solution.py:24
  85.6 20.2 %all-to-all-start.2 = ((bf16[16,54,128]{2,1,0:T(8,128)(2,1)}), bf16[16,54,128]{2,1,0:T(8,128)(2,1)S(1)}, u32[]{:S(2)}, u32[]{:S(2)}) async-start(bf16[16,54,128]{2,1,0:T(8,128)(2,1)} %head_side.1), calls=%async_computation.2 | async-start | bytes 458752 | tf_op jit(solution)/shard_map/all_to_all | solution.py:223
  93.8 1.5 %copy-start.4 = (bf16[1152,768]{1,0:T(8,128)(2,1)S(1)}, bf16[1152,768]{1,0:T(8,128)(2,1)}, u32[]{:S(2)}) copy-start(bf16[1152,768]{1,0:T(8,128)(2,1)} %head_ref.1) | copy-start | bytes 5308420

commit v10 on v9

--- a/solution.py
+++ b/solution.py
@@ -1,3 +1,5 @@
+import functools
+
 import jax
 import jax.numpy as jnp
 from jax import lax
@@ -120,15 +122,16 @@
         ref[...] = share[k * count : (k + 1) * count].astype(ref.dtype)
 
 
-def head_side(feat_ref, turned_ref, out_ref):
+def head_side(pieces, feat_ref, turned_ref, out_ref):
     part = jnp.zeros((turned_ref.shape[1], feat_ref.shape[2]), f32)
     for k in range(turned_ref.shape[0]):
         part = part + jnp.dot(turned_ref[k], feat_ref[k], preferred_element_type=f32)
     targets, groups = out_ref.shape[0], part.shape[1] // 128
     run = part.shape[0] // targets
     for c in range(targets):
+        place = c % (targets // pieces) * pieces + c // (targets // pieces)
         for g in range(groups):
-            out_ref[c, g * run : (g + 1) * run] = part[
+            out_ref[place, g * run : (g + 1) * run] = part[
                 c * run : (c + 1) * run, g * 128 : (g + 1) * 128
             ].astype(bf16)
 
@@ -167,7 +170,7 @@
         scratch_shapes=list(scratch),
         compiler_params=pltpu.CompilerParams(vmem_limit_bytes=room),
         cost_estimate=cost,
-        name=kernel.__name__,
+        name=getattr(kernel, "func", kernel).__name__,
     )(*args)
 
 
@@ -218,9 +221,9 @@
 
     rows = own_width // across
     parts = call(
-        head_side, [((across, rows * features // 128, 128), bf16)], feats, plane, room=ROOM,
-    )
-    parts = lax.all_to_all(parts, ("xh", "y"), 0, 0, tiled=True)
+        functools.partial(head_side, pieces), [((across, rows * features // 128, 128), bf16)], feats, plane, room=ROOM,
+    )
+    parts = lax.all_to_all(parts, ("y", "xh"), 0, 0, tiled=True)
     image_grad, text_grad = call(
         finish, [((images, features), bf16), ((texts, width), f32)],
         embed_grad, head, text_embed, kept, *backs, cost=lasting(60), room=ROOM,

time: 107 us -> 107 us (level)
  the two profiles are of different devices: /device:TPU:16 before, /device:TPU:4 now
where the time goes in v10:
time: 107 us
  starting transfers between devices  55.6 us (52%)
  waiting for transfers between devices  26.1 us (24%)
  blocking collectives  14.7 us (14%)
  Pallas kernels  8.13 us (8%)
  local copies, waits for them, and re-layouts  1.49 us (1%)
    ppermute x7, starting transfers between devices, shifted(): lax.ppermute(block, axis, [((i - distance) % size, i) for i in range(size)])  28.3 us
    all_to_all x1, starting transfers between devices, local(): feats = lax.all_to_all(feats, 'z', 0, 0, tiled=True)  16.8 us
    all_gather x1, blocking collectives, local(): here = lax.all_gather(own, 'xl', axis=0, tiled=True)  14.7 us
    ppermute x7, waiting for transfers between devices, shifted(): lax.ppermute(block, axis, [((i - distance) % size, i) for i in range(size)])  14.2 us
    all_to_all x1, waiting for transfers between devices, local(): parts = lax.all_to_all(parts, ('y', 'xh'), 0, 0, tiled=True)  11.6 us
    pallas_call x6, Pallas kernels, call(): pl.pallas_call(kernel, out_shape=outs[0] if single else outs, in_specs=sp...  8.13 us
    all_to_all x1, starting transfers between devices, local(): parts = lax.all_to_all(parts, ('y', 'xh'), 0, 0, tiled=True)  6.96 us
    all_to_all x1, starting transfers between devices, local(): lax.all_to_all(turned.reshape(planes, own_width, images), 'z', 0, 0, tile...  3.55 us
  transfers between devices with their start and end apart: 10, of which 6 were waited for; matrix products, arithmetic and copies ran while one was open for 0% of the time, Pallas kernels for 4%

profile of v10, /device:TPU:4, one launch (start us, length us, event | category | flops | bytes accessed | tf_op | source)
XLA Modules:
  0.0 106.8 jit_solution(10362455869651914116)
XLA Ops:
  0.6 2.9 %prepare.1 = (bf16[16,1280]{1,0:T(8,128)(2,1)}, bf16[8,128,768]{2,1,0:T(8,128)(2,1)}) custom-call(s32[1]{0:T(128)} %bitcast.pos_ref, bf16[16,1152]{1,0:T(8,128)(2,1)} %text_ref.1, s32[1,128]{1,0:T(1,128)} %bitcast.5, s32[1,128]{1,0:T(1,128)} %bitcast.7, f32[1,8]{1,0:T(1,128)} %bitcast.8, bf16[128,768]{1,0:T(8,128)(2,1)} %refs_4_.1), custom_call_target="tpu_custom_call" | custom-call | tf_op jit(solution)/shard_map/prepare/pallas_call | solution.py:165
  3.5 0.0 copy-start.1
  3.6 0.0 copy-start
  3.6 0.0 copy-start.3
  3.6 16.8 %all-to-all-start = ((bf16[8,128,768]{2,1,0:T(8,128)(2,1)}), bf16[8,128,768]{2,1,0:T(8,128)(2,1)S(1)}, u32[]{:S(2)}, u32[]{:S(2)}) async-start(bf16[8,128,768]{2,1,0:T(8,128)(2,1)} %get-tuple-element.24), calls=%async_computation | async-start | bytes 3145728 | tf_op jit(solution)/shard_map/all_to_all | solution.py:198
  20.4 5.9 %collective-permute-start.2 = (bf16[16,1280]{1,0:T(8,128)(2,1)S(1)}, bf16[16,1280]{1,0:T(8,128)(2,1)S(1)}, u32[]{:S(2)}, u32[]{:S(2)}) collective-permute-start(bf16[16,1280]{1,0:T(8,128)(2,1)S(1)} %copy-done.1), channel_id=1, source_target_pairs={{1000,0},{1008,8},{1016,16},{0,24},{8,32},{16,40},{24,48},{32,56},... | collective-permute-start | bytes 122888 | tf_op jit(solution)/shard_map/ppermute | solution.py:26
  26.3 5.0 %collective-permute-start.1 = (bf16[16,1280]{1,0:T(8,128)(2,1)S(1)}, bf16[16,1280]{1,0:T(8,128)(2,1)S(1)}, u32[]{:S(2)}, u32[]{:S(2)}) collective-permute-start(bf16[16,1280]{1,0:T(8,128)(2,1)S(1)} %copy-done.1), channel_id=1, source_target_pairs={{1008,0},{1016,8},{0,16},{8,24},{16,32},{24,40},{32,48},{40,56},{4... | collective-permute-start | bytes 122888 | tf_op jit(solution)/shard_map/ppermute | solution.py:26
  31.3 2.7 %collective-permute-start = (bf16[16,1280]{1,0:T(8,128)(2,1)S(1)}, bf16[16,1280]{1,0:T(8,128)(2,1)S(1)}, u32[]{:S(2)}, u32[]{:S(2)}) collective-permute-start(bf16[16,1280]{1,0:T(8,128)(2,1)S(1)} %copy-done.1), channel_id=1, source_target_pairs={{1016,0},{0,8},{8,16},{16,24},{24,32},{32,40},{40,48},{48,56},{56,... | collective-permute-start | bytes 122888 | tf_op jit(solution)/shard_map/ppermute | solution.py:26
  34.0 2.9 %collective-permute-done.2.refs_3_ = bf16[16,1280]{1,0:T(8,128)(2,1)S(1)} collective-permute-done((bf16[16,1280]{1,0:T(8,128)(2,1)S(1)}, bf16[16,1280]{1,0:T(8,128)(2,1)S(1)}, u32[]{:S(2)}, u32[]{:S(2)}) %collective-permute-start.2) | collective-permute-done | bytes 40992 | tf_op jit(solution)/shard_map/ppermute | solution.py:26
  36.9 5.0 %collective-permute-done.1.refs_2_ = bf16[16,1280]{1,0:T(8,128)(2,1)S(1)} collective-permute-done((bf16[16,1280]{1,0:T(8,128)(2,1)S(1)}, bf16[16,1280]{1,0:T(8,128)(2,1)S(1)}, u32[]{:S(2)}, u32[]{:S(2)}) %collective-permute-start.1) | collective-permute-done | bytes 40992 | tf_op jit(solution)/shard_map/ppermute | solution.py:26
  41.8 4.3 %collective-permute-done.refs_1_ = bf16[16,1280]{1,0:T(8,128)(2,1)S(1)} collective-permute-done((bf16[16,1280]{1,0:T(8,128)(2,1)S(1)}, bf16[16,1280]{1,0:T(8,128)(2,1)S(1)}, u32[]{:S(2)}, u32[]{:S(2)}) %collective-permute-start) | collective-permute-done | bytes 40992 | tf_op jit(solution)/shard_map/ppermute | solution.py:26
  46.2 14.7 %all_gather.3.a_ref = bf16[256,1280]{1,0:T(8,128)(2,1)S(1)} all-gather(bf16[64,1280]{1,0:T(8,128)(2,1)S(1)} %assemble.1.own_ref), channel_id=1, replica_groups=mesh['xh'=2,'z'=8,'y'=8,'xl'=4,'core'=2] {'xl'}, dimensions={0}, use_global_device_ids=true | all-gather | bytes 819200 | tf_op jit(solution)/shard_map/all_gather | solution.py:206
  60.9 1.9 %collective-permute-start.3 = (bf16[256,1280]{1,0:T(8,128)(2,1)S(1)}, bf16[256,1280]{1,0:T(8,128)(2,1)S(1)}, u32[]{:S(2)}, u32[]{:S(2)}) collective-permute-start(bf16[256,1280]{1,0:T(8,128)(2,1)S(1)} %all_gather.3.a_ref), channel_id=1, source_target_pairs={{1,0},{0,1},{3,2},{2,3},{5,4},{4,5},{7,6},{6,7},{9,8},{8,9},{11,10... | collective-permute-start | bytes 1966088 | tf_op jit(solution)/shard_map/ppermute | solution.py:26
  62.8 2.1 %collective-permute-done.3.b_ref = bf16[256,1280]{1,0:T(8,128)(2,1)S(1)} collective-permute-done((bf16[256,1280]{1,0:T(8,128)(2,1)S(1)}, bf16[256,1280]{1,0:T(8,128)(2,1)S(1)}, u32[]{:S(2)}, u32[]{:S(2)}) %collective-permute-start.3) | collective-permute-done | bytes 655392 | tf_op jit(solution)/shard_map/ppermute | solution.py:26
  64.8 0.0 copy-done.3
  64.8 2.0 %image_side.1 = (bf16[128,1152]{1,0:T(8,128)(2,1)S(1)}, bf16[8,2,72,128]{3,2,1,0:T(8,128)(2,1)}, f32[16,1152]{1,0:T(8,128)S(1)}, bf16[16,1152]{1,0:T(8,128)(2,1)...) custom-call(bf16[256,1280]{1,0:T(8,128)(2,1)S(1)} %all_gather.3.a_ref, ...), custom_call_target="tpu_custom_call" | custom-call | tf_op jit(solution)/shard_map/image_side/pallas_call | solution.py:165
  66.9 0.0 all-to-all-done.feat_ref
  66.9 3.6 %all-to-all-start.1 = ((bf16[8,144,128]{2,1,0:T(8,128)(2,1)}), bf16[8,144,128]{2,1,0:T(8,128)(2,1)S(1)}, u32[]{:S(2)}, u32[]{:S(2)}) async-start(bf16[8,144,128]{2,1,0:T(8,128)(2,1)} %bitcast.4), calls=%async_computation.1 | async-start | bytes 589824 | tf_op jit(solution)/shard_map/all_to_all | solution.py:218
  70.4 6.3 %collective-permute-start.4 = (bf16[16,1152]{1,0:T(8,128)(2,1)S(1)}, bf16[16,1152]{1,0:T(8,128)(2,1)S(1)}, u32[]{:S(2)}, u32[]{:S(2)}) collective-permute-start(bf16[16,1152]{1,0:T(8,128)(2,1)S(1)} %get-tuple-element.18), channel_id=1, source_target_pairs={{8,0},{16,8},{24,16},{32,24},{40,32},{48,40},{56,48},{64,56},{72,6... | collective-permute-start | bytes 110600 | tf_op jit(solution)/shard_map/ppermute | solution.py:26
  76.7 2.9 %collective-permute-start.5 = (bf16[16,1152]{1,0:T(8,128)(2,1)S(1)}, bf16[16,1152]{1,0:T(8,128)(2,1)S(1)}, u32[]{:S(2)}, u32[]{:S(2)}) collective-permute-start(bf16[16,1152]{1,0:T(8,128)(2,1)S(1)} %get-tuple-element.19), channel_id=1, source_target_pairs={{16,0},{24,8},{32,16},{40,24},{48,32},{56,40},{64,48},{72,56},{80,... | collective-permute-start | bytes 110600 | tf_op jit(solution)/shard_map/ppermute | solution.py:26
  79.7 3.6 %collective-permute-start.6 = (bf16[16,1152]{1,0:T(8,128)(2,1)S(1)}, bf16[16,1152]{1,0:T(8,128)(2,1)S(1)}, u32[]{:S(2)}, u32[]{:S(2)}) collective-permute-start(bf16[16,1152]{1,0:T(8,128)(2,1)S(1)} %get-tuple-element.20), channel_id=1, source_target_pairs={{24,0},{32,8},{40,16},{48,24},{56,32},{64,40},{72,48},{80,56},{88,... | collective-permute-start | bytes 110600 | tf_op jit(solution)/shard_map/ppermute | solution.py:26
  83.3 0.2 all-to-all-done.1.turned_ref
  83.5 1.4 %head_side.1 = bf16[16,54,128]{2,1,0:T(8,128)(2,1)} custom-call(bf16[8,128,768]{2,1,0:T(8,128)(2,1)S(1)} %all-to-all-done.feat_ref, bf16[8,144,128]{2,1,0:T(8,128)(2,1)S(1)} %all-to-all-done.1.turned_ref), custom_call_target="tpu_custom_call" | custom-call | tf_op jit(solution)/shard_map/head_side/pallas_call | solution.py:165
  84.9 7.0 %all-to-all-start.2 = ((bf16[16,54,128]{2,1,0:T(8,128)(2,1)}), bf16[16,54,128]{2,1,0:T(8,128)(2,1)S(1)}, u32[]{:S(2)}, u32[]{:S(2)}) async-start(bf16[16,54,128]{2,1,0:T(8,128)(2,1)} %head_side.1), calls=%async_computation.2 | async-start | bytes 458752 | tf_op jit(solution)/shard_map/all_to_all | solution.py:226
  91.9 0.0 collective-permute-done.4.one_ref
  91.9 0.0 collective-permute-done.5.two_ref
  91.9 0.0 collective-permute-done.6.three_ref
  91.9 0.0 copy-start.4
  91.9 1.5 %copy-done.4 = bf16[1152,768]{1,0:T(8,128)(2,1)S(1)} copy-done((bf16[1152,768]{1,0:T(8,128)(2,1)S(1)}, bf16[1152,768]{1,0:T(8,128)(2,1)}, u32[]{:S(2)}) %copy-start.4) | copy-done | bytes 1769496
  93.4 1.1 %finish.1 = (bf16[128,768]{1,0:T(8,128)(2,1)}, f32[16,1152]{1,0:T(8,128)}) custom-call(bf16[128,1152]{1,0:T(8,128)(2,1)S(1)} %get-tuple-element.16.grad_ref, bf16[1152,768]{1,0:T(8,128)(2,1)S(1)} %copy-done.4, bf16[16,1152]{1,0:T(8,128)(2,1)S(1)} %copy-done.2, f32[16,1152]{1,0:T(8,128)S(1)} %get-tuple-element.17.kept_ref, ...), custom_call_target="tpu_custom_call" | custom-call | flops 60000002048 | tf_op jit(solution)/shard_map/finish/pallas_call | solution.py:165
  94.5 11.6 %all-to-all-done.2.parts_ref = bf16[16,54,128]{2,1,0:T(8,128)(2,1)S(1)} async-done(((bf16[16,54,128]{2,1,0:T(8,128)(2,1)}), bf16[16,54,128]{2,1,0:T(8,128)(2,1)S(1)}, u32[]{:S(2)}, u32[]{:S(2)}) %all-to-all-start.2) | async-done | bytes 221216 | tf_op jit(solution)/shard_map/all_to_all | solution.py:226
  106.2 0.7 head_sum.1
  (5 shorter events, 0.0 us)
Async XLA Ops:
  3.5 16.9 %copy-start.1 = (bf16[16,1280]{1,0:T(8,128)(2,1)S(1)}, bf16[16,1280]{1,0:T(8,128)(2,1)}, u32[]{:S(2)}) copy-start(bf16[16,1280]{1,0:T(8,128)(2,1)} %get-tuple-element.15.refs_0_) | copy-start | bytes 122884
  3.6 61.3 %copy-start = (bf16[128,1152]{1,0:T(8,128)(2,1)S(1)}, bf16[128,1152]{1,0:T(8,128)(2,1)}, u32[]{:S(2)}) copy-start(bf16[128,1152]{1,0:T(8,128)(2,1)} %embed_ref.1) | copy-start | bytes 884740
  3.6 61.3 %copy-start.3 = (s32[128]{0:T(128)S(1)}, s32[128]{0:T(128)}, u32[]{:S(2)}) copy-start(s32[128]{0:T(128)} %param.11) | copy-start | bytes 1540
  3.6 63.3 %all-to-all-start = ((bf16[8,128,768]{2,1,0:T(8,128)(2,1)}), bf16[8,128,768]{2,1,0:T(8,128)(2,1)S(1)}, u32[]{:S(2)}, u32[]{:S(2)}) async-start(bf16[8,128,768]{2,1,0:T(8,128)(2,1)} %get-tuple-element.24), calls=%async_computation | async-start | bytes 3145728 | tf_op jit(solution)/shard_map/all_to_all | solution.py:198
  20.4 16.5 %collective-permute-start.2 = (bf16[16,1280]{1,0:T(8,128)(2,1)S(1)}, bf16[16,1280]{1,0:T(8,128)(2,1)S(1)}, u32[]{:S(2)}, u32[]{:S(2)}) collective-permute-start(bf16[16,1280]{1,0:T(8,128)(2,1)S(1)} %copy-done.1), channel_id=1, source_target_pairs={{1000,0},{1008,8},{1016,16},{0,24},{8,32},{16,40},{24,48},{32,56},... | collective-permute-start | bytes 122888 | tf_op jit(solution)/shard_map/ppermute | solution.py:26
  26.3 15.6 %collective-permute-start.1 = (bf16[16,1280]{1,0:T(8,128)(2,1)S(1)}, bf16[16,1280]{1,0:T(8,128)(2,1)S(1)}, u32[]{:S(2)}, u32[]{:S(2)}) collective-permute-start(bf16[16,1280]{1,0:T(8,128)(2,1)S(1)} %copy-done.1), channel_id=1, source_target_pairs={{1008,0},{1016,8},{0,16},{8,24},{16,32},{24,40},{32,48},{40,56},{4... | collective-permute-start | bytes 122888 | tf_op jit(solution)/shard_map/ppermute | solution.py:26
  31.3 14.8 %collective-permute-start = (bf16[16,1280]{1,0:T(8,128)(2,1)S(1)}, bf16[16,1280]{1,0:T(8,128)(2,1)S(1)}, u32[]{:S(2)}, u32[]{:S(2)}) collective-permute-start(bf16[16,1280]{1,0:T(8,128)(2,1)S(1)} %copy-done.1), channel_id=1, source_target_pairs={{1016,0},{0,8},{8,16},{16,24},{24,32},{32,40},{40,48},{48,56},{56,... | collective-permute-start | bytes 122888 | tf_op jit(solution)/shard_map/ppermute | solution.py:26
  60.9 4.0 %collective-permute-start.3 = (bf16[256,1280]{1,0:T(8,128)(2,1)S(1)}, bf16[256,1280]{1,0:T(8,128)(2,1)S(1)}, u32[]{:S(2)}, u32[]{:S(2)}) collective-permute-start(bf16[256,1280]{1,0:T(8,128)(2,1)S(1)} %all_gather.3.a_ref), channel_id=1, source_target_pairs={{1,0},{0,1},{3,2},{2,3},{5,4},{4,5},{7,6},{6,7},{9,8},{8,9},{11,10... | collective-permute-start | bytes 1966088 | tf_op jit(solution)/shard_map/ppermute | solution.py:26
  66.9 25.0 %copy-start.2 = (bf16[16,1152]{1,0:T(8,128)(2,1)S(1)}, bf16[16,1152]{1,0:T(8,128)(2,1)}, u32[]{:S(2)}) copy-start(bf16[16,1152]{1,0:T(8,128)(2,1)} %text_ref.1) | copy-start | bytes 110596
  66.9 16.6 %all-to-all-start.1 = ((bf16[8,144,128]{2,1,0:T(8,128)(2,1)}), bf16[8,144,128]{2,1,0:T(8,128)(2,1)S(1)}, u32[]{:S(2)}, u32[]{:S(2)}) async-start(bf16[8,144,128]{2,1,0:T(8,128)(2,1)} %bitcast.4), calls=%async_computation.1 | async-start | bytes 589824 | tf_op jit(solution)/shard_map/all_to_all | solution.py:218
  70.4 21.5 %collective-permute-start.4 = (bf16[16,1152]{1,0:T(8,128)(2,1)S(1)}, bf16[16,1152]{1,0:T(8,128)(2,1)S(1)}, u32[]{:S(2)}, u32[]{:S(2)}) collective-permute-start(bf16[16,1152]{1,0:T(8,128)(2,1)S(1)} %get-tuple-element.18), channel_id=1, source_target_pairs={{8,0},{16,8},{24,16},{32,24},{40,32},{48,40},{56,48},{64,56},{72,6... | collective-permute-start | bytes 110600 | tf_op jit(solution)/shard_map/ppermute | solution.py:26
  76.7 15.2 %collective-permute-start.5 = (bf16[16,1152]{1,0:T(8,128)(2,1)S(1)}, bf16[16,1152]{1,0:T(8,128)(2,1)S(1)}, u32[]{:S(2)}, u32[]{:S(2)}) collective-permute-start(bf16[16,1152]{1,0:T(8,128)(2,1)S(1)} %get-tuple-element.19), channel_id=1, source_target_pairs={{16,0},{24,8},{32,16},{40,24},{48,32},{56,40},{64,48},{72,56},{80,... | collective-permute-start | bytes 110600 | tf_op jit(solution)/shard_map/ppermute | solution.py:26
  79.7 12.2 %collective-permute-start.6 = (bf16[16,1152]{1,0:T(8,128)(2,1)S(1)}, bf16[16,1152]{1,0:T(8,128)(2,1)S(1)}, u32[]{:S(2)}, u32[]{:S(2)}) collective-permute-start(bf16[16,1152]{1,0:T(8,128)(2,1)S(1)} %get-tuple-element.20), channel_id=1, source_target_pairs={{24,0},{32,8},{40,16},{48,24},{56,32},{64,40},{72,48},{80,56},{88,... | collective-permute-start | bytes 110600 | tf_op jit(solution)/shard_map/ppermute | solution.py:26
  84.9 21.2 %all-to-all-start.2 = ((bf16[16,54,128]{2,1,0:T(8,128)(2,1)}), bf16[16,54,128]{2,1,0:T(8,128)(2,1)S(1)}, u32[]{:S(2)}, u32[]{:S(2)}) async-start(bf16[16,54,128]{2,1,0:T(8,128)(2,1)} %head_side.1), calls=%async_computation.2 | async-start | bytes 458752 | tf_op jit(solution)/shard_map/all_to_all | solution.py:226
  91.9 1.5 %copy-start.4 = (bf16[1152,768]{1,0:T(8,128)(2,1)S(1)}, bf16[1152,768]{1,0:T(8,128)(2,1)}, u32[]{:S(2)}) copy-start(bf16[1152,768]{1,0:T(8,128)(2,1)} %head_ref.1) | copy-start | bytes 5308420

commit v11 on v9

--- a/solution.py
+++ b/solution.py
@@ -93,18 +93,27 @@
     return (-signs * jax.nn.sigmoid(-signs * logits)).astype(bf16)
 
 
-def image_side(a_ref, b_ref, own_ref, embed_ref, ids_ref, grad_ref, turned_ref, *share_refs):
+def toward(rows, rounded, ids):
+    slope = slopes(rows, rounded, ids)
+    return lax.dot_general(slope, rows[:, : rounded.shape[1]], TN, preferred_element_type=f32)
+
+
+def near_side(rows_ref, own_ref, embed_ref, ids_ref, total_ref, *share_refs):
+    floats = embed_ref[...].astype(f32)
+    rounded = (floats / norms_of(floats)).astype(bf16)
+    total_ref[...] = toward(rows_ref[...], rounded, ids_ref[...])
+    slope = slopes(own_ref[...], rounded, ids_ref[...])
+    share = SCALE * jnp.dot(slope, rounded, preferred_element_type=f32)
+    count = share_refs[0].shape[0]
+    for k, ref in enumerate(share_refs):
+        ref[...] = share[k * count : (k + 1) * count].astype(ref.dtype)
+
+
+def image_side(near_ref, rows_ref, embed_ref, ids_ref, grad_ref, turned_ref):
     floats = embed_ref[...].astype(f32)
     norms = norms_of(floats)
     units = floats / norms
-    rounded = units.astype(bf16)
-    width = floats.shape[1]
-    total = jnp.zeros(floats.shape, f32)
-    for ref in (a_ref, b_ref):
-        rows = ref[...]
-        slope = slopes(rows, rounded, ids_ref[...])
-        total = total + lax.dot_general(slope, rows[:, :width], TN, preferred_element_type=f32)
-    total = SCALE * total
+    total = SCALE * (near_ref[...] + toward(rows_ref[...], units.astype(bf16), ids_ref[...]))
     grad = (total - units * jnp.sum(units * total, -1, keepdims=True)) / norms
     grad_ref[...] = grad.astype(bf16)
     turned = grad.T.astype(bf16)
@@ -113,11 +122,6 @@
         for z in range(planes):
             start = (p * planes + z) * run
             turned_ref[z, p] = turned[start : start + run]
-    slope = slopes(own_ref[...], rounded, ids_ref[...])
-    share = SCALE * jnp.dot(slope, rounded, preferred_element_type=f32)
-    count = share_refs[0].shape[0]
-    for k, ref in enumerate(share_refs):
-        ref[...] = share[k * count : (k + 1) * count].astype(ref.dtype)
 
 
 def head_side(feat_ref, turned_ref, out_ref):
@@ -205,11 +209,14 @@
 
     pieces = lax.axis_size("xh")
     run = width // (planes * pieces)
-    embed_grad, turned, kept, *aways = call(
-        image_side,
-        [((images, width), bf16), ((planes, pieces, run, images), bf16), ((texts, width), f32)]
-        + [((texts, width), bf16)] * 3,
-        here, there, own, image_embed, ids, room=ROOM,
+    near, kept, *aways = call(
+        near_side,
+        [((images, width), f32), ((texts, width), f32)] + [((texts, width), bf16)] * 3,
+        here, own, image_embed, ids, cost=lasting(20), room=ROOM,
+    )
+    embed_grad, turned = call(
+        image_side, [((images, width), bf16), ((planes, pieces, run, images), bf16)],
+        near, there, image_embed, ids, room=ROOM,
     )
     turned, feats = lax.optimization_barrier((turned, feats))
     plane = lax.all_to_all(turned.reshape(planes, own_width, images), "z", 0, 0, tiled=True)

time: 107 us -> 107 us (level)
  waiting for transfers between devices: 21.1 us -> 20 us
    ppermute x7, waiting for transfers between devices: 11.7 us -> 10.6 us  [shifted(): lax.ppermute(block, axis, [((i - distance) % size, i) for i in range(size)])]
    pallas_call x6 -> x7, Pallas kernels: 8.12 us -> 9.08 us  [call(): pl.pallas_call(kernel, out_shape=outs[0] if single else outs, in_specs=sp...]
  transfers between devices with their start and end apart: 10 -> 10, of which waited for: 4 -> 4; matrix products, arithmetic and copies ran while one was open for 0% -> 0% of each run, Pallas kernels for 4% -> 5%
where the time goes in v11:
time: 107 us; the launch traced here: 106 us
  starting transfers between devices  57.4 us (54%)
  waiting for transfers between devices  20 us (19%)
  blocking collectives  17.6 us (16%)
  Pallas kernels  9.08 us (8%)
  local copies, waits for them, and re-layouts  1.49 us (1%)
    ppermute x7, starting transfers between devices, shifted(): lax.ppermute(block, axis, [((i - distance) % size, i) for i in range(size)])  29 us
    all_gather x1, blocking collectives, local(): here = lax.all_gather(own, 'xl', axis=0, tiled=True)  17.6 us
    all_to_all x1, starting transfers between devices, local(): feats = lax.all_to_all(feats, 'z', 0, 0, tiled=True)  16.8 us
    ppermute x7, waiting for transfers between devices, shifted(): lax.ppermute(block, axis, [((i - distance) % size, i) for i in range(size)])  10.6 us
    all_to_all x1, waiting for transfers between devices, local(): parts = lax.all_to_all(parts, ('xh', 'y'), 0, 0, tiled=True)  9.39 us
    pallas_call x7, Pallas kernels, call(): pl.pallas_call(kernel, out_shape=outs[0] if single else outs, in_specs=sp...  9.08 us
    all_to_all x1, starting transfers between devices, local(): parts = lax.all_to_all(parts, ('xh', 'y'), 0, 0, tiled=True)  7.98 us
    all_to_all x1, starting transfers between devices, local(): lax.all_to_all(turned.reshape(planes, own_width, images), 'z', 0, 0, tile...  3.55 us
  transfers between devices with their start and end apart: 10, of which 4 were waited for; matrix products, arithmetic and copies ran while one was open for 0% of the time, Pallas kernels for 5%

profile of v11, /device:TPU:16, one launch (start us, length us, event | category | flops | bytes accessed | tf_op | source)
XLA Modules:
  0.0 106.3 jit_solution(13627946871579811238)
XLA Ops:
  0.6 2.9 %prepare.1 = (bf16[16,1280]{1,0:T(8,128)(2,1)}, bf16[8,128,768]{2,1,0:T(8,128)(2,1)}) custom-call(s32[1]{0:T(128)} %bitcast.pos_ref, bf16[16,1152]{1,0:T(8,128)(2,1)} %text_ref.1, s32[1,128]{1,0:T(1,128)} %bitcast.5, s32[1,128]{1,0:T(1,128)} %bitcast.8, f32[1,8]{1,0:T(1,128)} %bitcast.9, bf16[128,768]{1,0:T(8,128)(2,1)} %refs_4_.1), custom_call_target="tpu_custom_call" | custom-call | tf_op jit(solution)/shard_map/prepare/pallas_call | solution.py:166
  3.5 0.0 copy-start.1
  3.6 0.0 copy-start
  3.6 0.0 copy-start.3
  3.6 16.8 %all-to-all-start = ((bf16[8,128,768]{2,1,0:T(8,128)(2,1)}), bf16[8,128,768]{2,1,0:T(8,128)(2,1)S(1)}, u32[]{:S(2)}, u32[]{:S(2)}) async-start(bf16[8,128,768]{2,1,0:T(8,128)(2,1)} %get-tuple-element.26), calls=%async_computation | async-start | bytes 3145728 | tf_op jit(solution)/shard_map/all_to_all | solution.py:199
  20.4 7.1 %collective-permute-start.2 = (bf16[16,1280]{1,0:T(8,128)(2,1)S(1)}, bf16[16,1280]{1,0:T(8,128)(2,1)S(1)}, u32[]{:S(2)}, u32[]{:S(2)}) collective-permute-start(bf16[16,1280]{1,0:T(8,128)(2,1)S(1)} %copy-done.1), channel_id=1, source_target_pairs={{1000,0},{1008,8},{1016,16},{0,24},{8,32},{16,40},{24,48},{32,56},... | collective-permute-start | bytes 122888 | tf_op jit(solution)/shard_map/ppermute | solution.py:24
  27.5 2.9 %collective-permute-start.1 = (bf16[16,1280]{1,0:T(8,128)(2,1)S(1)}, bf16[16,1280]{1,0:T(8,128)(2,1)S(1)}, u32[]{:S(2)}, u32[]{:S(2)}) collective-permute-start(bf16[16,1280]{1,0:T(8,128)(2,1)S(1)} %copy-done.1), channel_id=1, source_target_pairs={{1008,0},{1016,8},{0,16},{8,24},{16,32},{24,40},{32,48},{40,56},{4... | collective-permute-start | bytes 122888 | tf_op jit(solution)/shard_map/ppermute | solution.py:24
  30.4 2.7 %collective-permute-start = (bf16[16,1280]{1,0:T(8,128)(2,1)S(1)}, bf16[16,1280]{1,0:T(8,128)(2,1)S(1)}, u32[]{:S(2)}, u32[]{:S(2)}) collective-permute-start(bf16[16,1280]{1,0:T(8,128)(2,1)S(1)} %copy-done.1), channel_id=1, source_target_pairs={{1016,0},{0,8},{8,16},{16,24},{24,32},{32,40},{40,48},{48,56},{56,... | collective-permute-start | bytes 122888 | tf_op jit(solution)/shard_map/ppermute | solution.py:24
  33.1 3.9 %collective-permute-done.2.refs_3_ = bf16[16,1280]{1,0:T(8,128)(2,1)S(1)} collective-permute-done((bf16[16,1280]{1,0:T(8,128)(2,1)S(1)}, bf16[16,1280]{1,0:T(8,128)(2,1)S(1)}, u32[]{:S(2)}, u32[]{:S(2)}) %collective-permute-start.2) | collective-permute-done | bytes 40992 | tf_op jit(solution)/shard_map/ppermute | solution.py:24
  37.0 5.8 %collective-permute-done.1.refs_2_ = bf16[16,1280]{1,0:T(8,128)(2,1)S(1)} collective-permute-done((bf16[16,1280]{1,0:T(8,128)(2,1)S(1)}, bf16[16,1280]{1,0:T(8,128)(2,1)S(1)}, u32[]{:S(2)}, u32[]{:S(2)}) %collective-permute-start.1) | collective-permute-done | bytes 40992 | tf_op jit(solution)/shard_map/ppermute | solution.py:24
  42.8 0.0 collective-permute-done.refs_1_
  42.8 17.6 %all_gather.3.rows_ref = bf16[256,1280]{1,0:T(8,128)(2,1)S(1)} all-gather(bf16[64,1280]{1,0:T(8,128)(2,1)S(1)} %assemble.1.own_ref), channel_id=1, replica_groups=mesh['xh'=2,'z'=8,'y'=8,'xl'=4,'core'=2] {'xl'}, dimensions={0}, use_global_device_ids=true | all-gather | bytes 819200 | tf_op jit(solution)/shard_map/all_gather | solution.py:207
  60.3 1.9 %collective-permute-start.3 = (bf16[256,1280]{1,0:T(8,128)(2,1)S(1)}, bf16[256,1280]{1,0:T(8,128)(2,1)S(1)}, u32[]{:S(2)}, u32[]{:S(2)}) collective-permute-start(bf16[256,1280]{1,0:T(8,128)(2,1)S(1)} %all_gather.3.rows_ref), channel_id=1, source_target_pairs={{1,0},{0,1},{3,2},{2,3},{5,4},{4,5},{7,6},{6,7},{9,8},{8,9},{11,10... | collective-permute-start | bytes 1966088 | tf_op jit(solution)/shard_map/ppermute | solution.py:24
  62.3 1.1 %near_side.1 = (f32[128,1152]{1,0:T(8,128)S(1)}, f32[16,1152]{1,0:T(8,128)S(1)}, bf16[16,1152]{1,0:T(8,128)(2,1)S(1)}, bf16[16,1152]{1,0:T(8,128)(2,1)S(1)}, bf16[16,1152]{1,0:T(8,128)(2,1)S(1)}) custom-call(bf16[256,1280]{1,0:T(8,128)(2,1)S(1)} %all_gather.3.rows_ref, bf16[64,1280]{1,0:T(8,128)(2,1)S(1)} %assemble.1.own_ref, bf16[128,1152]{1,0:T(8,128)(2,1)S(1)} %copy-done, ...), custom_call_target="tpu_custom_call" | custom-call | flops 20000000000 | tf_op jit(solution)/shard_map/near_side/pallas_call | solution.py:166
  63.4 0.9 collective-permute-done.3.rows_ref
  64.3 1.8 %image_side.1 = (bf16[128,1152]{1,0:T(8,128)(2,1)S(1)}, bf16[8,2,72,128]{3,2,1,0:T(8,128)(2,1)}) custom-call(f32[128,1152]{1,0:T(8,128)S(1)} %get-tuple-element.17.near_ref, bf16[256,1280]{1,0:T(8,128)(2,1)S(1)} %collective-permute-done.3.rows_ref, bf16[128,1152]{1,0:T(8,128)(2,1)S(1)} %copy-done, s32[1,128]{1,0:T(1,128)S(1)} %bitcast.7), custom_call_target="tpu_custom_call" | custom-call | tf_op jit(solution)/shard_map/image_side/pallas_call | solution.py:166
  66.2 0.0 all-to-all-done.feat_ref
  66.2 3.6 %all-to-all-start.1 = ((bf16[8,144,128]{2,1,0:T(8,128)(2,1)}), bf16[8,144,128]{2,1,0:T(8,128)(2,1)S(1)}, u32[]{:S(2)}, u32[]{:S(2)}) async-start(bf16[8,144,128]{2,1,0:T(8,128)(2,1)} %bitcast.4), calls=%async_computation.1 | async-start | bytes 589824 | tf_op jit(solution)/shard_map/all_to_all | solution.py:222
  69.7 4.4 %collective-permute-start.4 = (bf16[16,1152]{1,0:T(8,128)(2,1)S(1)}, bf16[16,1152]{1,0:T(8,128)(2,1)S(1)}, u32[]{:S(2)}, u32[]{:S(2)}) collective-permute-start(bf16[16,1152]{1,0:T(8,128)(2,1)S(1)} %get-tuple-element.20), channel_id=1, source_target_pairs={{8,0},{16,8},{24,16},{32,24},{40,32},{48,40},{56,48},{64,56},{72,6... | collective-permute-start | bytes 110600 | tf_op jit(solution)/shard_map/ppermute | solution.py:24
  74.1 6.4 %collective-permute-start.5 = (bf16[16,1152]{1,0:T(8,128)(2,1)S(1)}, bf16[16,1152]{1,0:T(8,128)(2,1)S(1)}, u32[]{:S(2)}, u32[]{:S(2)}) collective-permute-start(bf16[16,1152]{1,0:T(8,128)(2,1)S(1)} %get-tuple-element.21), channel_id=1, source_target_pairs={{16,0},{24,8},{32,16},{40,24},{48,32},{56,40},{64,48},{72,56},{80,... | collective-permute-start | bytes 110600 | tf_op jit(solution)/shard_map/ppermute | solution.py:24
  80.6 3.6 %collective-permute-start.6 = (bf16[16,1152]{1,0:T(8,128)(2,1)S(1)}, bf16[16,1152]{1,0:T(8,128)(2,1)S(1)}, u32[]{:S(2)}, u32[]{:S(2)}) collective-permute-start(bf16[16,1152]{1,0:T(8,128)(2,1)S(1)} %get-tuple-element.22), channel_id=1, source_target_pairs={{24,0},{32,8},{40,16},{48,24},{56,32},{64,40},{72,48},{80,56},{88,... | collective-permute-start | bytes 110600 | tf_op jit(solution)/shard_map/ppermute | solution.py:24
  84.1 0.0 all-to-all-done.1.turned_ref
  84.2 1.4 %head_side.1 = bf16[16,54,128]{2,1,0:T(8,128)(2,1)} custom-call(bf16[8,128,768]{2,1,0:T(8,128)(2,1)S(1)} %all-to-all-done.feat_ref, bf16[8,144,128]{2,1,0:T(8,128)(2,1)S(1)} %all-to-all-done.1.turned_ref), custom_call_target="tpu_custom_call" | custom-call | tf_op jit(solution)/shard_map/head_side/pallas_call | solution.py:166
  85.6 8.0 %all-to-all-start.2 = ((bf16[16,54,128]{2,1,0:T(8,128)(2,1)}), bf16[16,54,128]{2,1,0:T(8,128)(2,1)S(1)}, u32[]{:S(2)}, u32[]{:S(2)}) async-start(bf16[16,54,128]{2,1,0:T(8,128)(2,1)} %head_side.1), calls=%async_computation.2 | async-start | bytes 458752 | tf_op jit(solution)/shard_map/all_to_all | solution.py:230
  93.6 0.0 collective-permute-done.4.one_ref
  93.6 0.0 collective-permute-done.5.two_ref
  93.6 0.0 collective-permute-done.6.three_ref
  93.6 0.0 copy-start.4
  93.6 1.5 %copy-done.4 = bf16[1152,768]{1,0:T(8,128)(2,1)S(1)} copy-done((bf16[1152,768]{1,0:T(8,128)(2,1)S(1)}, bf16[1152,768]{1,0:T(8,128)(2,1)}, u32[]{:S(2)}) %copy-start.4) | copy-done | bytes 1769496
  95.1 1.1 %finish.1 = (bf16[128,768]{1,0:T(8,128)(2,1)}, f32[16,1152]{1,0:T(8,128)}) custom-call(bf16[128,1152]{1,0:T(8,128)(2,1)S(1)} %get-tuple-element.18.grad_ref, bf16[1152,768]{1,0:T(8,128)(2,1)S(1)} %copy-done.4, bf16[16,1152]{1,0:T(8,128)(2,1)S(1)} %copy-done.2, f32[16,1152]{1,0:T(8,128)S(1)} %get-tuple-element.19.kept_ref, ...), custom_call_target="tpu_custom_call" | custom-call | flops 60000002048 | tf_op jit(solution)/shard_map/finish/pallas_call | solution.py:166
  96.2 9.4 %all-to-all-done.2.parts_ref = bf16[16,54,128]{2,1,0:T(8,128)(2,1)S(1)} async-done(((bf16[16,54,128]{2,1,0:T(8,128)(2,1)}), bf16[16,54,128]{2,1,0:T(8,128)(2,1)S(1)}, u32[]{:S(2)}, u32[]{:S(2)}) %all-to-all-start.2) | async-done | bytes 221216 | tf_op jit(solution)/shard_map/all_to_all | solution.py:230
  105.6 0.7 head_sum.1
  (6 shorter events, 0.0 us)
Async XLA Ops:
  3.5 16.9 %copy-start.1 = (bf16[16,1280]{1,0:T(8,128)(2,1)S(1)}, bf16[16,1280]{1,0:T(8,128)(2,1)}, u32[]{:S(2)}) copy-start(bf16[16,1280]{1,0:T(8,128)(2,1)} %get-tuple-element.16.refs_0_) | copy-start | bytes 122884
  3.6 58.7 %copy-start = (bf16[128,1152]{1,0:T(8,128)(2,1)S(1)}, bf16[128,1152]{1,0:T(8,128)(2,1)}, u32[]{:S(2)}) copy-start(bf16[128,1152]{1,0:T(8,128)(2,1)} %embed_ref.3) | copy-start | bytes 884740
  3.6 58.7 %copy-start.3 = (s32[128]{0:T(128)S(1)}, s32[128]{0:T(128)}, u32[]{:S(2)}) copy-start(s32[128]{0:T(128)} %param.11) | copy-start | bytes 1540
  3.6 62.6 %all-to-all-start = ((bf16[8,128,768]{2,1,0:T(8,128)(2,1)}), bf16[8,128,768]{2,1,0:T(8,128)(2,1)S(1)}, u32[]{:S(2)}, u32[]{:S(2)}) async-start(bf16[8,128,768]{2,1,0:T(8,128)(2,1)} %get-tuple-element.26), calls=%async_computation | async-start | bytes 3145728 | tf_op jit(solution)/shard_map/all_to_all | solution.py:199
  20.4 16.6 %collective-permute-start.2 = (bf16[16,1280]{1,0:T(8,128)(2,1)S(1)}, bf16[16,1280]{1,0:T(8,128)(2,1)S(1)}, u32[]{:S(2)}, u32[]{:S(2)}) collective-permute-start(bf16[16,1280]{1,0:T(8,128)(2,1)S(1)} %copy-done.1), channel_id=1, source_target_pairs={{1000,0},{1008,8},{1016,16},{0,24},{8,32},{16,40},{24,48},{32,56},... | collective-permute-start | bytes 122888 | tf_op jit(solution)/shard_map/ppermute | solution.py:24
  27.5 15.3 %collective-permute-start.1 = (bf16[16,1280]{1,0:T(8,128)(2,1)S(1)}, bf16[16,1280]{1,0:T(8,128)(2,1)S(1)}, u32[]{:S(2)}, u32[]{:S(2)}) collective-permute-start(bf16[16,1280]{1,0:T(8,128)(2,1)S(1)} %copy-done.1), channel_id=1, source_target_pairs={{1008,0},{1016,8},{0,16},{8,24},{16,32},{24,40},{32,48},{40,56},{4... | collective-permute-start | bytes 122888 | tf_op jit(solution)/shard_map/ppermute | solution.py:24
  30.4 12.4 %collective-permute-start = (bf16[16,1280]{1,0:T(8,128)(2,1)S(1)}, bf16[16,1280]{1,0:T(8,128)(2,1)S(1)}, u32[]{:S(2)}, u32[]{:S(2)}) collective-permute-start(bf16[16,1280]{1,0:T(8,128)(2,1)S(1)} %copy-done.1), channel_id=1, source_target_pairs={{1016,0},{0,8},{8,16},{16,24},{24,32},{32,40},{40,48},{48,56},{56,... | collective-permute-start | bytes 122888 | tf_op jit(solution)/shard_map/ppermute | solution.py:24
  60.3 4.0 %collective-permute-start.3 = (bf16[256,1280]{1,0:T(8,128)(2,1)S(1)}, bf16[256,1280]{1,0:T(8,128)(2,1)S(1)}, u32[]{:S(2)}, u32[]{:S(2)}) collective-permute-start(bf16[256,1280]{1,0:T(8,128)(2,1)S(1)} %all_gather.3.rows_ref), channel_id=1, source_target_pairs={{1,0},{0,1},{3,2},{2,3},{5,4},{4,5},{7,6},{6,7},{9,8},{8,9},{11,10... | collective-permute-start | bytes 1966088 | tf_op jit(solution)/shard_map/ppermute | solution.py:24
  66.2 27.4 %copy-start.2 = (bf16[16,1152]{1,0:T(8,128)(2,1)S(1)}, bf16[16,1152]{1,0:T(8,128)(2,1)}, u32[]{:S(2)}) copy-start(bf16[16,1152]{1,0:T(8,128)(2,1)} %text_ref.1) | copy-start | bytes 110596
  66.2 18.0 %all-to-all-start.1 = ((bf16[8,144,128]{2,1,0:T(8,128)(2,1)}), bf16[8,144,128]{2,1,0:T(8,128)(2,1)S(1)}, u32[]{:S(2)}, u32[]{:S(2)}) async-start(bf16[8,144,128]{2,1,0:T(8,128)(2,1)} %bitcast.4), calls=%async_computation.1 | async-start | bytes 589824 | tf_op jit(solution)/shard_map/all_to_all | solution.py:222
  69.7 23.8 %collective-permute-start.4 = (bf16[16,1152]{1,0:T(8,128)(2,1)S(1)}, bf16[16,1152]{1,0:T(8,128)(2,1)S(1)}, u32[]{:S(2)}, u32[]{:S(2)}) collective-permute-start(bf16[16,1152]{1,0:T(8,128)(2,1)S(1)} %get-tuple-element.20), channel_id=1, source_target_pairs={{8,0},{16,8},{24,16},{32,24},{40,32},{48,40},{56,48},{64,56},{72,6... | collective-permute-start | bytes 110600 | tf_op jit(solution)/shard_map/ppermute | solution.py:24
  74.1 19.4 %collective-permute-start.5 = (bf16[16,1152]{1,0:T(8,128)(2,1)S(1)}, bf16[16,1152]{1,0:T(8,128)(2,1)S(1)}, u32[]{:S(2)}, u32[]{:S(2)}) collective-permute-start(bf16[16,1152]{1,0:T(8,128)(2,1)S(1)} %get-tuple-element.21), channel_id=1, source_target_pairs={{16,0},{24,8},{32,16},{40,24},{48,32},{56,40},{64,48},{72,56},{80,... | collective-permute-start | bytes 110600 | tf_op jit(solution)/shard_map/ppermute | solution.py:24
  80.6 13.0 %collective-permute-start.6 = (bf16[16,1152]{1,0:T(8,128)(2,1)S(1)}, bf16[16,1152]{1,0:T(8,128)(2,1)S(1)}, u32[]{:S(2)}, u32[]{:S(2)}) collective-permute-start(bf16[16,1152]{1,0:T(8,128)(2,1)S(1)} %get-tuple-element.22), channel_id=1, source_target_pairs={{24,0},{32,8},{40,16},{48,24},{56,32},{64,40},{72,48},{80,56},{88,... | collective-permute-start | bytes 110600 | tf_op jit(solution)/shard_map/ppermute | solution.py:24
  85.6 20.0 %all-to-all-start.2 = ((bf16[16,54,128]{2,1,0:T(8,128)(2,1)}), bf16[16,54,128]{2,1,0:T(8,128)(2,1)S(1)}, u32[]{:S(2)}, u32[]{:S(2)}) async-start(bf16[16,54,128]{2,1,0:T(8,128)(2,1)} %head_side.1), calls=%async_computation.2 | async-start | bytes 458752 | tf_op jit(solution)/shard_map/all_to_all | solution.py:230
  93.6 1.5 %copy-start.4 = (bf16[1152,768]{1,0:T(8,128)(2,1)S(1)}, bf16[1152,768]{1,0:T(8,128)(2,1)}, u32[]{:S(2)}) copy-start(bf16[1152,768]{1,0:T(8,128)(2,1)} %head_ref.1) | copy-start | bytes 5308420

commit v12 on v11

--- a/solution.py
+++ b/solution.py
@@ -75,7 +75,7 @@
 
 def assemble(*refs):
     out_ref, count = refs[-1], refs[0].shape[0]
-    for k, ref in enumerate(refs[:-1]):
+    for k, ref in enumerate(refs[-2::-1]):
         out_ref[k * count : (k + 1) * count] = ref[...]
 
 
@@ -200,7 +200,7 @@
 
     window = [payload] + [shifted(payload, BLK, d) for d in (1, 2, 3)]
     own = call(
-        assemble, [((len(window) * texts, width + TAIL), bf16)], *window,
+        assemble, [((len(window) * texts, width + TAIL), bf16)], *window[::-1],
         room=ROOM,
     )
 

time: 107 us -> 110 us (1.028)
  waiting for transfers between devices: 20 us -> 23.3 us
  blocking collectives: 17.6 us -> 16.5 us
    ppermute x7, waiting for transfers between devices: 10.6 us -> 13.8 us  [shifted(): lax.ppermute(block, axis, [((i - distance) % size, i) for i in range(size)])]
    all_to_all x1, starting transfers between devices: 7.98 us -> 9.58 us  [local(): parts = lax.all_to_all(parts, ('xh', 'y'), 0, 0, tiled=True)]
where the time goes in v12:
time: 110 us; the launch traced here: 109 us
  starting transfers between devices  57.9 us (53%)
  waiting for transfers between devices  23.3 us (21%)
  blocking collectives  16.5 us (15%)
  Pallas kernels  9.08 us (8%)
  local copies, waits for them, and re-layouts  1.49 us (1%)
    ppermute x7, starting transfers between devices, shifted(): lax.ppermute(block, axis, [((i - distance) % size, i) for i in range(size)])  27.9 us
    all_to_all x1, starting transfers between devices, local(): feats = lax.all_to_all(feats, 'z', 0, 0, tiled=True)  16.8 us
    all_gather x1, blocking collectives, local(): here = lax.all_gather(own, 'xl', axis=0, tiled=True)  16.5 us
    ppermute x7, waiting for transfers between devices, shifted(): lax.ppermute(block, axis, [((i - distance) % size, i) for i in range(size)])  13.8 us
    all_to_all x1, starting transfers between devices, local(): parts = lax.all_to_all(parts, ('xh', 'y'), 0, 0, tiled=True)  9.58 us
    all_to_all x1, waiting for transfers between devices, local(): parts = lax.all_to_all(parts, ('xh', 'y'), 0, 0, tiled=True)  9.55 us
    pallas_call x7, Pallas kernels, call(): pl.pallas_call(kernel, out_shape=outs[0] if single else outs, in_specs=sp...  9.08 us
    all_to_all x1, starting transfers between devices, local(): lax.all_to_all(turned.reshape(planes, own_width, images), 'z', 0, 0, tile...  3.55 us
  transfers between devices with their start and end apart: 10, of which 4 were waited for; matrix products, arithmetic and copies ran while one was open for 0% of the time, Pallas kernels for 5%

profile of v12, /device:TPU:16, one launch (start us, length us, event | category | flops | bytes accessed | tf_op | source)
XLA Modules:
  0.0 109.1 jit_solution(6129258718449257095)
XLA Ops:
  0.6 2.9 %prepare.1 = (bf16[16,1280]{1,0:T(8,128)(2,1)}, bf16[8,128,768]{2,1,0:T(8,128)(2,1)}) custom-call(s32[1]{0:T(128)} %bitcast.pos_ref, bf16[16,1152]{1,0:T(8,128)(2,1)} %text_ref.1, s32[1,128]{1,0:T(1,128)} %bitcast.5, s32[1,128]{1,0:T(1,128)} %bitcast.8, f32[1,8]{1,0:T(1,128)} %bitcast.9, bf16[128,768]{1,0:T(8,128)(2,1)} %refs_4_.1), custom_call_target="tpu_custom_call" | custom-call | tf_op jit(solution)/shard_map/prepare/pallas_call | solution.py:166
  3.5 0.0 copy-start.1
  3.6 0.0 copy-start
  3.6 0.0 copy-start.3
  3.6 16.8 %all-to-all-start = ((bf16[8,128,768]{2,1,0:T(8,128)(2,1)}), bf16[8,128,768]{2,1,0:T(8,128)(2,1)S(1)}, u32[]{:S(2)}, u32[]{:S(2)}) async-start(bf16[8,128,768]{2,1,0:T(8,128)(2,1)} %get-tuple-element.26), calls=%async_computation | async-start | bytes 3145728 | tf_op jit(solution)/shard_map/all_to_all | solution.py:199
  20.4 3.6 %collective-permute-start.2 = (bf16[16,1280]{1,0:T(8,128)(2,1)S(1)}, bf16[16,1280]{1,0:T(8,128)(2,1)S(1)}, u32[]{:S(2)}, u32[]{:S(2)}) collective-permute-start(bf16[16,1280]{1,0:T(8,128)(2,1)S(1)} %copy-done.1), channel_id=1, source_target_pairs={{1016,0},{0,8},{8,16},{16,24},{24,32},{32,40},{40,48},{48,56},{56,... | collective-permute-start | bytes 122888 | tf_op jit(solution)/shard_map/ppermute | solution.py:24
  24.0 5.9 %collective-permute-start.1 = (bf16[16,1280]{1,0:T(8,128)(2,1)S(1)}, bf16[16,1280]{1,0:T(8,128)(2,1)S(1)}, u32[]{:S(2)}, u32[]{:S(2)}) collective-permute-start(bf16[16,1280]{1,0:T(8,128)(2,1)S(1)} %copy-done.1), channel_id=1, source_target_pairs={{1008,0},{1016,8},{0,16},{8,24},{16,32},{24,40},{32,48},{40,56},{4... | collective-permute-start | bytes 122888 | tf_op jit(solution)/shard_map/ppermute | solution.py:24
  30.0 3.2 %collective-permute-start = (bf16[16,1280]{1,0:T(8,128)(2,1)S(1)}, bf16[16,1280]{1,0:T(8,128)(2,1)S(1)}, u32[]{:S(2)}, u32[]{:S(2)}) collective-permute-start(bf16[16,1280]{1,0:T(8,128)(2,1)S(1)} %copy-done.1), channel_id=1, source_target_pairs={{1000,0},{1008,8},{1016,16},{0,24},{8,32},{16,40},{24,48},{32,56},... | collective-permute-start | bytes 122888 | tf_op jit(solution)/shard_map/ppermute | solution.py:24
  33.1 0.0 collective-permute-done.2.refs_2_
  33.1 5.9 %collective-permute-done.1.refs_1_ = bf16[16,1280]{1,0:T(8,128)(2,1)S(1)} collective-permute-done((bf16[16,1280]{1,0:T(8,128)(2,1)S(1)}, bf16[16,1280]{1,0:T(8,128)(2,1)S(1)}, u32[]{:S(2)}, u32[]{:S(2)}) %collective-permute-start.1) | collective-permute-done | bytes 40992 | tf_op jit(solution)/shard_map/ppermute | solution.py:24
  39.1 6.9 %collective-permute-done.refs_0_ = bf16[16,1280]{1,0:T(8,128)(2,1)S(1)} collective-permute-done((bf16[16,1280]{1,0:T(8,128)(2,1)S(1)}, bf16[16,1280]{1,0:T(8,128)(2,1)S(1)}, u32[]{:S(2)}, u32[]{:S(2)}) %collective-permute-start) | collective-permute-done | bytes 40992 | tf_op jit(solution)/shard_map/ppermute | solution.py:24
  46.0 16.5 %all_gather.3.rows_ref = bf16[256,1280]{1,0:T(8,128)(2,1)S(1)} all-gather(bf16[64,1280]{1,0:T(8,128)(2,1)S(1)} %assemble.1.own_ref), channel_id=1, replica_groups=mesh['xh'=2,'z'=8,'y'=8,'xl'=4,'core'=2] {'xl'}, dimensions={0}, use_global_device_ids=true | all-gather | bytes 819200 | tf_op jit(solution)/shard_map/all_gather | solution.py:207
  62.5 1.9 %collective-permute-start.3 = (bf16[256,1280]{1,0:T(8,128)(2,1)S(1)}, bf16[256,1280]{1,0:T(8,128)(2,1)S(1)}, u32[]{:S(2)}, u32[]{:S(2)}) collective-permute-start(bf16[256,1280]{1,0:T(8,128)(2,1)S(1)} %all_gather.3.rows_ref), channel_id=1, source_target_pairs={{1,0},{0,1},{3,2},{2,3},{5,4},{4,5},{7,6},{6,7},{9,8},{8,9},{11,10... | collective-permute-start | bytes 1966088 | tf_op jit(solution)/shard_map/ppermute | solution.py:24
  64.5 1.1 %near_side.1 = (f32[128,1152]{1,0:T(8,128)S(1)}, f32[16,1152]{1,0:T(8,128)S(1)}, bf16[16,1152]{1,0:T(8,128)(2,1)S(1)}, bf16[16,1152]{1,0:T(8,128)(2,1)S(1)}, bf16[16,1152]{1,0:T(8,128)(2,1)S(1)}) custom-call(bf16[256,1280]{1,0:T(8,128)(2,1)S(1)} %all_gather.3.rows_ref, bf16[64,1280]{1,0:T(8,128)(2,1)S(1)} %assemble.1.own_ref, bf16[128,1152]{1,0:T(8,128)(2,1)S(1)} %copy-done, ...), custom_call_target="tpu_custom_call" | custom-call | flops 20000000000 | tf_op jit(solution)/shard_map/near_side/pallas_call | solution.py:166
  65.6 0.9 collective-permute-done.3.rows_ref
  66.5 1.8 %image_side.1 = (bf16[128,1152]{1,0:T(8,128)(2,1)S(1)}, bf16[8,2,72,128]{3,2,1,0:T(8,128)(2,1)}) custom-call(f32[128,1152]{1,0:T(8,128)S(1)} %get-tuple-element.17.near_ref, bf16[256,1280]{1,0:T(8,128)(2,1)S(1)} %collective-permute-done.3.rows_ref, bf16[128,1152]{1,0:T(8,128)(2,1)S(1)} %copy-done, s32[1,128]{1,0:T(1,128)S(1)} %bitcast.7), custom_call_target="tpu_custom_call" | custom-call | tf_op jit(solution)/shard_map/image_side/pallas_call | solution.py:166
  68.3 0.0 all-to-all-done.feat_ref
  68.3 3.6 %all-to-all-start.1 = ((bf16[8,144,128]{2,1,0:T(8,128)(2,1)}), bf16[8,144,128]{2,1,0:T(8,128)(2,1)S(1)}, u32[]{:S(2)}, u32[]{:S(2)}) async-start(bf16[8,144,128]{2,1,0:T(8,128)(2,1)} %bitcast.4), calls=%async_computation.1 | async-start | bytes 589824 | tf_op jit(solution)/shard_map/all_to_all | solution.py:222
  71.9 1.9 %collective-permute-start.4 = (bf16[16,1152]{1,0:T(8,128)(2,1)S(1)}, bf16[16,1152]{1,0:T(8,128)(2,1)S(1)}, u32[]{:S(2)}, u32[]{:S(2)}) collective-permute-start(bf16[16,1152]{1,0:T(8,128)(2,1)S(1)} %get-tuple-element.20), channel_id=1, source_target_pairs={{8,0},{16,8},{24,16},{32,24},{40,32},{48,40},{56,48},{64,56},{72,6... | collective-permute-start | bytes 110600 | tf_op jit(solution)/shard_map/ppermute | solution.py:24
  73.8 7.1 %collective-permute-start.5 = (bf16[16,1152]{1,0:T(8,128)(2,1)S(1)}, bf16[16,1152]{1,0:T(8,128)(2,1)S(1)}, u32[]{:S(2)}, u32[]{:S(2)}) collective-permute-start(bf16[16,1152]{1,0:T(8,128)(2,1)S(1)} %get-tuple-element.21), channel_id=1, source_target_pairs={{16,0},{24,8},{32,16},{40,24},{48,32},{56,40},{64,48},{72,56},{80,... | collective-permute-start | bytes 110600 | tf_op jit(solution)/shard_map/ppermute | solution.py:24
  80.9 4.3 %collective-permute-start.6 = (bf16[16,1152]{1,0:T(8,128)(2,1)S(1)}, bf16[16,1152]{1,0:T(8,128)(2,1)S(1)}, u32[]{:S(2)}, u32[]{:S(2)}) collective-permute-start(bf16[16,1152]{1,0:T(8,128)(2,1)S(1)} %get-tuple-element.22), channel_id=1, source_target_pairs={{24,0},{32,8},{40,16},{48,24},{56,32},{64,40},{72,48},{80,56},{88,... | collective-permute-start | bytes 110600 | tf_op jit(solution)/shard_map/ppermute | solution.py:24
  85.3 0.0 all-to-all-done.1.turned_ref
  85.3 1.4 %head_side.1 = bf16[16,54,128]{2,1,0:T(8,128)(2,1)} custom-call(bf16[8,128,768]{2,1,0:T(8,128)(2,1)S(1)} %all-to-all-done.feat_ref, bf16[8,144,128]{2,1,0:T(8,128)(2,1)S(1)} %all-to-all-done.1.turned_ref), custom_call_target="tpu_custom_call" | custom-call | tf_op jit(solution)/shard_map/head_side/pallas_call | solution.py:166
  86.7 9.6 %all-to-all-start.2 = ((bf16[16,54,128]{2,1,0:T(8,128)(2,1)}), bf16[16,54,128]{2,1,0:T(8,128)(2,1)S(1)}, u32[]{:S(2)}, u32[]{:S(2)}) async-start(bf16[16,54,128]{2,1,0:T(8,128)(2,1)} %head_side.1), calls=%async_computation.2 | async-start | bytes 458752 | tf_op jit(solution)/shard_map/all_to_all | solution.py:230
  96.3 0.0 collective-permute-done.4.one_ref
  96.3 0.0 collective-permute-done.5.two_ref
  96.3 0.0 collective-permute-done.6.three_ref
  96.3 0.0 copy-start.4
  96.3 1.5 %copy-done.4 = bf16[1152,768]{1,0:T(8,128)(2,1)S(1)} copy-done((bf16[1152,768]{1,0:T(8,128)(2,1)S(1)}, bf16[1152,768]{1,0:T(8,128)(2,1)}, u32[]{:S(2)}) %copy-start.4) | copy-done | bytes 1769496
  97.8 1.1 %finish.1 = (bf16[128,768]{1,0:T(8,128)(2,1)}, f32[16,1152]{1,0:T(8,128)}) custom-call(bf16[128,1152]{1,0:T(8,128)(2,1)S(1)} %get-tuple-element.18.grad_ref, bf16[1152,768]{1,0:T(8,128)(2,1)S(1)} %copy-done.4, bf16[16,1152]{1,0:T(8,128)(2,1)S(1)} %copy-done.2, f32[16,1152]{1,0:T(8,128)S(1)} %get-tuple-element.19.kept_ref, ...), custom_call_target="tpu_custom_call" | custom-call | flops 60000002048 | tf_op jit(solution)/shard_map/finish/pallas_call | solution.py:166
  98.9 9.5 %all-to-all-done.2.parts_ref = bf16[16,54,128]{2,1,0:T(8,128)(2,1)S(1)} async-done(((bf16[16,54,128]{2,1,0:T(8,128)(2,1)}), bf16[16,54,128]{2,1,0:T(8,128)(2,1)S(1)}, u32[]{:S(2)}, u32[]{:S(2)}) %all-to-all-start.2) | async-done | bytes 221216 | tf_op jit(solution)/shard_map/all_to_all | solution.py:230
  108.5 0.7 head_sum.1
  (6 shorter events, 0.0 us)
Async XLA Ops:
  3.5 16.9 %copy-start.1 = (bf16[16,1280]{1,0:T(8,128)(2,1)S(1)}, bf16[16,1280]{1,0:T(8,128)(2,1)}, u32[]{:S(2)}) copy-start(bf16[16,1280]{1,0:T(8,128)(2,1)} %get-tuple-element.16.refs_3_) | copy-start | bytes 122884
  3.6 60.9 %copy-start = (bf16[128,1152]{1,0:T(8,128)(2,1)S(1)}, bf16[128,1152]{1,0:T(8,128)(2,1)}, u32[]{:S(2)}) copy-start(bf16[128,1152]{1,0:T(8,128)(2,1)} %embed_ref.3) | copy-start | bytes 884740
  3.6 60.9 %copy-start.3 = (s32[128]{0:T(128)S(1)}, s32[128]{0:T(128)}, u32[]{:S(2)}) copy-start(s32[128]{0:T(128)} %param.11) | copy-start | bytes 1540
  3.6 64.8 %all-to-all-start = ((bf16[8,128,768]{2,1,0:T(8,128)(2,1)}), bf16[8,128,768]{2,1,0:T(8,128)(2,1)S(1)}, u32[]{:S(2)}, u32[]{:S(2)}) async-start(bf16[8,128,768]{2,1,0:T(8,128)(2,1)} %get-tuple-element.26), calls=%async_computation | async-start | bytes 3145728 | tf_op jit(solution)/shard_map/all_to_all | solution.py:199
  20.4 12.7 %collective-permute-start.2 = (bf16[16,1280]{1,0:T(8,128)(2,1)S(1)}, bf16[16,1280]{1,0:T(8,128)(2,1)S(1)}, u32[]{:S(2)}, u32[]{:S(2)}) collective-permute-start(bf16[16,1280]{1,0:T(8,128)(2,1)S(1)} %copy-done.1), channel_id=1, source_target_pairs={{1016,0},{0,8},{8,16},{16,24},{24,32},{32,40},{40,48},{48,56},{56,... | collective-permute-start | bytes 122888 | tf_op jit(solution)/shard_map/ppermute | solution.py:24
  24.0 15.1 %collective-permute-start.1 = (bf16[16,1280]{1,0:T(8,128)(2,1)S(1)}, bf16[16,1280]{1,0:T(8,128)(2,1)S(1)}, u32[]{:S(2)}, u32[]{:S(2)}) collective-permute-start(bf16[16,1280]{1,0:T(8,128)(2,1)S(1)} %copy-done.1), channel_id=1, source_target_pairs={{1008,0},{1016,8},{0,16},{8,24},{16,32},{24,40},{32,48},{40,56},{4... | collective-permute-start | bytes 122888 | tf_op jit(solution)/shard_map/ppermute | solution.py:24
  30.0 16.0 %collective-permute-start = (bf16[16,1280]{1,0:T(8,128)(2,1)S(1)}, bf16[16,1280]{1,0:T(8,128)(2,1)S(1)}, u32[]{:S(2)}, u32[]{:S(2)}) collective-permute-start(bf16[16,1280]{1,0:T(8,128)(2,1)S(1)} %copy-done.1), channel_id=1, source_target_pairs={{1000,0},{1008,8},{1016,16},{0,24},{8,32},{16,40},{24,48},{32,56},... | collective-permute-start | bytes 122888 | tf_op jit(solution)/shard_map/ppermute | solution.py:24
  62.5 4.0 %collective-permute-start.3 = (bf16[256,1280]{1,0:T(8,128)(2,1)S(1)}, bf16[256,1280]{1,0:T(8,128)(2,1)S(1)}, u32[]{:S(2)}, u32[]{:S(2)}) collective-permute-start(bf16[256,1280]{1,0:T(8,128)(2,1)S(1)} %all_gather.3.rows_ref), channel_id=1, source_target_pairs={{1,0},{0,1},{3,2},{2,3},{5,4},{4,5},{7,6},{6,7},{9,8},{8,9},{11,10... | collective-permute-start | bytes 1966088 | tf_op jit(solution)/shard_map/ppermute | solution.py:24
  68.3 28.0 %copy-start.2 = (bf16[16,1152]{1,0:T(8,128)(2,1)S(1)}, bf16[16,1152]{1,0:T(8,128)(2,1)}, u32[]{:S(2)}) copy-start(bf16[16,1152]{1,0:T(8,128)(2,1)} %text_ref.1) | copy-start | bytes 110596
  68.3 16.9 %all-to-all-start.1 = ((bf16[8,144,128]{2,1,0:T(8,128)(2,1)}), bf16[8,144,128]{2,1,0:T(8,128)(2,1)S(1)}, u32[]{:S(2)}, u32[]{:S(2)}) async-start(bf16[8,144,128]{2,1,0:T(8,128)(2,1)} %bitcast.4), calls=%async_computation.1 | async-start | bytes 589824 | tf_op jit(solution)/shard_map/all_to_all | solution.py:222
  71.9 24.4 %collective-permute-start.4 = (bf16[16,1152]{1,0:T(8,128)(2,1)S(1)}, bf16[16,1152]{1,0:T(8,128)(2,1)S(1)}, u32[]{:S(2)}, u32[]{:S(2)}) collective-permute-start(bf16[16,1152]{1,0:T(8,128)(2,1)S(1)} %get-tuple-element.20), channel_id=1, source_target_pairs={{8,0},{16,8},{24,16},{32,24},{40,32},{48,40},{56,48},{64,56},{72,6... | collective-permute-start | bytes 110600 | tf_op jit(solution)/shard_map/ppermute | solution.py:24
  73.8 22.4 %collective-permute-start.5 = (bf16[16,1152]{1,0:T(8,128)(2,1)S(1)}, bf16[16,1152]{1,0:T(8,128)(2,1)S(1)}, u32[]{:S(2)}, u32[]{:S(2)}) collective-permute-start(bf16[16,1152]{1,0:T(8,128)(2,1)S(1)} %get-tuple-element.21), channel_id=1, source_target_pairs={{16,0},{24,8},{32,16},{40,24},{48,32},{56,40},{64,48},{72,56},{80,... | collective-permute-start | bytes 110600 | tf_op jit(solution)/shard_map/ppermute | solution.py:24
  80.9 15.3 %collective-permute-start.6 = (bf16[16,1152]{1,0:T(8,128)(2,1)S(1)}, bf16[16,1152]{1,0:T(8,128)(2,1)S(1)}, u32[]{:S(2)}, u32[]{:S(2)}) collective-permute-start(bf16[16,1152]{1,0:T(8,128)(2,1)S(1)} %get-tuple-element.22), channel_id=1, source_target_pairs={{24,0},{32,8},{40,16},{48,24},{56,32},{64,40},{72,48},{80,56},{88,... | collective-permute-start | bytes 110600 | tf_op jit(solution)/shard_map/ppermute | solution.py:24
  86.7 21.8 %all-to-all-start.2 = ((bf16[16,54,128]{2,1,0:T(8,128)(2,1)}), bf16[16,54,128]{2,1,0:T(8,128)(2,1)S(1)}, u32[]{:S(2)}, u32[]{:S(2)}) async-start(bf16[16,54,128]{2,1,0:T(8,128)(2,1)} %head_side.1), calls=%async_computation.2 | async-start | bytes 458752 | tf_op jit(solution)/shard_map/all_to_all | solution.py:230
  96.3 1.5 %copy-start.4 = (bf16[1152,768]{1,0:T(8,128)(2,1)S(1)}, bf16[1152,768]{1,0:T(8,128)(2,1)}, u32[]{:S(2)}) copy-start(bf16[1152,768]{1,0:T(8,128)(2,1)} %head_ref.1) | copy-start | bytes 5308420
